TPU v7x, 128 devices: a whole 4x4x4 slice. The times are simulated.
128 devices in a mesh: replica: 64 (over y, z, x_lo, core), shard: 2 (over x_hi).
Axes of the slice: x: 4 (x_hi: 2, x_lo: 2; x = x_hi * 2 + x_lo), y: 4, z: 4, core: 2. Of those that a mesh axis runs over, the one named last changes fastest.
Arguments:
- tokens: bfloat16 [768, 196, 512], P(('replica', 'shard')), may hold values from -6 to 6
- image_counts: int32 [128], P(('replica', 'shard')), may hold values from 1 to 6, as said below
- shift_mask: int32 [4, 49, 49], replicated, may hold values from 0 to 1, as said below
- rel_index: int32 [49, 49], replicated, may hold values from 0 to 168, as said below
- norm1_gain: bfloat16 [512], P('shard'), may hold values from 0.25 to 1.75
- norm1_bias: bfloat16 [512], P('shard'), may hold values from -1.5 to 1.5
- qkv_weight: bfloat16 [512, 1536], P('shard'), may hold values from -0.25 to 0.25
- q_bias: bfloat16 [512], P('shard'), may hold values from -1.5 to 1.5
- v_bias: bfloat16 [512], P('shard'), may hold values from -1.5 to 1.5
- rel_table: bfloat16 [169, 16], P(None, 'shard'), may hold values from -4 to 4
- proj_weight: bfloat16 [512, 512], P('shard'), may hold values from -1 to 1
- proj_bias: bfloat16 [512], P('shard'), may hold values from -1.5 to 1.5
- norm2_gain: bfloat16 [512], P('shard'), may hold values from 0.25 to 1.75
- norm2_bias: bfloat16 [512], P('shard'), may hold values from -1.5 to 1.5
- fc1_weight: bfloat16 [512, 2048], P('shard'), may hold values from -0.25 to 0.25
- fc1_bias: bfloat16 [2048], P('shard'), may hold values from -1.5 to 1.5
- fc2_weight: bfloat16 [2048, 512], P('shard'), may hold values from -0.1875 to 0.1875
- fc2_bias: bfloat16 [512], P('shard'), may hold values from -1.5 to 1.5
- out_grad: bfloat16 [768, 196, 512], P(('replica', 'shard')), may hold values from -6 to 6
Outputs:
- block_out: bfloat16 [768, 196, 512], P(('replica', 'shard'))
- tokens_grad: float32 [768, 196, 512], P(('replica', 'shard'))
- norm1_gain_grad: float32 [512], P('shard')
- norm1_bias_grad: float32 [512], P('shard')
- qkv_weight_grad: float32 [512, 1536], P('shard')
- q_bias_grad: float32 [512], P('shard')
- v_bias_grad: float32 [512], P('shard')
- rel_table_grad: float32 [169, 16], P(None, 'shard')
- proj_weight_grad: float32 [512, 512], P('shard')
- proj_bias_grad: float32 [512], P('shard')
- norm2_gain_grad: float32 [512], P('shard')
- norm2_bias_grad: float32 [512], P('shard')
- fc1_weight_grad: float32 [512, 2048], P('shard')
- fc1_bias_grad: float32 [2048], P('shard')
- fc2_weight_grad: float32 [2048, 512], P('shard')
- fc2_bias_grad: float32 [512], P('shard')
Inputs may be any that keep to these rules, and one draw needn't show every extreme that they name: `image_counts`: images held by each device in its first slots; some device holds 6 images and some device holds 1. `shift_mask`: 1 where a query may attend a key of the same window; symmetric, and 1 on the diagonal. `rel_index`: pairs with the same offset between query and key name the same table row, different offsets different rows.
All inputs are finite; a program needn't handle non-finite values.
Results may differ from a plain program's by a relative error of at most 0.013.
Values may be sent and summed in bfloat16 or wider, within the bound.
A program may use at most 192 MiB of HBM per device.

v0:
```python
from functools import partial

import jax
import jax.numpy as jnp
from jax import lax
from jax.sharding import PartitionSpec as P

WIN = 7
SIDE = 14
SHIFT = 3


EPSILON = 1e-05
HIGH = lax.Precision.HIGHEST


def layer_norm(values, gain, shift):
    center = values - jnp.mean(values, -1, keepdims=True)
    spread = jnp.mean(center * center, -1, keepdims=True)
    return center * lax.rsqrt(spread + EPSILON) * gain + shift


def to_windows(values):
    images = values.shape[0]
    feats = values.shape[-1]
    blocks_side = SIDE // WIN
    grid = values.reshape(images, SIDE, SIDE, feats)
    grid = jnp.roll(grid, (-SHIFT, -SHIFT), (1, 2))
    grid = grid.reshape(images, blocks_side, WIN, blocks_side, WIN, feats).transpose(
        0, 1, 3, 2, 4, 5
    )
    return grid.reshape(images * blocks_side * blocks_side, WIN * WIN, feats)


def from_windows(values, images):
    feats = values.shape[-1]
    blocks_side = SIDE // WIN
    grid = values.reshape(images, blocks_side, blocks_side, WIN, WIN, feats).transpose(
        0, 1, 3, 2, 4, 5
    )
    grid = jnp.roll(grid.reshape(images, SIDE, SIDE, feats), (SHIFT, SHIFT), (1, 2))
    return grid.reshape(images, SIDE * SIDE, feats)


def row_sum(values):
    return jnp.sum(values.reshape(-1, values.shape[-1]), 0)


def weight_grad(left, right):
    return jnp.einsum("nf,ng->fg", left, right, preferred_element_type=jnp.float32)


def back_product(grad_low, weights):
    return jnp.einsum("ng,fg->nf", grad_low, weights, preferred_element_type=jnp.float32)


def local(
    tokens,
    image_counts,
    shift_mask,
    rel_index,
    norm1_gain,
    norm1_bias,
    qkv_weight,
    q_bias,
    v_bias,
    rel_table,
    proj_weight,
    proj_bias,
    norm2_gain,
    norm2_bias,
    fc1_weight,
    fc1_bias,
    fc2_weight,
    fc2_bias,
    out_grad,
):
    images = tokens.shape[0]
    width = tokens.shape[2]
    heads = rel_table.shape[1] * lax.axis_size("shard")
    head_dim = width // heads
    scale = head_dim ** (-0.5)
    valid = (jnp.arange(images, dtype=jnp.int32) < image_counts[0]).astype(jnp.float32)[
        :, None, None
    ]
    gathered = (
        lax.all_gather(norm1_gain, "shard", axis=0, tiled=True),
        lax.all_gather(norm1_bias, "shard", axis=0, tiled=True),
        lax.all_gather(qkv_weight, "shard", axis=0, tiled=True),
        lax.all_gather(q_bias, "shard", axis=0, tiled=True),
        lax.all_gather(v_bias, "shard", axis=0, tiled=True),
        lax.all_gather(rel_table, "shard", axis=1, tiled=True),
        lax.all_gather(proj_weight, "shard", axis=0, tiled=True),
        lax.all_gather(proj_bias, "shard", axis=0, tiled=True),
        lax.all_gather(norm2_gain, "shard", axis=0, tiled=True),
        lax.all_gather(norm2_bias, "shard", axis=0, tiled=True),
        lax.all_gather(fc1_weight, "shard", axis=0, tiled=True),
        lax.all_gather(fc1_bias, "shard", axis=0, tiled=True),
        lax.all_gather(fc2_weight, "shard", axis=0, tiled=True),
        lax.all_gather(fc2_bias, "shard", axis=0, tiled=True),
    )
    small = [item.astype(jnp.float32) for item in gathered]
    gain_one, shift_one, qbias, vbias, table = (small[0], small[1], small[3], small[4], small[5])
    pbias, gain_two, shift_two, fbias_one, fbias_two = (
        small[7],
        small[8],
        small[9],
        small[11],
        small[13],
    )
    inputs = tokens.astype(jnp.float32)
    normed = layer_norm(inputs, gain_one, shift_one).astype(jnp.bfloat16)
    win_rows = to_windows(normed)
    windows = win_rows.shape[0]
    wtok = win_rows.shape[1]
    flat_rows = win_rows.reshape(-1, width)
    qkv = jnp.dot(flat_rows, gathered[2], preferred_element_type=jnp.float32).reshape(
        windows, wtok, 3 * width
    )
    qkv = qkv + jnp.concatenate([qbias, jnp.zeros_like(qbias), vbias])
    queries = (
        (qkv[..., :width] * scale).astype(jnp.bfloat16).reshape(windows, wtok, heads, head_dim)
    )
    key_rows = (
        qkv[..., width : 2 * width].astype(jnp.bfloat16).reshape(windows, wtok, heads, head_dim)
    )
    value_rows = qkv[..., 2 * width :].astype(jnp.bfloat16).reshape(windows, wtok, heads, head_dim)
    onehot = (
        rel_index.reshape(-1)[:, None] == jnp.arange(table.shape[0], dtype=jnp.int32)[None, :]
    ).astype(jnp.float32)
    position_bias = (
        jnp.dot(onehot, table, precision=HIGH).reshape(wtok, wtok, heads).transpose(2, 0, 1)
    )
    mask_add = jnp.where(shift_mask == 1, 0.0, -100.0).astype(jnp.float32)

    def scores_of(query_part, key_part):
        raw = jnp.einsum(
            "wqhd,wkhd->whqk", query_part, key_part, preferred_element_type=jnp.float32
        )
        total = (
            raw.reshape(images, -1, heads, wtok, wtok)
            + position_bias[None, None]
            + mask_add[None, :, None]
        )
        return total.reshape(windows, heads, wtok, wtok)

    scores = scores_of(queries, key_rows)
    log_total = jax.nn.logsumexp(scores, -1, keepdims=True)
    probs_low = jnp.exp(scores - log_total).astype(jnp.bfloat16)
    attended = jnp.einsum(
        "whqk,wkhd->wqhd", probs_low, value_rows, preferred_element_type=jnp.float32
    )
    attended = attended.astype(jnp.bfloat16).reshape(windows * wtok, width)
    projected = jnp.dot(attended, gathered[6], preferred_element_type=jnp.float32) + pbias
    middle = inputs + from_windows(projected.reshape(windows, wtok, width), images)
    normed_two = layer_norm(middle, gain_two, shift_two).astype(jnp.bfloat16).reshape(-1, width)
    hidden_pre = jnp.dot(normed_two, gathered[10], preferred_element_type=jnp.float32) + fbias_one
    hidden_act = jax.nn.gelu(hidden_pre, approximate=False).astype(jnp.bfloat16)
    branch = jnp.dot(hidden_act, gathered[12], preferred_element_type=jnp.float32) + fbias_two
    result = middle + branch.reshape(inputs.shape)
    block_out = (result * valid).astype(jnp.bfloat16)
    back_params = (
        lax.all_gather(norm1_gain, "shard", axis=0, tiled=True),
        lax.all_gather(norm1_bias, "shard", axis=0, tiled=True),
        lax.all_gather(qkv_weight, "shard", axis=0, tiled=True),
        lax.all_gather(q_bias, "shard", axis=0, tiled=True),
        lax.all_gather(v_bias, "shard", axis=0, tiled=True),
        lax.all_gather(rel_table, "shard", axis=1, tiled=True),
        lax.all_gather(proj_weight, "shard", axis=0, tiled=True),
        lax.all_gather(proj_bias, "shard", axis=0, tiled=True),
        lax.all_gather(norm2_gain, "shard", axis=0, tiled=True),
        lax.all_gather(norm2_bias, "shard", axis=0, tiled=True),
        lax.all_gather(fc1_weight, "shard", axis=0, tiled=True),
        lax.all_gather(fc1_bias, "shard", axis=0, tiled=True),
        lax.all_gather(fc2_weight, "shard", axis=0, tiled=True),
        lax.all_gather(fc2_bias, "shard", axis=0, tiled=True),
    )
    upstream = out_grad.astype(jnp.float32) * valid
    flat_up = upstream.reshape(-1, width)
    up_low = flat_up.astype(jnp.bfloat16)
    grad_fbias_two = jnp.sum(flat_up, 0)
    grad_fc2 = weight_grad(hidden_act, up_low)
    grad_act = back_product(up_low, back_params[12])
    gelu_out, gelu_back = jax.vjp(partial(jax.nn.gelu, approximate=False), hidden_pre)
    grad_pre = gelu_back(grad_act)[0]
    grad_fbias_one = jnp.sum(grad_pre, 0)
    pre_low = grad_pre.astype(jnp.bfloat16)
    grad_fc1 = weight_grad(normed_two, pre_low)
    grad_normed_two = back_product(pre_low, back_params[10])
    norm_out, norm_back = jax.vjp(
        layer_norm, middle, back_params[8].astype(jnp.float32), back_params[9].astype(jnp.float32)
    )
    grad_mid_part, grad_gain_two, grad_shift_two = norm_back(grad_normed_two.reshape(middle.shape))
    grad_middle = upstream + grad_mid_part
    grad_pbias = row_sum(grad_middle)
    proj_low = to_windows(grad_middle.astype(jnp.bfloat16)).reshape(-1, width)
    grad_projw = weight_grad(attended, proj_low)
    grad_att = (
        back_product(proj_low, back_params[6])
        .astype(jnp.bfloat16)
        .reshape(windows, wtok, heads, head_dim)
    )
    scores_again = scores_of(queries, key_rows)
    probs = jnp.exp(scores_again - log_total)
    probs_again = probs.astype(jnp.bfloat16)
    grad_values = jnp.einsum(
        "whqk,wqhd->wkhd", probs_again, grad_att, preferred_element_type=jnp.float32
    )
    grad_probs = jnp.einsum(
        "wqhd,wkhd->whqk", grad_att, value_rows, preferred_element_type=jnp.float32
    )
    grad_scores = probs * (grad_probs - jnp.sum(grad_probs * probs, -1, keepdims=True))
    per_pair = jnp.sum(grad_scores, 0).reshape(heads, -1)
    grad_table = jnp.einsum("pt,hp->th", onehot, per_pair, precision=HIGH)
    scores_low = grad_scores.astype(jnp.bfloat16)
    grad_queries = (
        jnp.einsum("whqk,wkhd->wqhd", scores_low, key_rows, preferred_element_type=jnp.float32)
        * scale
    )
    grad_keys = jnp.einsum(
        "whqk,wqhd->wkhd", scores_low, queries, preferred_element_type=jnp.float32
    )
    grad_queries = grad_queries.reshape(windows, wtok, width)
    grad_keys = grad_keys.reshape(windows, wtok, width)
    grad_values = grad_values.reshape(windows, wtok, width)
    grad_qbias = row_sum(grad_queries)
    grad_vbias = row_sum(grad_values)
    qkv_low = (
        jnp.concatenate([grad_queries, grad_keys, grad_values], -1)
        .astype(jnp.bfloat16)
        .reshape(-1, 3 * width)
    )
    grad_qkvw = weight_grad(flat_rows, qkv_low)
    grad_normed = from_windows(
        back_product(qkv_low, back_params[2]).reshape(windows, wtok, width), images
    )
    norm_first, norm_back_one = jax.vjp(
        layer_norm, inputs, back_params[0].astype(jnp.float32), back_params[1].astype(jnp.float32)
    )
    grad_in_part, grad_gain_one, grad_shift_one = norm_back_one(grad_normed)
    tokens_grad = grad_middle + grad_in_part
    all_share = (
        lax.psum_scatter(
            grad_gain_one.astype(jnp.bfloat16), "shard", scatter_dimension=0, tiled=True
        ).astype(jnp.float32),
        lax.psum_scatter(
            grad_shift_one.astype(jnp.bfloat16), "shard", scatter_dimension=0, tiled=True
        ).astype(jnp.float32),
        lax.psum_scatter(
            grad_qkvw.astype(jnp.bfloat16), "shard", scatter_dimension=0, tiled=True
        ).astype(jnp.float32),
        lax.psum_scatter(
            grad_qbias.astype(jnp.bfloat16), "shard", scatter_dimension=0, tiled=True
        ).astype(jnp.float32),
        lax.psum_scatter(
            grad_vbias.astype(jnp.bfloat16), "shard", scatter_dimension=0, tiled=True
        ).astype(jnp.float32),
        lax.psum_scatter(
            grad_table.astype(jnp.bfloat16), "shard", scatter_dimension=1, tiled=True
        ).astype(jnp.float32),
        lax.psum_scatter(
            grad_projw.astype(jnp.bfloat16), "shard", scatter_dimension=0, tiled=True
        ).astype(jnp.float32),
        lax.psum_scatter(
            grad_pbias.astype(jnp.bfloat16), "shard", scatter_dimension=0, tiled=True
        ).astype(jnp.float32),
        lax.psum_scatter(
            grad_gain_two.astype(jnp.bfloat16), "shard", scatter_dimension=0, tiled=True
        ).astype(jnp.float32),
        lax.psum_scatter(
            grad_shift_two.astype(jnp.bfloat16), "shard", scatter_dimension=0, tiled=True
        ).astype(jnp.float32),
        lax.psum_scatter(
            grad_fc1.astype(jnp.bfloat16), "shard", scatter_dimension=0, tiled=True
        ).astype(jnp.float32),
        lax.psum_scatter(
            grad_fbias_one.astype(jnp.bfloat16), "shard", scatter_dimension=0, tiled=True
        ).astype(jnp.float32),
        lax.psum_scatter(
            grad_fc2.astype(jnp.bfloat16), "shard", scatter_dimension=0, tiled=True
        ).astype(jnp.float32),
        lax.psum_scatter(
            grad_fbias_two.astype(jnp.bfloat16), "shard", scatter_dimension=0, tiled=True
        ).astype(jnp.float32),
    )
    totals = lax.psum(
        (
            all_share[0],
            all_share[1],
            all_share[2],
            all_share[3],
            all_share[4],
            all_share[5],
            all_share[6],
            all_share[7],
            all_share[8],
            all_share[9],
            all_share[10],
            all_share[11],
            all_share[12],
            all_share[13],
        ),
        "replica",
    )
    return (
        block_out,
        tokens_grad,
        totals[0],
        totals[1],
        totals[2],
        totals[3],
        totals[4],
        totals[5],
        totals[6],
        totals[7],
        totals[8],
        totals[9],
        totals[10],
        totals[11],
        totals[12],
        totals[13],
    )


def solution(mesh):
    placed = (
        P(("replica", "shard"), None, None),
        P(("replica", "shard")),
        P(),
        P(),
        P("shard"),
        P("shard"),
        P("shard", None),
        P("shard"),
        P("shard"),
        P(None, "shard"),
        P("shard", None),
        P("shard"),
        P("shard"),
        P("shard"),
        P("shard", None),
        P("shard"),
        P("shard", None),
        P("shard"),
        P(("replica", "shard"), None, None),
    )
    return jax.shard_map(
        local,
        mesh=mesh,
        in_specs=placed,
        out_specs=(
            P(("replica", "shard"), None, None),
            P(("replica", "shard"), None, None),
            P("shard"),
            P("shard"),
            P("shard", None),
            P("shard"),
            P("shard"),
            P(None, "shard"),
            P("shard", None),
            P("shard"),
            P("shard"),
            P("shard"),
            P("shard", None),
            P("shard"),
            P("shard", None),
            P("shard"),
        ),
        check_vma=False,
    )
```

profile of v0, /device:TPU:1, one launch (start us, length us, event | category | flops | bytes accessed | tf_op | source)
XLA Modules:
  0.0 769.8 jit_solution(2766020518451182277)
XLA Ops:
  9.5 5.2 all-gather
  14.7 4.6 all-gather.1
  26.0 5.0 all-gather.2
  31.0 5.0 all-gather.3
  36.0 5.0 all-gather.4
  41.6 4.6 all-gather.5
  46.2 4.6 all-gather.6
  50.8 4.6 all-gather.7
  56.0 5.0 all_gather.59
  61.0 5.1 all_gather.53
  69.2 15.3 %all_gather.54 = bf16[512,512]{1,0:T(8,128)(2,1)} all-gather(bf16[256,512]{1,0:T(8,128)(2,1)} %param.29), channel_id=1, replica_groups=mesh['replica'=64,'shard'=2] {'shard'}, dimensions={0}, use_global_device_ids=true | all-gather | bytes 786432 | tf_op jit(solution)/shard_map/all_gather | solution.py:93
  86.0 2.6 convert_element_type.203
  90.6 3.5 fusion.75
  95.6 3.1 copy.166
  98.7 4.3 copy.167
  103.0 3.1 copy.165
  106.1 6.1 fusion.6
  112.3 3.9 exponential_reduce_fusion
  117.0 3.4 convert_bitcast_fusion.1
  120.5 3.8 copy.130
  124.2 4.9 reshape.223
  133.3 3.8 copy.131
  137.1 3.9 reshape.224
  145.1 2.9 reshape.225
  154.8 26.9 %multiply_convert_fusion = (bf16[1176,2048]{1,0:T(8,128)(2,1)}, f32[1176,2048]{1,0:T(8,128)}, f32[1176,2048]{1,0:T(8,128)}) fusion(f32[2048]{0:T(1024)S(1)} %convert_element_type.196, bf16[1176,512]{1,0:T(8,128)(2,1)} %reshape.226, bf16[512,2048]{1,0:T(8,128)(2,1)} %all-gather.14.cloned.1.call-done), kind=kOutput, calls=%fused_computation.8 | convolution fusion | flops 2625208320 | bytes 27394048 | tf_op jit(solution)/shard_map/dot_general | solution.py:157
  181.7 7.2 convolution_add_fusion.3
  188.8 3.1 reshape.227
  191.9 11.7 %fusion.77 = (bf16[2048]{0:T(1024)(128)(2,1)S(1)}, bf16[1176,2048]{1,0:T(8,128)(2,1)S(1)}) fusion(f32[1176,2048]{1,0:T(8,128)} %get-tuple-element.50, f32[1176,2048]{1,0:T(8,128)} %get-tuple-element.63, bf16[1176,512]{1,0:T(8,128)(2,1)} %convert_element_type.203, bf16[2048,512]{1,0:T(8,128)(2,1)} %all-gather.16.cloned.1.call-done), kind=kOutput, calls=%fused_computation.145 | convolution fusion | flops 2502375424 | bytes 27389952 | tf_op jit(solution)/shard_map/ng,fg->nf/dot_general | solution.py:54
  203.7 4.2 fusion.76
  208.0 3.0 reshape.228
  211.0 2.5 multiply_reduce_fusion.2
  215.5 2.4 fusion.70
  229.1 4.1 reshape.275
  233.3 7.8 %copy.134 = bf16[24,49,16,32]{1,3,2,0:T(8,128)(2,1)} copy(bf16[24,49,16,32]{3,2,1,0:T(8,128)(2,1)} %reshape.275) | data formatting | bytes 2408448 | tf_op jit(solution)/shard_map/reshape | solution.py:201
  241.1 14.2 %multiply_reduce_fusion = (f32[24,16,49]{2,1,0:T(8,128)S(1)}, f32[24,16,49,49]{2,3,1,0:T(8,128)}) fusion(f32[24,16,49,49]{2,3,1,0:T(8,128)} %copy-done, f32[24,16,49]{2,1,0:T(8,128)S(1)} %log_add_fusion, f32[24,49,49]{1,2,0:T(8,128)S(1)} %bitcast.102, f32[16,49,49]{1,2,0:T(8,128)S(1)} %copy-done.12, bf16[24,49,16,32]{1,3,2,0:T(8,128)(2,1)} %copy.134, ...), kind=kOutput, calls=%fused_computation.2 | convolution fusion | flops 63598080 | bytes 10319008 | tf_op jit(solution)/shard_map/wqhd,wkhd->whqk/dot_general | solution.py:209
  255.3 9.3 %fusion.69 = (f32[16,49,49]{1,2,0:T(8,128)S(1)}, bf16[24,16,49,49]{2,3,1,0:T(8,128)(2,1)S(1)}) fusion(f32[24,16,49,49]{2,3,1,0:T(8,128)} %get-tuple-element.67, f32[24,16,49]{2,1,0:T(8,128)S(1)} %get-tuple-element.66, f32[24,16,49]{2,1,0:T(8,128)S(1)} %log_add_fusion, f32[24,49,49]{1,2,0:T(8,128)S(1)} %bitcast.103, f32[24,16,49,49]{2,3,1,0:T(8,128)} %copy-done, ...), kind=kLoop, calls=%fused_computation.138 | loop fusion | flops 6415472 | bytes 9908192 | tf_op jit(solution)/shard_map/reduce_sum | solution.py:213
  264.6 4.2 convert_bitcast_fusion
  268.9 4.5 bitcast_convert_fusion.1
  275.4 3.3 convolution_convert_fusion.3
  278.8 5.6 copy.150
  284.4 5.1 concatenate.65
  289.5 5.6 copy.151
  295.1 4.9 concatenate.66
  300.1 10.7 %bitcast_convert_fusion = (bf16[24,49,16,32]{1,3,2,0:T(8,128)(2,1)S(1)}, f32[24,16,32,49]{3,2,1,0:T(8,128)}) fusion(bf16[24,49,16,32]{1,3,2,0:T(8,128)(2,1)} %copy.134, f32[24,16,49,49]{2,3,1,0:T(8,128)} %copy-done, f32[24,16,49]{2,1,0:T(8,128)S(1)} %log_add_fusion, f32[24,49,49]{1,2,0:T(8,128)S(1)} %bitcast.104, f32[16,49,49]{1,2,0:T(8,128)S(1)} %copy-done.12), kind=kOutput, calls=%fused_computation.25 | convolution fusion | flops 63297024 | bytes 8964256 | tf_op jit(solution)/shard_map/whqk,wqhd->wkhd/dot_general | solution.py:206
  314.5 2.9 concatenate.67
  317.4 6.0 fusion.24
  323.5 6.8 convolution_convert_fusion
  330.4 7.1 convolution_convert_fusion.1
  339.5 5.8 copy.162
  345.3 7.5 copy.163
  352.8 5.6 copy.164
  358.4 6.5 reshape.263
  364.9 6.5 reshape.264
  371.3 7.4 reshape.265
  378.8 5.6 fusion.49
  386.1 2.6 reshape.232
  392.2 3.4 bitcast_reduce_fusion
  395.7 3.6 bitcast_reduce_fusion.1
  402.2 3.3 reshape.233
  405.5 2.5 fusion.40
  409.5 8.6 %all-reduce.10 = (bf16[512]{0:T(512)(128)(2,1)S(1)}, bf16[512]{0:T(512)(128)(2,1)S(1)}, bf16[512]{0:T(512)(128)(2,1)S(1)}, bf16[512]{0:T(512)(128)(2,1)S(1)}, bf...) all-reduce(bf16[512]{0:T(512)(128)(2,1)S(1)} %get-tuple-element.18,, ...), channel_id=2, replica_groups=mesh['replica'=64,'shard'=2] {'shard'}, use_global_device_ids=true, to_apply=%region_12.13.clone | all-reduce | flops 6144 | bytes 24576
  418.3 4.0 add_add_fusion.3
  422.4 14.3 %reduce-scatter.12.cloned.1.call-done = bf16[256,2048]{1,0:T(8,128)(2,1)} async-done(((bf16[512,2048]{1,0:T(8,128)(2,1)}), bf16[256,2048]{1,0:T(8,128)(2,1)}) %reduce-scatter.12.cloned.1.call-update) | async-done | bytes 1048592 | tf_op jit(solution)/shard_map/reduce_scatter | solution.py:273
  436.6 325.9 %all-reduce.12 = (f32[256]{0:T(256)}, f32[256]{0:T(256)}, f32[256,1536]{1,0:T(8,128)}, f32[256]{0:T(256)}, f32[256]{0:T(256)}, /*index=5*/f32[169,8]{0,1:T(8,128...) all-reduce(f32[256]{0:T(256)S(1)} %get-tuple-element.81, ...), channel_id=1, replica_groups=mesh['replica'=64,'shard'=2] {'replica'}, use_global_device_ids=true, to_apply=%region_13.14 | all-reduce | flops 1577288 | bytes 9469872 | tf_op jit(solution)/shard_map/psum | solution.py:286
  (218 shorter events, 62.6 us)
Async XLA Ops:
  7.2 2.3 copy-start.40
  7.2 7.5 copy-start.41
  7.2 12.1 %copy-start.1 = (bf16[6,196,512]{2,1,0:T(8,128)(2,1)S(1)}, bf16[6,196,512]{2,1,0:T(8,128)(2,1)}, u32[]{:S(2)}) copy-start(bf16[6,196,512]{2,1,0:T(8,128)(2,1)} %param.19) | copy-start | bytes 3612676
  7.2 83.4 %all-gather.12.cloned.1.call-start = ((), (), s32[]{:S(2)}) async-start(), calls=%async_computation.5 | async-start | bytes 2359296 | tf_op jit(solution)/shard_map/all_gather | solution.py:89
  7.9 146.8 %all-gather.14.cloned.1.call-start = ((), (), s32[]{:S(2)}) async-start(), calls=%async_computation.6 | async-start | bytes 3145728 | tf_op jit(solution)/shard_map/all_gather | solution.py:97
  8.7 173.0 %all-gather.16.cloned.1.call-start = ((), (), s32[]{:S(2)}) async-start(), calls=%async_computation.7 | async-start | bytes 3145728 | tf_op jit(solution)/shard_map/all_gather | solution.py:99
  9.4 412.9 %reduce-scatter.8.cloned.1.call-start = ((), (), s32[]{:S(2)}) async-start(), calls=%async_computation.9 | async-start | bytes 12288 | tf_op jit(solution)/shard_map/reduce_scatter | solution.py:258
  14.7 6.1 copy-start.28
  19.6 1.2 copy-start.21
  20.2 0.6 copy-start.26
  20.2 0.6 copy-start.23
  23.0 3.0 copy-start.42
  23.0 8.0 %copy-start.43 = (bf16[256]{0:T(256)(128)(2,1)S(1)}, bf16[256]{0:T(256)(128)(2,1)}, u32[]{:S(2)}) copy-start(bf16[256]{0:T(256)(128)(2,1)} %param.27) | copy-start | bytes 1540
  23.0 13.0 %copy-start.44 = (bf16[256]{0:T(256)(128)(2,1)S(1)}, bf16[256]{0:T(256)(128)(2,1)}, u32[]{:S(2)}) copy-start(bf16[256]{0:T(256)(128)(2,1)} %param.30) | copy-start | bytes 1540
  23.0 18.6 %copy-start.45 = (bf16[256]{0:T(256)(128)(2,1)S(1)}, bf16[256]{0:T(256)(128)(2,1)}, u32[]{:S(2)}) copy-start(bf16[256]{0:T(256)(128)(2,1)} %param.31) | copy-start | bytes 1540
  23.0 23.2 %copy-start.46 = (bf16[256]{0:T(256)(128)(2,1)S(1)}, bf16[256]{0:T(256)(128)(2,1)}, u32[]{:S(2)}) copy-start(bf16[256]{0:T(256)(128)(2,1)} %param.32) | copy-start | bytes 1540
  23.0 27.8 %copy-start.47 = (bf16[256]{0:T(256)(128)(2,1)S(1)}, bf16[256]{0:T(256)(128)(2,1)}, u32[]{:S(2)}) copy-start(bf16[256]{0:T(256)(128)(2,1)} %param.36) | copy-start | bytes 1540
  23.0 33.0 %copy-start.34 = (bf16[1024]{0:T(1024)(128)(2,1)S(1)}, bf16[1024]{0:T(1024)(128)(2,1)}, u32[]{:S(2)}) copy-start(bf16[1024]{0:T(1024)(128)(2,1)} %param.34) | copy-start | bytes 6148
  23.1 38.0 %copy-start.33 = (bf16[169,8]{0,1:T(8,128)(2,1)S(1)}, bf16[169,8]{0,1:T(8,128)(2,1)}, u32[]{:S(2)}) copy-start(bf16[169,8]{0,1:T(8,128)(2,1)} %param.28) | copy-start | bytes 8116
  23.1 43.0 %copy-start.30 = (s32[49,49]{1,0:T(8,128)S(1)}, s32[49,49]{1,0:T(8,128)}, u32[]{:S(2)}) copy-start(s32[49,49]{1,0:T(8,128)} %param.22) | copy-start | bytes 28816
  23.1 43.1 %copy-start.25 = (s32[4,49,49]{2,0,1:T(4,128)S(1)}, s32[4,49,49]{2,0,1:T(4,128)}, u32[]{:S(2)}) copy-start(s32[4,49,49]{2,0,1:T(4,128)} %param.21) | copy-start | bytes 115252
  25.2 59.4 %copy-start.16 = (bf16[6,196,512]{2,1,0:T(8,128)(2,1)S(1)}, bf16[6,196,512]{2,1,0:T(8,128)(2,1)}, u32[]{:S(2)}) copy-start(bf16[6,196,512]{2,1,0:T(8,128)(2,1)} %param.37) | copy-start | bytes 3612676
  26.0 60.0 %copy-start.37 = (f32[6]{0:T(128)}, f32[6]{0:T(128)S(1)}, u32[]{:S(2)}) copy-start(f32[6]{0:T(128)S(1)} %compare_convert_fusion) | copy-start | bytes 76
  66.2 19.8 %copy-start.31 = (s32[2401]{0:T(1024)}, s32[2401]{0:T(1024)S(1)}, u32[]{:S(2)}) copy-start(s32[2401]{0:T(1024)S(1)} %eq.21) | copy-start | bytes 28816
  69.2 47.0 %copy-start.11 = (f32[16,49,49]{1,2,0:T(8,128)}, f32[16,49,49]{1,2,0:T(8,128)S(1)}, u32[]{:S(2)}) copy-start(f32[16,49,49]{1,2,0:T(8,128)S(1)} %copy.126) | copy-start | bytes 460996
  86.0 4.1 copy-start.18
  112.2 4.8 copy-start
  112.3 4.8 copy-start.9
  124.2 5.0 copy-start.36
  141.0 1.1 slice-start
  141.0 1.8 slice-start.1
  154.8 26.9 %copy-start.35 = (f32[2,1,256]{2,1,0:T(1,128)S(1)}, f32[2,1,256]{2,1,0:T(1,128)}, u32[]{:S(2)}) copy-start(f32[2,1,256]{2,1,0:T(1,128)} %convert_element_type.245) | copy-start | bytes 6148
  191.9 11.8 %copy-start.39 = (bf16[512,2048]{1,0:T(8,128)(2,1)S(1)}, bf16[512,2048]{1,0:T(8,128)(2,1)}, u32[]{:S(2)}) copy-start(bf16[512,2048]{1,0:T(8,128)(2,1)} %all-gather.14.cloned.1.call-done) | copy-start | bytes 6291460
  203.7 4.3 copy-start.49
  211.0 2.5 copy-start.4
  213.4 1.7 copy-start.15
  213.4 2.0 copy-start.17
  213.4 2.0 copy-start.38
  217.9 1.4 copy-start.13
  224.1 2.9 copy-start.20
  233.3 7.8 %copy-start.12 = (f32[16,49,49]{1,2,0:T(8,128)S(1)}, f32[16,49,49]{1,2,0:T(8,128)}, u32[]{:S(2)}) copy-start(f32[16,49,49]{1,2,0:T(8,128)} %copy-done.11) | copy-start | bytes 460996
  255.3 9.3 %copy-start.7 = (bf16[24,49,512]{1,2,0:T(8,128)(2,1)S(1)}, bf16[24,49,512]{1,2,0:T(8,128)(2,1)}, u32[]{:S(2)}) copy-start(bf16[24,49,512]{1,2,0:T(8,128)(2,1)} %copy.166) | copy-start | bytes 3612676
  264.6 4.3 copy-start.8
  268.9 5.0 copy-start.32
  275.4 146.9 %reduce-scatter.10.cloned.1.call-start = ((), (), s32[]{:S(2)}) async-start(), calls=%async_computation.10 | async-start | bytes 786432 | tf_op jit(solution)/shard_map/reduce_scatter | solution.py:261
  300.0 122.3 %reduce-scatter.6.cloned.1.call-start = ((), (), s32[]{:S(2)}) async-start(), calls=%async_computation.8 | async-start | bytes 2359296 | tf_op jit(solution)/shard_map/reduce_scatter | solution.py:249
  310.8 1.7 copy-start.5
  317.4 6.0 copy-start.19
  323.4 98.9 %reduce-scatter.14.cloned.1.call-start = ((), (), s32[]{:S(2)}) async-start(), calls=%async_computation.12 | async-start | bytes 3145728 | tf_op jit(solution)/shard_map/reduce_scatter | solution.py:279
  330.3 7.2 copy-start.48
  330.3 106.3 %reduce-scatter.12.cloned.1.call-start = ((), (), s32[]{:S(2)}) async-start(), calls=%async_computation.11 | async-start | bytes 3145728 | tf_op jit(solution)/shard_map/reduce_scatter | solution.py:273
  330.4 9.1 %copy-start.10 = (bf16[24,49,16,32]{1,3,2,0:T(8,128)(2,1)S(1)}, bf16[24,49,16,32]{1,3,2,0:T(8,128)(2,1)}, u32[]{:S(2)}) copy-start(bf16[24,49,16,32]{1,3,2,0:T(8,128)(2,1)} %get-tuple-element.68) | copy-start | bytes 3612676
  345.3 7.5 copy-start.6
  388.8 1.5 copy-start.14
  402.2 3.3 copy-start.2
  402.2 3.3 copy-start.22
  402.2 3.3 copy-start.29
  405.4 2.6 copy-start.27
  405.4 2.6 copy-start.3
  405.5 2.6 copy-start.24
Sparse Core Ops, SparseCore 0:
  9.7 34.4 all-gather.11
  45.9 39.5 all-gather.13
  87.1 36.5 all-gather.15
  275.5 19.2 reduce-scatter.7
  300.2 24.5 reduce-scatter.9
  327.6 31.9 reduce-scatter.5
  362.6 35.3 reduce-scatter.13
  401.0 35.6 reduce-scatter.11
where the time goes:
time: 782 us; the launch traced here: 770 us
  blocking collectives  398 us (51%)
  local copies, waits for them, and re-layouts  154 us (20%)
  matrix products  132 us (17%)
  other arithmetic  51.3 us (7%)
  between operations  17.5 us (2%)
  waiting for transfers between devices  16.5 us (2%)
    psum x1, blocking collectives, local(): lax.psum((all_share[0], all_share[1], all_share[2], all_share[3], all_sha...  326 us
    concatenate x9, local copies, waits for them, and re-layouts, local(): jnp.concatenate([grad_queries, grad_keys, grad_values], -1)  52.2 us
    dot_general x1, matrix products, local(): jnp.dot(normed_two, gathered[10], preferred_element_type=jnp.float32)  26.9 us
    dot_general x4, matrix products, back_product(): jnp.einsum('ng,fg->nf', grad_low, weights, preferred_element_type=jnp.flo...  23.7 us
    dot_general x4, matrix products, weight_grad(): jnp.einsum('nf,ng->fg', left, right, preferred_element_type=jnp.float32)  23.2 us
  transfers between devices with their start and end apart: 8, of which 1 were waited for; matrix products, arithmetic and copies ran while one was open for 31% of the time, Pallas kernels for 0%

commit v1 on v0

v1 whole, which is shorter than its diff:
```python
from functools import partial

import jax
import jax.numpy as jnp
import numpy as np
from jax import lax
from jax.experimental import pallas as pl
from jax.experimental.pallas import tpu as pltpu
from jax.sharding import PartitionSpec as P

WIN = 7
SIDE = 14
SHIFT = 3
EPSILON = 1e-05
MASKED = -1e30
WTOK = WIN * WIN
ROWS = 56
WPAD = 64
BLOCK = 512
F32 = jnp.float32
BF16 = jnp.bfloat16


def nn(left, right):
    return jnp.dot(left, right, preferred_element_type=F32)


def nt(left, right):
    return lax.dot_general(left, right, (((1,), (1,)), ((), ())), preferred_element_type=F32)


def tn(left, right):
    return lax.dot_general(left, right, (((0,), (0,)), ((), ())), preferred_element_type=F32)


def window_places():
    place = np.zeros((4 * ROWS, SIDE * SIDE), np.float32)
    for window in range(4):
        for cell in range(WTOK):
            i = window // 2 * WIN + cell // WIN
            j = window % 2 * WIN + cell % WIN
            source = (i + SHIFT) % SIDE * SIDE + (j + SHIFT) % SIDE
            place[window * ROWS + cell, source] = 1
    return place


def normalize(values):
    center = values - jnp.mean(values, -1, keepdims=True)
    rate = lax.rsqrt(jnp.mean(center * center, -1, keepdims=True) + EPSILON)
    return center * rate, rate


def norm_back(grad, unit, rate, gain):
    scaled = grad * gain
    return rate * (
        scaled
        - jnp.mean(scaled, -1, keepdims=True)
        - unit * jnp.mean(scaled * unit, -1, keepdims=True)
    )


def normal_parts(v):
    size = jnp.abs(v) * 0.7071067811865476
    bell = jnp.exp(-0.5 * v * v)
    t = 1.0 / (1.0 + 0.3275911 * size)
    tail = t * (
        0.254829592
        + t * (-0.284496736 + t * (1.421413741 + t * (-1.453152027 + t * 1.061405429)))
    )
    half = 0.5 * tail * bell
    return jnp.where(v < 0, half, 1.0 - half), 0.3989422804014327 * bell


def col_sum(values):
    return jnp.sum(values, 0, keepdims=True)


def pad_window(values):
    return jnp.concatenate([values, jnp.zeros((WPAD - ROWS, values.shape[1]), F32)], 0)


def layer_kernel(
    heads,
    count_ref,
    tok_ref,
    up_ref,
    place_ref,
    back_ref,
    hmask_ref,
    bias_ref,
    w_ref,
    vec_ref,
    out_ref,
    tg_ref,
    acts_ref,
    small_ref,
    pair_ref,
    qkv_s,
    prob_s,
    att_s,
    gatt_s,
    dqkv_s,
):
    image = pl.program_id(0)
    valid = (image < count_ref[0]).astype(F32)
    width = tok_ref.shape[2]
    scale = (width // heads) ** (-0.5)
    lanes = 128
    per = 4
    groups = heads // per

    @pl.when(image == 0)
    def _():
        small_ref[...] = jnp.zeros_like(small_ref)
        pair_ref[...] = jnp.zeros_like(pair_ref)

    def vec(row, count=1):
        return vec_ref[row : row + count, :].reshape(1, count * BLOCK)

    def note(row, values):
        small_ref[row : row + 1, :] += col_sum(values)

    def keep(block, values):
        acts_ref[0, :, block * BLOCK : (block + 1) * BLOCK] = values

    hmask = hmask_ref[...]
    hmask_f = hmask.astype(F32)

    def spread(part):
        return jnp.concatenate([part] * per, 0) * hmask

    def fold(full):
        full = full * hmask_f
        total = full[:WPAD]
        for h in range(1, per):
            total = total + full[h * WPAD : (h + 1) * WPAD]
        return total[:ROWS]

    inputs = nn(place_ref[...], tok_ref[0])
    unit_one, rate_one = normalize(inputs)
    normed = (unit_one * vec(0) + vec(1)).astype(BF16)
    keep(0, normed)
    for n in range(3):
        part = nn(normed, w_ref[n])
        if n == 0:
            part = (part + vec(2)) * scale
        if n == 2:
            part = part + vec(3)
        for w in range(4):
            qkv_s[w, :, n * BLOCK : (n + 1) * BLOCK] = pad_window(
                part[w * ROWS : (w + 1) * ROWS]
            ).astype(BF16)

    for w in range(4):
        for g in range(groups):
            at = slice(g * lanes, (g + 1) * lanes)
            wide = slice(g * per * WPAD, (g + 1) * per * WPAD)
            q = qkv_s[w, :, g * lanes : (g + 1) * lanes]
            k = qkv_s[w, :, BLOCK + g * lanes : BLOCK + (g + 1) * lanes]
            v = qkv_s[w, :, 2 * BLOCK + g * lanes : 2 * BLOCK + (g + 1) * lanes]
            scores = nt(k, spread(q)) + bias_ref[w, :, wide]
            raised = jnp.exp(scores - jnp.max(scores, 0, keepdims=True))
            probs = raised * (1.0 / jnp.sum(raised, 0, keepdims=True))
            prob_s[w, :, wide] = probs
            att_s[w * ROWS : (w + 1) * ROWS, at] = fold(tn(probs.astype(BF16), v))
    attended = att_s[...].astype(BF16)
    keep(4, attended)
    middle = inputs + (nn(attended, w_ref[3]) + vec(4))

    unit_two, rate_two = normalize(middle)
    normed_two = (unit_two * vec(5) + vec(6)).astype(BF16)
    keep(6, normed_two)
    upstream = nn(place_ref[...], up_ref[0]) * valid
    up_low = upstream.astype(BF16)
    keep(15, up_low)
    note(7, upstream)
    branch = None
    grad_two = None
    for c in range(4):
        pre = nn(normed_two, w_ref[4 + c]) + vec(8 + c)
        below, density = normal_parts(pre)
        act = (pre * below).astype(BF16)
        keep(11 + c, act)
        grad_pre = nt(up_low, w_ref[8 + c]) * (below + pre * density)
        note(8 + c, grad_pre)
        pre_low = grad_pre.astype(BF16)
        keep(7 + c, pre_low)
        first = nn(act, w_ref[8 + c])
        second = nt(pre_low, w_ref[4 + c])
        branch = first if c == 0 else branch + first
        grad_two = second if c == 0 else grad_two + second
    result = middle + (branch + vec(7))
    out_ref[0] = nn(back_ref[...], (result * valid).astype(BF16)).astype(BF16)
    note(5, grad_two * unit_two)
    note(6, grad_two)
    grad_middle = upstream + norm_back(grad_two, unit_two, rate_two, vec(5))
    note(4, grad_middle)
    proj_low = grad_middle.astype(BF16)
    keep(5, proj_low)
    grad_att = nt(proj_low, w_ref[3])
    for w in range(4):
        gatt_s[w] = pad_window(grad_att[w * ROWS : (w + 1) * ROWS]).astype(BF16)

    for w in range(4):
        rows = slice(w * ROWS, (w + 1) * ROWS)
        for g in range(groups):
            at = slice(g * lanes, (g + 1) * lanes)
            wide = slice(g * per * WPAD, (g + 1) * per * WPAD)
            q = qkv_s[w, :, g * lanes : (g + 1) * lanes]
            k = qkv_s[w, :, BLOCK + g * lanes : BLOCK + (g + 1) * lanes]
            v = qkv_s[w, :, 2 * BLOCK + g * lanes : 2 * BLOCK + (g + 1) * lanes]
            probs = prob_s[w, :, wide]
            spread_grad = spread(gatt_s[w, :, at])
            grad_v = nn(probs.astype(BF16), spread_grad)
            grad_probs = nt(v, spread_grad)
            weighted = probs * grad_probs
            grad_scores = weighted - probs * jnp.sum(weighted, 0, keepdims=True)
            pair_ref[:, wide] += grad_scores
            scores_low = grad_scores.astype(BF16)
            grad_k = nn(scores_low, spread(q))
            grad_q = fold(tn(scores_low, k)) * scale
            dqkv_s[rows, g * lanes : (g + 1) * lanes] = grad_q
            dqkv_s[rows, BLOCK + g * lanes : BLOCK + (g + 1) * lanes] = grad_k[:ROWS]
            dqkv_s[rows, 2 * BLOCK + g * lanes : 2 * BLOCK + (g + 1) * lanes] = grad_v[:ROWS]
    grad_one = None
    for n in range(3):
        part = dqkv_s[:, n * BLOCK : (n + 1) * BLOCK]
        if n == 0:
            note(2, part)
        if n == 2:
            note(3, part)
        low = part.astype(BF16)
        keep(1 + n, low)
        term = nt(low, w_ref[n])
        grad_one = term if n == 0 else grad_one + term
    note(0, grad_one * unit_one)
    note(1, grad_one)
    total = grad_middle + norm_back(grad_one, unit_one, rate_one, vec(0))
    high = total.astype(BF16)
    rest = (total - high.astype(F32)).astype(BF16)
    tg_ref[0] = nn(back_ref[...], high) + nn(back_ref[...], rest)


def run_layer(tokens, out_grad, count, bias, weights, vectors, heads):
    images, tokens_image, width = tokens.shape
    place = window_places()
    hmask = np.zeros((4 * WPAD, 128), np.float32)
    for h in range(4):
        hmask[h * WPAD : (h + 1) * WPAD, h * 32 : (h + 1) * 32] = 1
    hidden = weights.shape[0]

    def whole(array):
        zeros = (0,) * array.ndim
        return pl.BlockSpec(array.shape, lambda b: zeros, pipeline_mode=pl.Buffered(1))

    def per_image(*shape):
        return pl.BlockSpec((1,) + shape, lambda b: (b,) + (0,) * len(shape))

    consts = [jnp.asarray(place, BF16), jnp.asarray(place.T, BF16), jnp.asarray(hmask, BF16)]
    shared = consts + [bias, weights, vectors]
    rows = 4 * ROWS
    return pl.pallas_call(
        partial(layer_kernel, heads),
        grid=(images,),
        in_specs=[
            pl.BlockSpec(memory_space=pltpu.SMEM),
            per_image(tokens_image, width),
            per_image(tokens_image, width),
        ]
        + [whole(item) for item in shared],
        out_specs=[
            per_image(tokens_image, width),
            per_image(tokens_image, width),
            per_image(rows, 16 * BLOCK),
            pl.BlockSpec((12, BLOCK), lambda b: (0, 0)),
            pl.BlockSpec((WPAD, heads * WPAD), lambda b: (0, 0)),
        ],
        out_shape=[
            jax.ShapeDtypeStruct(tokens.shape, BF16),
            jax.ShapeDtypeStruct(tokens.shape, F32),
            jax.ShapeDtypeStruct((images, rows, 16 * BLOCK), BF16),
            jax.ShapeDtypeStruct((12, BLOCK), F32),
            jax.ShapeDtypeStruct((WPAD, heads * WPAD), F32),
        ],
        scratch_shapes=[
            pltpu.VMEM((4, WPAD, 3 * BLOCK), BF16),
            pltpu.VMEM((4, WPAD, heads * WPAD), F32),
            pltpu.VMEM((rows, BLOCK), F32),
            pltpu.VMEM((4, WPAD, BLOCK), BF16),
            pltpu.VMEM((rows, 3 * BLOCK), F32),
        ],
        compiler_params=pltpu.CompilerParams(vmem_limit_bytes=56 * 1024 * 1024),
        name="layer",
    )(count, tokens, out_grad, *shared)


def grads_kernel(left_ref, right_ref, out_ref):
    out_ref[0] = tn(left_ref[...], right_ref[...]).astype(BF16)


def run_grads(acts):
    acts = acts.reshape(-1, acts.shape[2])

    def left(m):
        return 0, jnp.where(m < 3, 0, jnp.where(m == 3, 4, jnp.where(m < 8, 6, m + 3)))

    def right(m):
        return 0, jnp.where(m < 3, m + 1, jnp.where(m == 3, 5, jnp.where(m < 8, m + 3, 15)))

    rows = acts.shape[0]
    return pl.pallas_call(
        grads_kernel,
        grid=(12,),
        in_specs=[pl.BlockSpec((rows, BLOCK), left), pl.BlockSpec((rows, BLOCK), right)],
        out_specs=pl.BlockSpec((1, BLOCK, BLOCK), lambda m: (m, 0, 0)),
        out_shape=jax.ShapeDtypeStruct((12, BLOCK, BLOCK), BF16),
        compiler_params=pltpu.CompilerParams(vmem_limit_bytes=40 * 1024 * 1024),
        name="weight_grads",
    )(acts, acts)


def pair_onehot(rel_index, rows):
    index = jnp.pad(
        rel_index.T, ((0, WPAD - WTOK), (0, WPAD - WTOK)), constant_values=-1
    ).reshape(-1)
    return (index[:, None] == jnp.arange(rows, dtype=jnp.int32)[None, :]).astype(BF16)


def score_bias(table, rel_index, shift_mask):
    rows, heads = table.shape
    bias = lax.dot_general(
        table, pair_onehot(rel_index, rows), (((0,), (1,)), ((), ())), preferred_element_type=F32
    )
    bias = bias.reshape(heads, WPAD, WPAD).transpose(1, 0, 2)
    mask = jnp.where(shift_mask == 1, 0.0, -100.0).astype(F32).transpose(0, 2, 1)
    mask = jnp.pad(mask, ((0, 0), (0, 0), (0, WPAD - WTOK)))
    mask = jnp.pad(mask, ((0, 0), (0, WPAD - WTOK), (0, 0)), constant_values=MASKED)
    return (bias[None] + mask[:, :, None, :]).reshape(4, WPAD, heads * WPAD)


def table_grad_of(pair, rel_index, rows):
    heads = pair.shape[1] // WPAD
    pair = pair.reshape(WPAD, heads, WPAD).transpose(1, 0, 2).reshape(heads, -1)
    high = pair.astype(BF16)
    rest = (pair - high.astype(F32)).astype(BF16)
    both = lax.dot_general(
        pair_onehot(rel_index, rows),
        jnp.concatenate([high, rest], 0),
        (((0,), (1,)), ((), ())),
        preferred_element_type=F32,
    )
    return both[:, :heads] + both[:, heads:]


MESH = pl.DeviceIdType.MESH
SIDE_CHIPS = 4


class Place:
    def __init__(self):
        replica = lax.axis_index("replica")
        self.hi = lax.axis_index("shard")
        self.core = lax.rem(replica, 2)
        self.at = {
            "x": self.hi * 2 + lax.rem(replica // 2, 2),
            "z": lax.rem(replica // 4, SIDE_CHIPS),
            "y": replica // 16,
        }
        self.lo = lax.rem(replica // 2, 2)

    def id_of(self, core=None, **at):
        place = dict(self.at, **at)
        core = self.core if core is None else core
        lo, hi = lax.rem(place["x"], 2), place["x"] // 2
        return (((place["y"] * SIDE_CHIPS + place["z"]) * 2 + lo) * 2 + core, hi)

    def other_core(self):
        return self.id_of(core=1 - self.core)

    def along(self, axis, step):
        return self.id_of(**{axis: lax.rem(self.at[axis] + step, SIDE_CHIPS)})


def greet(devices):
    barrier = pltpu.get_barrier_semaphore()
    for device in devices:
        pl.semaphore_signal(barrier, inc=1, device_id=device, device_id_type=MESH)
    pl.semaphore_wait(barrier, len(devices))


class Sender:
    def __init__(self, send_sem, recv_sem):
        self.send_sem, self.recv_sem, self.sent = send_sem, recv_sem, []

    def __call__(self, source, target, device):
        number = len(self.sent)
        copy = pltpu.make_async_remote_copy(
            src_ref=source,
            dst_ref=target,
            send_sem=self.send_sem.at[number],
            recv_sem=self.recv_sem.at[number],
            device_id=device,
            device_id_type=MESH,
        )
        copy.start()
        self.sent.append(copy)
        return copy

    def finish(self):
        for copy in self.sent:
            copy.wait_send()


def gather_kernel(qkv_ref, proj_ref, fc1_ref, fc2_ref, vec_ref, w_ref, v_ref, local_sem, send_sem, recv_sem):
    me = Place()
    hi, other = me.hi, 1 - me.hi
    local = []

    def load(source, target):
        copy = pltpu.make_async_copy(source, target, local_sem.at[len(local)])
        copy.start()
        local.append(copy)

    def rows_of(block):
        return pl.ds(block * 256, 256)

    for n in range(3):
        load(qkv_ref.at[:, pl.ds(n * BLOCK, BLOCK)], w_ref.at[hi, rows_of(n)])
    load(proj_ref, w_ref.at[hi, rows_of(3)])
    for m in range(4):
        for half in range(2):
            load(
                fc1_ref.at[:, pl.ds(half * 1024 + m * 256, 256)],
                w_ref.at[hi, rows_of(4 + m), pl.ds(half * 256, 256)],
            )
    load(fc2_ref, w_ref.at[hi, pl.ds(8 * 256, 1024)])
    load(vec_ref, v_ref.at[hi])

    facing = me.id_of(x=3 - me.at["x"])
    peers = [facing, me.other_core()]
    peers += [me.along(axis, step) for axis in ("y", "z") for step in (1, 2, 3)]
    greet(peers)
    send = Sender(send_sem, recv_sem)
    for copy in local:
        copy.wait()

    flows = []
    for flow, (first, second) in enumerate((("z", "y"), ("y", "z"))):
        base = flow * 1536 + me.core * 768
        outer = base + me.at[second] * 192
        flows.append((base, outer, outer + me.at[first] * 48, first, second))
    crossing = [
        send(w_ref.at[hi, pl.ds(piece, 48)], w_ref.at[hi, pl.ds(piece, 48)], facing)
        for _, _, piece, _, _ in flows
    ]
    vectors = send(v_ref.at[hi], v_ref.at[hi], facing)

    def share(start, size, axis):
        part = w_ref.at[other, pl.ds(start, size)]
        return [send(part, part, me.along(axis, step)) for step in (1, 2, 3)]

    firsts = []
    for copy, (base, outer, piece, first, second) in zip(crossing, flows):
        copy.wait_recv()
        firsts.append(share(piece, 48, first))
    seconds = []
    for copies, (base, outer, piece, first, second) in zip(firsts, flows):
        for copy in copies:
            copy.wait_recv()
        seconds.append(share(outer, 192, second))
    lasts = []
    for copies, (base, outer, piece, first, second) in zip(seconds, flows):
        for copy in copies:
            copy.wait_recv()
        part = w_ref.at[other, pl.ds(base, 768)]
        lasts.append(send(part, part, me.other_core()))
    for copy in lasts:
        copy.wait_recv()
    vectors.wait_recv()
    send.finish()


def gather_weights(qkv, proj, fc1, fc2, vectors):
    vmem = pl.BlockSpec(memory_space=pltpu.VMEM)
    return pl.pallas_call(
        gather_kernel,
        in_specs=[pl.BlockSpec(memory_space=pl.ANY)] * 5,
        out_specs=[vmem, vmem],
        out_shape=[
            jax.ShapeDtypeStruct((2, 12 * 256, BLOCK), BF16),
            jax.ShapeDtypeStruct((2,) + vectors.shape, BF16),
        ],
        scratch_shapes=[
            pltpu.SemaphoreType.DMA((14,)),
            pltpu.SemaphoreType.DMA((17,)),
            pltpu.SemaphoreType.DMA((17,)),
        ],
        compiler_params=pltpu.CompilerParams(
            collective_id=0, has_side_effects=True, vmem_limit_bytes=30 * 1024 * 1024
        ),
        name="gather_weights",
    )(qkv, proj, fc1, fc2, vectors)


ORDERS = (("x", "y", "z"), ("y", "z", "x"), ("z", "x", "y"))
STAGE_ROWS = (256, 64, 16)


def add_up(target, at, sources, rows, step):
    def body(i, carry):
        total = None
        for ref, first in sources:
            value = ref[pl.ds(pl.multiple_of(first + i * step, 16), step), :].astype(F32)
            total = value if total is None else total + value
        target[pl.ds(pl.multiple_of(at + i * step, 16), step), :] = total.astype(target.dtype)
        return carry

    lax.fori_loop(0, rows // step, body, 0)


def sum_kernel(
    g_ref, small_ref, f_ref, small_out, pair, sums, got_one, got_two, got_three, sum_two, sum_three,
    small_pair, small_x, small_y, small_z, send_sem, recv_sem,
):
    me = Place()
    peers = [me.other_core()]
    peers += [me.along(axis, step) for axis in ("x", "y", "z") for step in (1, 2, 3)]
    greet(peers)
    send = Sender(send_sem, recv_sem)
    mine, theirs = me.core, 1 - me.core

    pairs = [
        send(g_ref.at[pl.ds((4 * p + 2 * theirs) * 512, 1024)], pair.at[p], me.other_core())
        for p in range(3)
    ]
    small_pair[pl.ds(me.core, 1)] = small_ref[...][None]
    own = small_pair.at[me.core]
    small_copy = send(own, own, me.other_core())

    def exchange(stage, p, source):
        axis = ORDERS[p][stage]
        rows = STAGE_ROWS[stage]
        got = (got_one, got_two, got_three)[stage]
        copies = []
        for step in (1, 2, 3):
            chunk = lax.rem(me.at[axis] + step, SIDE_CHIPS)
            copies.append(
                send(source.at[pl.ds(chunk * rows, rows)], got.at[p, step - 1], me.along(axis, step))
            )
        return copies

    small_bufs = {"x": small_x, "y": small_y, "z": small_z}

    def small_exchange(axis, value):
        buf = small_bufs[axis]
        buf[pl.ds(me.at[axis], 1)] = value[None]
        part = buf.at[me.at[axis]]
        return [send(part, part, me.along(axis, step)) for step in (1, 2, 3)]

    def small_sum(axis, copies):
        for copy in copies:
            copy.wait_recv()
        buf = small_bufs[axis]
        return (buf[0] + buf[1]) + (buf[2] + buf[3])

    stage = []
    for p in range(3):
        pairs[p].wait_recv()
        size = (256, 32, 128)[p]
        own_rows = (4 * p + 2 * mine) * 512

        def body(i, carry, p=p, size=size, own_rows=own_rows):
            per = 256 // size
            block, rest = i // (2 * per), lax.rem(i, 2 * per)
            hi, sub = rest // per, lax.rem(rest, per)
            if p == 0:
                target = (hi * 2 + block) * 256
            else:
                target = (block * per + sub) * (2 * size) + hi * size
            from_row = (block * 2 + hi) * 256 + sub * size
            value = g_ref[pl.ds(pl.multiple_of(own_rows + from_row, 16), size), :].astype(F32)
            value += pair[p, pl.ds(pl.multiple_of(from_row, 16), size), :].astype(F32)
            sums[p, pl.ds(pl.multiple_of(target, 16), size), :] = value.astype(BF16)
            return carry

        lax.fori_loop(0, 1024 // size, body, 0)
        stage.append(exchange(0, p, sums.at[p]))
    small_copy.wait_recv()
    small_copies = small_exchange("x", small_pair[0] + small_pair[1])

    held = (sums, sum_two, sum_three)
    got = (got_one, got_two, got_three)
    strides = [{}, {}, {}]
    for p in range(3):
        extent, size = {"x": 2, "y": 4, "z": 4}, 16
        for axis in reversed(ORDERS[p]):
            strides[p][axis] = size
            size *= extent[axis]
    near = {"x": me.lo, "y": me.at["y"], "z": me.at["z"]}

    def start_of(p, smallest):
        start = me.core * 512
        for axis, size in strides[p].items():
            if size >= smallest:
                start = start + near[axis] * size
        return start

    for number in range(3):
        rows = STAGE_ROWS[number]
        following = []
        for p in range(3):
            for copy in stage[p]:
                copy.wait_recv()
            sources = [(held[number].at[p], me.at[ORDERS[p][number]] * rows)]
            sources += [(got[number].at[p, slot], 0) for slot in range(3)]
            step = min(rows, 64)
            if number < 2:
                add_up(held[number + 1].at[p], 0, sources, rows, step)
                following.append(exchange(number + 1, p, held[number + 1].at[p]))
            else:
                add_up(f_ref.at[p], start_of(p, 16), sources, rows, step)
        stage = following
        small_total = small_sum("xyz"[number], small_copies)
        if number < 2:
            small_copies = small_exchange("xyz"[number + 1], small_total)
        else:
            small_out[...] = small_total

    def share(p, axis):
        size = strides[p][axis]
        part = f_ref.at[p, pl.ds(start_of(p, size), size)]
        if axis == "x":
            x = me.at["x"]
            return [send(part, part, me.id_of(x=x + 1 - 2 * lax.rem(x, 2)))]
        return [send(part, part, me.along(axis, step)) for step in (1, 2, 3)]

    stage = [share(p, ORDERS[p][2]) for p in range(3)]
    for number in (1, 0, -1):
        following = []
        for p in range(3):
            for copy in stage[p]:
                copy.wait_recv()
            if number >= 0:
                following.append(share(p, ORDERS[p][number]))
            else:
                part = f_ref.at[p, pl.ds(me.core * 512, 512)]
                following.append([send(part, part, me.other_core())])
        stage = following
    for copies in stage:
        copies[0].wait_recv()
    send.finish()


def sum_grads(grads, small):
    vmem = pl.BlockSpec(memory_space=pltpu.VMEM)
    rows = small.shape[0]
    return pl.pallas_call(
        sum_kernel,
        in_specs=[vmem, vmem],
        out_specs=[vmem, vmem],
        out_shape=[
            jax.ShapeDtypeStruct((3, 1024, BLOCK), BF16),
            jax.ShapeDtypeStruct(small.shape, F32),
        ],
        scratch_shapes=[
            pltpu.VMEM((3, 1024, BLOCK), BF16),
            pltpu.VMEM((3, 1024, BLOCK), BF16),
            pltpu.VMEM((3, 3, 256, BLOCK), BF16),
            pltpu.VMEM((3, 3, 64, BLOCK), BF16),
            pltpu.VMEM((3, 3, 16, BLOCK), BF16),
            pltpu.VMEM((3, 256, BLOCK), BF16),
            pltpu.VMEM((3, 64, BLOCK), BF16),
            pltpu.VMEM((2, rows, BLOCK), F32),
            pltpu.VMEM((4, rows, BLOCK), F32),
            pltpu.VMEM((4, rows, BLOCK), F32),
            pltpu.VMEM((4, rows, BLOCK), F32),
            pltpu.SemaphoreType.DMA((64,)),
            pltpu.SemaphoreType.DMA((64,)),
        ],
        compiler_params=pltpu.CompilerParams(
            collective_id=1, has_side_effects=True, vmem_limit_bytes=40 * 1024 * 1024
        ),
        name="sum_grads",
    )(grads.reshape(12 * 512, BLOCK), small)


def hidden_order(values):
    return values.reshape(-1, 2, 4, 256).transpose(0, 2, 1, 3).reshape(-1, 2048)


def hidden_back(values):
    return values.reshape(-1, 4, 2, 256).transpose(0, 2, 1, 3).reshape(-1, 2048)


def local(
    tokens, image_counts, shift_mask, rel_index, norm1_gain, norm1_bias, qkv_weight, q_bias, v_bias,
    rel_table, proj_weight, proj_bias, norm2_gain, norm2_bias, fc1_weight, fc1_bias, fc2_weight,
    fc2_bias, out_grad,
):
    width = tokens.shape[2]
    table_rows, heads_here = rel_table.shape
    heads = heads_here * 2
    vectors = jnp.concatenate(
        [norm1_gain, norm1_bias, q_bias, v_bias, proj_bias, norm2_gain, norm2_bias, fc2_bias]
        + [fc1_bias, rel_table.T.reshape(-1)]
    )
    used = vectors.shape[0]
    vectors = jnp.pad(vectors, (0, 16 * BLOCK - used)).reshape(16, BLOCK)
    weights, both = gather_weights(qkv_weight, proj_weight, fc1_weight, fc2_weight, vectors)
    weights = weights.reshape(2, 12, 256, BLOCK).transpose(1, 0, 2, 3).reshape(12, BLOCK, BLOCK)
    flat = both.reshape(2, -1)
    eight = flat[:, :2048].reshape(2, 8, 256).transpose(1, 0, 2).reshape(8, BLOCK)
    hidden_bias = hidden_order(flat[:, 2048:3072].reshape(1, 2048)).reshape(4, BLOCK)
    table = flat[:, 3072:used].reshape(heads, table_rows).T
    vecs = jnp.concatenate([eight, hidden_bias]).astype(F32)
    bias = score_bias(table, rel_index, shift_mask)
    block_out, tokens_grad, acts, small, pair = run_layer(
        tokens, out_grad, image_counts, bias, weights, vecs, heads
    )
    grads = run_grads(acts)
    table_grad = table_grad_of(pair, rel_index, table_rows).T.reshape(-1)
    small = jnp.concatenate([small.reshape(-1), table_grad])
    small_used = small.shape[0]
    small = jnp.pad(small, (0, 24 * BLOCK - small_used)).reshape(24, BLOCK)
    grads, small = sum_grads(grads, small)
    grads = grads.reshape(12, 256, BLOCK).astype(F32)
    hi = lax.axis_index("shard")
    flat = small.reshape(-1)

    def half(values):
        size = values.shape[0] // 2
        return lax.dynamic_slice(values, (hi * size,), (size,))

    n1g, n1b, qb, vb, pb, n2g, n2b, f2b = (half(small[row]) for row in range(8))
    f1b = half(hidden_back(flat[8 * BLOCK : 12 * BLOCK].reshape(1, 2048))[0])
    table_out = half(flat[12 * BLOCK : small_used]).reshape(heads_here, table_rows).T
    qkv_out = grads[:3].transpose(1, 0, 2).reshape(256, 3 * BLOCK)
    fc1_out = hidden_back(grads[4:8].transpose(1, 0, 2).reshape(256, 4 * BLOCK))
    fc2_out = grads[8:].reshape(1024, BLOCK)
    return (
        block_out, tokens_grad, n1g, n1b, qkv_out, qb, vb, table_out, grads[3], pb, n2g, n2b,
        fc1_out, f1b, fc2_out, f2b,
    )


def solution(mesh):
    split = P(("replica", "shard"), None, None)
    vector, matrix, table = P("shard"), P("shard", None), P(None, "shard")
    return jax.shard_map(
        local,
        mesh=mesh,
        in_specs=(
            split, P(("replica", "shard")), P(), P(), vector, vector, matrix, vector, vector, table,
            matrix, vector, vector, vector, matrix, vector, matrix, vector, split,
        ),
        out_specs=(
            split, split, vector, vector, matrix, vector, vector, table, matrix, vector, vector,
            vector, matrix, vector, matrix, vector,
        ),
        check_vma=False,
    )
```

time: 782 us -> 219 us (0.28); the launches traced: 770 us -> 218 us
  blocking collectives: 398 us -> 0 us
  Pallas kernels: 0 us -> 167 us
  matrix products: 132 us -> 2.17 us
  local copies, waits for them, and re-layouts: 154 us -> 44.1 us
  other arithmetic: 51.3 us -> 3.55 us
  waiting for transfers between devices: 16.5 us -> 0 us
  between operations: 17.5 us -> 1.57 us
    psum x1 -> x0, blocking collectives: 326 us -> none  [local(): lax.psum((all_share[0], all_share[1], all_share[2], all_share[3], all_sha...]
    pallas_call x0 -> x4, Pallas kernels: none -> 167 us  [the longest x1 69.5 us: run_layer(): pl.pallas_call(partial(layer_kernel, heads), grid=(images,), in_specs=[pl...]
    dot_general x20 -> x2, matrix products: 132 us -> 2.17 us  [the longest x1 1.58 us: score_bias(): lax.dot_general(table, pair_onehot(rel_index, rows), (((0,), (1,)), ((),...]
    all_gather x11 -> x0, blocking collectives: 64 us -> none  [the longest x1 15.3 us: local(): lax.all_gather(proj_weight, 'shard', axis=0, tiled=True)]
    concatenate x9 -> x1, local copies, waits for them, and re-layouts: 52.2 us -> 0.01 us  [local(): jnp.concatenate([norm1_gain, norm1_bias, q_bias, v_bias, proj_bias, norm2...]
    reshape x19 -> x13, local copies, waits for them, and re-layouts: 53.1 us -> 13.6 us  [the longest x1 3.34 us: local(): weights.reshape(2, 12, 256, BLOCK).transpose(1, 0, 2, 3)]
    reduce_sum x15 -> x0, other arithmetic: 34.8 us -> none  [the longest x3 9.46 us: row_sum(): return jnp.sum(values.reshape(-1, values.shape[-1]), 0)]
    reduce_scatter x5 -> x0, waiting for transfers between devices: 14.3 us -> none  [the longest x1 14.3 us: local(): lax.psum_scatter(grad_fc1.astype(jnp.bfloat16), 'shard', scatter_dimensio...]
  transfers between devices with their start and end apart: 8 -> 0, of which waited for: 1 -> 0; matrix products, arithmetic and copies ran while one was open for 31% -> 0% of each run, Pallas kernels for 0% -> 0%
where the time goes in v1:
time: 219 us; the launch traced here: 218 us
  Pallas kernels  167 us (76%)
  local copies, waits for them, and re-layouts  44.1 us (20%)
  other arithmetic  3.55 us (2%)
    pallas_call x1, Pallas kernels, run_layer(): pl.pallas_call(partial(layer_kernel, heads), grid=(images,), in_specs=[pl...  69.5 us
    pallas_call x1, Pallas kernels, sum_grads(): pl.pallas_call(sum_kernel, in_specs=[vmem, vmem], out_specs=[vmem, vmem],...  51.4 us
    pallas_call x1, Pallas kernels, gather_weights(): pl.pallas_call(gather_kernel, in_specs=[pl.BlockSpec(memory_space=pl.ANY)...  29.1 us
    pallas_call x1, Pallas kernels, run_grads(): pl.pallas_call(grads_kernel, grid=(12,), in_specs=[pl.BlockSpec((rows, BL...  16.7 us
    unnamed x30, local copies, waits for them, and re-layouts  12.4 us
    another operation x2, local copies, waits for them, and re-layouts, hidden_back(): return values.reshape(-1, 4, 2, 256).transpose(0, 2, 1, 3).reshape(-1, 2048)  7.77 us
    add x3, local copies, waits for them, and re-layouts, score_bias(): return (bias[None] + mask[:, :, None, :]).reshape(4, WPAD, heads * WPAD)  4.57 us

profile of v1, /device:TPU:1, one launch (start us, length us, event | category | flops | bytes accessed | tf_op | source)
XLA Modules:
  0.0 218.0 jit_solution(11758406698600624999)
XLA Ops:
  1.3 0.8 reshape.136
  2.1 0.9 dynamic-update-slice
  2.9 0.8 dynamic-update-slice.1
  3.8 0.8 dynamic-update-slice.2
  4.6 0.8 dynamic-update-slice.3
  5.4 0.8 dynamic-update-slice.4
  6.3 0.8 dynamic-update-slice.5
  7.1 0.8 dynamic-update-slice.6
  7.9 0.8 dynamic-update-slice.7
  8.8 0.7 constant_dynamic-update-slice_fusion.1
  9.5 0.8 copy.61
  10.4 0.1 eq.56
  10.4 0.9 select_bitcast_fusion
  11.4 0.1 copy.63
  11.5 0.0 copy-start
  11.5 0.0 copy-start.1
  11.5 0.0 copy-start.2
  11.5 0.0 copy-start.3
  11.6 1.5 add.49
  13.0 2.9 %add.50 = f32[4,64,1024]{2,1,0:T(8,128)} reshape(f32[4,64,16,64]{3,2,1,0:T(8,128)} %add.49) | data formatting | bytes 2097152 | tf_op jit(solution)/shard_map/add | solution.py:338
  15.9 0.0 copy-done
  15.9 0.0 copy-done.1
  16.0 0.0 copy-done.2
  16.0 0.0 copy-done.3
  16.0 29.1 %gather_weights.1 = (bf16[2,3072,512]{2,1,0:T(8,128)(2,1)S(1)}, bf16[2,16,512]{2,1,0:T(8,128)(2,1)S(1)}) custom-call(bf16[256,1536]{1,0:T(8,128)(2,1)S(1)} %copy-done.2, bf16[256,512]{1,0:T(8,128)(2,1)S(1)} %copy-done.3, bf16[256,2048]{1,0:T(8,128)(2,1)S(1)} %copy-done, bf16[1024,512]{1,0:T(8,128)(2,1)S(1)} %copy-done.1, bf16[16,512]{1,0:T(8,128)(2,1)S(1)} %reshape.137.vec_ref), custom_call_target="tpu_custom_call" | custom-call | tf_op jit(solution)/shard_map/gather_weights/pallas_call | solution.py:485
  45.1 3.3 %copy.53 = bf16[2,12,256,512]{3,2,0,1:T(8,128)(2,1)} copy(bf16[2,12,256,512]{3,2,1,0:T(8,128)(2,1)S(1)} %bitcast.73) | data formatting | bytes 12582912 | tf_op jit(solution)/shard_map/reshape | solution.py:710
  48.4 0.0 copy-start.5
  48.5 0.1 reshape.156
  48.6 0.6 maximum_convert_fusion.vec_ref
  49.2 1.6 fusion.6
  50.8 0.2 add.47
  51.0 0.0 copy-done.5
  51.0 1.1 broadcast_add_fusion.bias_ref
  52.0 69.5 %layer.1 = (bf16[6,196,512]{2,1,0:T(8,128)(2,1)}, f32[6,196,512]{2,1,0:T(8,128)}, bf16[6,224,8192]{2,1,0:T(8,128)(2,1)}, f32[12,512]{1,0:T(8,128)}, f32[64,1024]{1,0:T(8,128)}) custom-call(s32[1]{0:T(128)S(6)} %copy.85.count_ref, bf16[6,196,512]{2,1,0:T(8,128)(2,1)} %tok_ref.1, bf16[6,196,512]{2,1,0:T(8,128)(2,1)} %up_ref.1, ...), custom_call_target="tpu_custom_call" | custom-call | tf_op jit(solution)/shard_map/layer/pallas_call | solution.py:262
  121.5 0.8 reshape.146
  122.3 1.1 reshape.147
  123.3 0.2 copy.73
  123.5 0.2 reshape.148
  123.7 0.6 fusion.3
  124.3 0.1 reshape.149
  124.5 16.7 %weight_grads.1 = bf16[12,512,512]{2,1,0:T(8,128)(2,1)S(1)} custom-call(bf16[1344,8192]{1,0:T(8,128)(2,1)} %bitcast.76, bf16[1344,8192]{1,0:T(8,128)(2,1)} %bitcast.77), custom_call_target="tpu_custom_call" | custom-call | tf_op jit(solution)/shard_map/weight_grads/pallas_call | solution.py:311
  141.2 51.4 %sum_grads.1 = (bf16[3,1024,512]{2,1,0:T(8,128)(2,1)S(1)}, f32[24,512]{1,0:T(8,128)S(1)}) custom-call(bf16[6144,512]{1,0:T(8,128)(2,1)S(1)} %bitcast.72, f32[24,512]{1,0:T(8,128)S(1)} %reshape.150.small_ref), custom_call_target="tpu_custom_call" | custom-call | tf_op jit(solution)/shard_map/sum_grads/pallas_call | solution.py:657
  192.7 0.6 dynamic_slice.61
  193.3 0.6 constant_dynamic-slice_fusion
  193.9 0.6 constant_dynamic-slice_fusion.2
  194.4 0.6 constant_dynamic-slice_fusion.4
  195.0 0.6 constant_dynamic-slice_fusion.6
  195.6 0.1 dynamic_slice.54
  195.7 0.7 reshape.153
  196.4 1.6 slice.90
  198.0 3.5 %reshape_reshape.14 = f32[256,4,2,256]{3,2,0,1:T(2,128)} reshape(f32[256,4,512]{2,0,1:T(8,128)} %bitcast.82) | data formatting | bytes 4194304 | tf_op jit(solution)/shard_map/reshape;reshape | solution.py:692
  201.5 4.3 %copy.72 = f32[256,4,2,256]{3,1,2,0:T(4,128)} copy(f32[256,4,2,256]{3,2,0,1:T(2,128)} %reshape_reshape.14) | data formatting | bytes 4194304 | tf_op jit(solution)/shard_map/reshape;reshape | solution.py:692
  205.8 3.3 %reshape.154 = f32[256,2048]{1,0:T(8,128)} reshape(f32[256,2,4,256]{3,2,1,0:T(4,128)} %bitcast.81) | data formatting | bytes 4194304 | tf_op jit(solution)/shard_map/reshape | solution.py:692
  209.0 0.9 convert_element_type.30
  209.9 0.0 copy-start.4
  209.9 0.9 slice_bitcast_fusion.1
  210.8 1.9 copy-done.4
  212.7 0.1 slice.87
  212.9 0.5 copy.60
  213.3 1.6 copy.59
  214.9 3.1 %slice_bitcast_fusion = f32[1024,512]{1,0:T(8,128)} fusion(f32[3,1024,512]{2,1,0:T(8,128)} %copy-done.4), kind=kLoop, calls=%fused_computation.5 | loop fusion | bytes 4194304 | tf_op jit(solution)/shard_map/reshape | solution.py:739
  (21 shorter events, 0.2 us)
Async XLA Ops:
  11.5 4.4 %copy-start = (bf16[256,2048]{1,0:T(8,128)(2,1)S(1)}, bf16[256,2048]{1,0:T(8,128)(2,1)}, u32[]{:S(2)}) copy-start(bf16[256,2048]{1,0:T(8,128)(2,1)} %fc1_ref.1) | copy-start | bytes 3145732
  11.5 4.4 %copy-start.1 = (bf16[1024,512]{1,0:T(8,128)(2,1)S(1)}, bf16[1024,512]{1,0:T(8,128)(2,1)}, u32[]{:S(2)}) copy-start(bf16[1024,512]{1,0:T(8,128)(2,1)} %fc2_ref.1) | copy-start | bytes 3145732
  11.5 4.4 %copy-start.2 = (bf16[256,1536]{1,0:T(8,128)(2,1)S(1)}, bf16[256,1536]{1,0:T(8,128)(2,1)}, u32[]{:S(2)}) copy-start(bf16[256,1536]{1,0:T(8,128)(2,1)} %qkv_ref.1) | copy-start | bytes 2359300
  11.5 4.4 %copy-start.3 = (bf16[256,512]{1,0:T(8,128)(2,1)S(1)}, bf16[256,512]{1,0:T(8,128)(2,1)}, u32[]{:S(2)}) copy-start(bf16[256,512]{1,0:T(8,128)(2,1)} %proj_ref.1) | copy-start | bytes 786436
  48.4 2.6 %copy-start.5 = (f32[4,64,1024]{2,1,0:T(8,128)S(1)}, f32[4,64,1024]{2,1,0:T(8,128)}, u32[]{:S(2)}) copy-start(f32[4,64,1024]{2,1,0:T(8,128)} %add.50) | copy-start | bytes 3145732
  209.9 2.8 %copy-start.4 = (f32[3,1024,512]{2,1,0:T(8,128)}, f32[3,1024,512]{2,1,0:T(8,128)S(1)}, u32[]{:S(2)}) copy-start(f32[3,1024,512]{2,1,0:T(8,128)S(1)} %convert_element_type.30) | copy-start | bytes 18874372

commit v2 on v1

--- a/solution.py
+++ b/solution.py
@@ -88,13 +88,17 @@
     back_ref,
     hmask_ref,
     bias_ref,
-    w_ref,
+    rel_ref,
     vec_ref,
+    w_any,
     out_ref,
     tg_ref,
     acts_ref,
     small_ref,
+    w_ref,
+    w_sem,
     pair_ref,
+    fold_s,
     qkv_s,
     prob_s,
     att_s,
@@ -109,13 +113,28 @@
     per = 4
     groups = heads // per
 
+    def weight_copies(blocks):
+        return [
+            pltpu.make_async_copy(
+                w_any.at[half, pl.ds(n * 256, 256)],
+                w_ref.at[n, pl.ds(half * 256, 256)],
+                w_sem.at[n, half],
+            )
+            for n in blocks
+            for half in range(2)
+        ]
+
     @pl.when(image == 0)
     def _():
+        for copy in weight_copies(range(12)):
+            copy.start()
         small_ref[...] = jnp.zeros_like(small_ref)
         pair_ref[...] = jnp.zeros_like(pair_ref)
-
-    def vec(row, count=1):
-        return vec_ref[row : row + count, :].reshape(1, count * BLOCK)
+        for copy in weight_copies(range(3)):
+            copy.wait()
+
+    def vec(row):
+        return jnp.concatenate([vec_ref[0, row : row + 1, :], vec_ref[1, row : row + 1, :]], 1)
 
     def note(row, values):
         small_ref[row : row + 1, :] += col_sum(values)
@@ -150,6 +169,11 @@
             qkv_s[w, :, n * BLOCK : (n + 1) * BLOCK] = pad_window(
                 part[w * ROWS : (w + 1) * ROWS]
             ).astype(BF16)
+
+    @pl.when(image == 0)
+    def _():
+        for copy in weight_copies(range(3, 12)):
+            copy.wait()
 
     for w in range(4):
         for g in range(groups):
@@ -240,14 +264,37 @@
     rest = (total - high.astype(F32)).astype(BF16)
     tg_ref[0] = nn(back_ref[...], high) + nn(back_ref[...], rest)
 
-
-def run_layer(tokens, out_grad, count, bias, weights, vectors, heads):
+    @pl.when(image == pl.num_programs(0) - 1)
+    def _():
+        half = WPAD // 2
+        for h in range(heads):
+            at = slice(h * WPAD, (h + 1) * WPAD)
+            both = jnp.concatenate([pair_ref[:half, at], pair_ref[half:, at]], 1)
+            fold_s[pl.ds(h, half, stride=heads), :] = both
+
+        def body(j, total):
+            values = fold_s[pl.ds(pl.multiple_of(j * heads, heads), heads), :]
+            high = values.astype(BF16)
+            rest = (values - high.astype(F32)).astype(BF16)
+            return total + nt(jnp.concatenate([high, rest], 0), pair_rows(rel_ref, j))
+
+        total = lax.fori_loop(0, half, body, jnp.zeros((2 * heads, 256), F32))
+        table = total[:heads] + total[heads:]
+        small_ref[12 : 12 + heads // 2, :256] = table[: heads // 2]
+        small_ref[12 : 12 + heads // 2, 256:] = table[heads // 2 :]
+
+
+def pair_rows(rel_ref, j):
+    rows = lax.broadcasted_iota(jnp.int32, (256, 128), 0).astype(F32)
+    return jnp.where(rows == rel_ref[pl.ds(j, 1), :], 1.0, 0.0).astype(BF16)
+
+
+def run_layer(tokens, out_grad, count, bias, rel_rows, weights, vectors, heads):
     images, tokens_image, width = tokens.shape
     place = window_places()
     hmask = np.zeros((4 * WPAD, 128), np.float32)
     for h in range(4):
         hmask[h * WPAD : (h + 1) * WPAD, h * 32 : (h + 1) * 32] = 1
-    hidden = weights.shape[0]
 
     def whole(array):
         zeros = (0,) * array.ndim
@@ -257,7 +304,7 @@
         return pl.BlockSpec((1,) + shape, lambda b: (b,) + (0,) * len(shape))
 
     consts = [jnp.asarray(place, BF16), jnp.asarray(place.T, BF16), jnp.asarray(hmask, BF16)]
-    shared = consts + [bias, weights, vectors]
+    shared = consts + [bias, rel_rows, vectors]
     rows = 4 * ROWS
     return pl.pallas_call(
         partial(layer_kernel, heads),
@@ -267,22 +314,25 @@
             per_image(tokens_image, width),
             per_image(tokens_image, width),
         ]
-        + [whole(item) for item in shared],
+        + [whole(item) for item in shared]
+        + [pl.BlockSpec(memory_space=pl.ANY)],
         out_specs=[
             per_image(tokens_image, width),
             per_image(tokens_image, width),
             per_image(rows, 16 * BLOCK),
-            pl.BlockSpec((12, BLOCK), lambda b: (0, 0)),
-            pl.BlockSpec((WPAD, heads * WPAD), lambda b: (0, 0)),
+            pl.BlockSpec((24, BLOCK), lambda b: (0, 0)),
         ],
         out_shape=[
             jax.ShapeDtypeStruct(tokens.shape, BF16),
             jax.ShapeDtypeStruct(tokens.shape, F32),
             jax.ShapeDtypeStruct((images, rows, 16 * BLOCK), BF16),
-            jax.ShapeDtypeStruct((12, BLOCK), F32),
-            jax.ShapeDtypeStruct((WPAD, heads * WPAD), F32),
+            jax.ShapeDtypeStruct((24, BLOCK), F32),
         ],
         scratch_shapes=[
+            pltpu.VMEM((12, BLOCK, BLOCK), BF16),
+            pltpu.SemaphoreType.DMA((12, 2)),
+            pltpu.VMEM((WPAD, heads * WPAD), F32),
+            pltpu.VMEM((heads * WPAD // 2, 128), F32),
             pltpu.VMEM((4, WPAD, 3 * BLOCK), BF16),
             pltpu.VMEM((4, WPAD, heads * WPAD), F32),
             pltpu.VMEM((rows, BLOCK), F32),
@@ -291,7 +341,7 @@
         ],
         compiler_params=pltpu.CompilerParams(vmem_limit_bytes=56 * 1024 * 1024),
         name="layer",
-    )(count, tokens, out_grad, *shared)
+    )(count, tokens, out_grad, *shared, weights)
 
 
 def grads_kernel(left_ref, right_ref, out_ref):
@@ -317,39 +367,6 @@
         compiler_params=pltpu.CompilerParams(vmem_limit_bytes=40 * 1024 * 1024),
         name="weight_grads",
     )(acts, acts)
-
-
-def pair_onehot(rel_index, rows):
-    index = jnp.pad(
-        rel_index.T, ((0, WPAD - WTOK), (0, WPAD - WTOK)), constant_values=-1
-    ).reshape(-1)
-    return (index[:, None] == jnp.arange(rows, dtype=jnp.int32)[None, :]).astype(BF16)
-
-
-def score_bias(table, rel_index, shift_mask):
-    rows, heads = table.shape
-    bias = lax.dot_general(
-        table, pair_onehot(rel_index, rows), (((0,), (1,)), ((), ())), preferred_element_type=F32
-    )
-    bias = bias.reshape(heads, WPAD, WPAD).transpose(1, 0, 2)
-    mask = jnp.where(shift_mask == 1, 0.0, -100.0).astype(F32).transpose(0, 2, 1)
-    mask = jnp.pad(mask, ((0, 0), (0, 0), (0, WPAD - WTOK)))
-    mask = jnp.pad(mask, ((0, 0), (0, WPAD - WTOK), (0, 0)), constant_values=MASKED)
-    return (bias[None] + mask[:, :, None, :]).reshape(4, WPAD, heads * WPAD)
-
-
-def table_grad_of(pair, rel_index, rows):
-    heads = pair.shape[1] // WPAD
-    pair = pair.reshape(WPAD, heads, WPAD).transpose(1, 0, 2).reshape(heads, -1)
-    high = pair.astype(BF16)
-    rest = (pair - high.astype(F32)).astype(BF16)
-    both = lax.dot_general(
-        pair_onehot(rel_index, rows),
-        jnp.concatenate([high, rest], 0),
-        (((0,), (1,)), ((), ())),
-        preferred_element_type=F32,
-    )
-    return both[:, :heads] + both[:, heads:]
 
 
 MESH = pl.DeviceIdType.MESH
@@ -411,7 +428,13 @@
             copy.wait_send()
 
 
-def gather_kernel(qkv_ref, proj_ref, fc1_ref, fc2_ref, vec_ref, w_ref, v_ref, local_sem, send_sem, recv_sem):
+def gather_kernel(
+    qkv_ref, proj_ref, fc1_ref, fc2_ref, *refs
+):
+    vec_refs = refs[:8]
+    hidden_ref, table_ref, index_ref, mask_ref = refs[8:12]
+    w_ref, v_ref, bias_ref, rel_ref = refs[12:16]
+    square, square_mask, pairs, local_sem, send_sem, recv_sem = refs[16:]
     me = Place()
     hi, other = me.hi, 1 - me.hi
     local = []
@@ -434,13 +457,21 @@
                 w_ref.at[hi, rows_of(4 + m), pl.ds(half * 256, 256)],
             )
     load(fc2_ref, w_ref.at[hi, pl.ds(8 * 256, 1024)])
-    load(vec_ref, v_ref.at[hi])
 
     facing = me.id_of(x=3 - me.at["x"])
     peers = [facing, me.other_core()]
     peers += [me.along(axis, step) for axis in ("y", "z") for step in (1, 2, 3)]
     greet(peers)
     send = Sender(send_sem, recv_sem)
+
+    rows = [ref[...].astype(F32).reshape(1, 256) for ref in vec_refs]
+    rows += [hidden_ref[pl.ds(m * 256, 256)].astype(F32).reshape(1, 256) for m in range(4)]
+    rows.append(jnp.zeros((4, 256), F32))
+    v_ref[pl.ds(hi, 1), 0:16] = jnp.concatenate(rows, 0)[None]
+    table_rows, heads_here = table_ref.shape
+    square[...] = jnp.zeros_like(square)
+    square[0:table_rows, 0:heads_here] = table_ref[...].astype(F32)
+    v_ref[pl.ds(hi, 1), 16:24] = jnp.concatenate([square[0:128].T, square[128:256].T], 1)[None, 0:8]
     for copy in local:
         copy.wait()
 
@@ -459,10 +490,36 @@
         part = w_ref.at[other, pl.ds(start, size)]
         return [send(part, part, me.along(axis, step)) for step in (1, 2, 3)]
 
+    square[0:128] = jnp.full((128, 128), -1.0, F32)
+    square[0:WTOK, 0:WTOK] = index_ref[...].astype(F32)
+    turned = square[0:128].T
+    half = WPAD // 2
+    rel_ref[...] = jnp.concatenate([turned[:half, :WPAD], turned[half:WPAD, :WPAD]], 1)
+    for w in range(4):
+        below = lax.broadcasted_iota(jnp.int32, (WPAD, WPAD), 0)
+        square_mask[w] = jnp.where(below < WTOK, 0.0, MASKED)
+        square_mask[w, 0:WTOK, 0:WTOK] = jnp.where(mask_ref[w] == 1, 0.0, -100.0)
+
     firsts = []
     for copy, (base, outer, piece, first, second) in zip(crossing, flows):
         copy.wait_recv()
         firsts.append(share(piece, 48, first))
+    vectors.wait_recv()
+    table = jnp.concatenate([v_ref[0, 16:24], v_ref[1, 16:24]], 0).astype(BF16)
+    heads = table.shape[0]
+
+    def body(j, carry):
+        pairs[pl.ds(pl.multiple_of(j * heads, heads), heads), :] = nn(table, pair_rows(rel_ref, j))
+        return carry
+
+    lax.fori_loop(0, half, body, 0)
+    for h in range(heads):
+        at = slice(h * WPAD, (h + 1) * WPAD)
+        both = pairs[pl.ds(h, half, stride=heads), :]
+        for w in range(4):
+            bias_ref[w, :half, at] = both[:, :WPAD] + square_mask[w, :half]
+            bias_ref[w, half:, at] = both[:, WPAD:] + square_mask[w, half:]
+
     seconds = []
     for copies, (base, outer, piece, first, second) in zip(firsts, flows):
         for copy in copies:
@@ -476,21 +533,27 @@
         lasts.append(send(part, part, me.other_core()))
     for copy in lasts:
         copy.wait_recv()
-    vectors.wait_recv()
     send.finish()
 
 
-def gather_weights(qkv, proj, fc1, fc2, vectors):
+def gather_weights(matrices, vectors, hidden_bias, table, rel_index, shift_mask):
     vmem = pl.BlockSpec(memory_space=pltpu.VMEM)
+    heads = table.shape[1] * 2
+    small = vectors + [hidden_bias, table, rel_index, shift_mask]
     return pl.pallas_call(
         gather_kernel,
-        in_specs=[pl.BlockSpec(memory_space=pl.ANY)] * 5,
-        out_specs=[vmem, vmem],
+        in_specs=[pl.BlockSpec(memory_space=pl.ANY)] * 4 + [vmem] * len(small),
+        out_specs=[vmem] * 4,
         out_shape=[
             jax.ShapeDtypeStruct((2, 12 * 256, BLOCK), BF16),
-            jax.ShapeDtypeStruct((2,) + vectors.shape, BF16),
+            jax.ShapeDtypeStruct((2, 24, 256), F32),
+            jax.ShapeDtypeStruct((4, WPAD, heads * WPAD), F32),
+            jax.ShapeDtypeStruct((WPAD // 2, 2 * WPAD), F32),
         ],
         scratch_shapes=[
+            pltpu.VMEM((256, 128), F32),
+            pltpu.VMEM((4, WPAD, WPAD), F32),
+            pltpu.VMEM((heads * WPAD // 2, 2 * WPAD), F32),
             pltpu.SemaphoreType.DMA((14,)),
             pltpu.SemaphoreType.DMA((17,)),
             pltpu.SemaphoreType.DMA((17,)),
@@ -499,7 +562,7 @@
             collective_id=0, has_side_effects=True, vmem_limit_bytes=30 * 1024 * 1024
         ),
         name="gather_weights",
-    )(qkv, proj, fc1, fc2, vectors)
+    )(*matrices, *small)
 
 
 ORDERS = (("x", "y", "z"), ("y", "z", "x"), ("z", "x", "y"))
@@ -624,7 +687,7 @@
         if number < 2:
             small_copies = small_exchange("xyz"[number + 1], small_total)
         else:
-            small_out[...] = small_total
+            small_out[...] = jnp.where(me.hi == 0, small_total[:, :256], small_total[:, 256:])
 
     def share(p, axis):
         size = strides[p][axis]
@@ -660,7 +723,7 @@
         out_specs=[vmem, vmem],
         out_shape=[
             jax.ShapeDtypeStruct((3, 1024, BLOCK), BF16),
-            jax.ShapeDtypeStruct(small.shape, F32),
+            jax.ShapeDtypeStruct((rows, 256), F32),
         ],
         scratch_shapes=[
             pltpu.VMEM((3, 1024, BLOCK), BF16),
@@ -684,12 +747,65 @@
     )(grads.reshape(12 * 512, BLOCK), small)
 
 
-def hidden_order(values):
-    return values.reshape(-1, 2, 4, 256).transpose(0, 2, 1, 3).reshape(-1, 2048)
-
-
-def hidden_back(values):
-    return values.reshape(-1, 4, 2, 256).transpose(0, 2, 1, 3).reshape(-1, 2048)
+def finish_kernel(
+    f_ref, small_ref, n1g, n1b, qkv, qb, vb, table, proj, pb, n2g, n2b, fc1, f1b, fc2, f2b, wide, turn, sem
+):
+    copies = []
+
+    def store(source, target):
+        copy = pltpu.make_async_copy(source, target, sem.at[len(copies)])
+        copy.start()
+        copies.append(copy)
+
+    for n in range(12):
+        wide[n] = f_ref[n].astype(F32)
+        if n < 3:
+            store(wide.at[n], qkv.at[:, pl.ds(n * BLOCK, BLOCK)])
+        elif n == 3:
+            store(wide.at[n], proj)
+        elif n < 8:
+            for half in range(2):
+                store(
+                    wide.at[n, :, pl.ds(half * 256, 256)],
+                    fc1.at[:, pl.ds(half * 1024 + (n - 4) * 256, 256)],
+                )
+        else:
+            store(wide.at[n], fc2.at[pl.ds((n - 8) * 256, 256)])
+    for row, ref in enumerate((n1g, n1b, qb, vb, pb, n2g, n2b, f2b)):
+        ref[...] = small_ref[row : row + 1, :].reshape(256)
+    for m in range(4):
+        f1b[pl.ds(m * 256, 256)] = small_ref[8 + m : 9 + m, :].reshape(256)
+    turn[...] = jnp.zeros_like(turn)
+    turn[0:8, :] = small_ref[12:20, :]
+    table[...] = jnp.concatenate([turn[:, 0:128].T, turn[:, 128:256].T], 0)[
+        : table.shape[0], : table.shape[1]
+    ]
+    for copy in copies:
+        copy.wait()
+
+
+def finish(grads, small, table_rows, heads_here):
+    vmem = pl.BlockSpec(memory_space=pltpu.VMEM)
+    far = pl.BlockSpec(memory_space=pl.ANY)
+    vector, hidden = ((256,), vmem), ((1024,), vmem)
+    outs = [
+        vector, vector, ((256, 3 * BLOCK), far), vector, vector, ((table_rows, heads_here), vmem),
+        ((256, BLOCK), far), vector, vector, vector, ((256, 4 * BLOCK), far), hidden,
+        ((1024, BLOCK), far), vector,
+    ]
+    return pl.pallas_call(
+        finish_kernel,
+        in_specs=[vmem, vmem],
+        out_specs=[spec for _, spec in outs],
+        out_shape=[jax.ShapeDtypeStruct(shape, F32) for shape, _ in outs],
+        scratch_shapes=[
+            pltpu.VMEM((12, 256, BLOCK), F32),
+            pltpu.VMEM((128, 256), F32),
+            pltpu.SemaphoreType.DMA((16,)),
+        ],
+        compiler_params=pltpu.CompilerParams(vmem_limit_bytes=30 * 1024 * 1024),
+        name="finish",
+    )(grads, small)
 
 
 def local(
@@ -697,50 +813,18 @@
     rel_table, proj_weight, proj_bias, norm2_gain, norm2_bias, fc1_weight, fc1_bias, fc2_weight,
     fc2_bias, out_grad,
 ):
-    width = tokens.shape[2]
     table_rows, heads_here = rel_table.shape
-    heads = heads_here * 2
-    vectors = jnp.concatenate(
-        [norm1_gain, norm1_bias, q_bias, v_bias, proj_bias, norm2_gain, norm2_bias, fc2_bias]
-        + [fc1_bias, rel_table.T.reshape(-1)]
+    weights, vecs, bias, rel_rows = gather_weights(
+        [qkv_weight, proj_weight, fc1_weight, fc2_weight],
+        [norm1_gain, norm1_bias, q_bias, v_bias, proj_bias, norm2_gain, norm2_bias, fc2_bias],
+        fc1_bias, rel_table, rel_index, shift_mask,
     )
-    used = vectors.shape[0]
-    vectors = jnp.pad(vectors, (0, 16 * BLOCK - used)).reshape(16, BLOCK)
-    weights, both = gather_weights(qkv_weight, proj_weight, fc1_weight, fc2_weight, vectors)
-    weights = weights.reshape(2, 12, 256, BLOCK).transpose(1, 0, 2, 3).reshape(12, BLOCK, BLOCK)
-    flat = both.reshape(2, -1)
-    eight = flat[:, :2048].reshape(2, 8, 256).transpose(1, 0, 2).reshape(8, BLOCK)
-    hidden_bias = hidden_order(flat[:, 2048:3072].reshape(1, 2048)).reshape(4, BLOCK)
-    table = flat[:, 3072:used].reshape(heads, table_rows).T
-    vecs = jnp.concatenate([eight, hidden_bias]).astype(F32)
-    bias = score_bias(table, rel_index, shift_mask)
-    block_out, tokens_grad, acts, small, pair = run_layer(
-        tokens, out_grad, image_counts, bias, weights, vecs, heads
+    block_out, tokens_grad, acts, small = run_layer(
+        tokens, out_grad, image_counts, bias, rel_rows, weights, vecs, heads_here * 2
     )
-    grads = run_grads(acts)
-    table_grad = table_grad_of(pair, rel_index, table_rows).T.reshape(-1)
-    small = jnp.concatenate([small.reshape(-1), table_grad])
-    small_used = small.shape[0]
-    small = jnp.pad(small, (0, 24 * BLOCK - small_used)).reshape(24, BLOCK)
-    grads, small = sum_grads(grads, small)
-    grads = grads.reshape(12, 256, BLOCK).astype(F32)
-    hi = lax.axis_index("shard")
-    flat = small.reshape(-1)
-
-    def half(values):
-        size = values.shape[0] // 2
-        return lax.dynamic_slice(values, (hi * size,), (size,))
-
-    n1g, n1b, qb, vb, pb, n2g, n2b, f2b = (half(small[row]) for row in range(8))
-    f1b = half(hidden_back(flat[8 * BLOCK : 12 * BLOCK].reshape(1, 2048))[0])
-    table_out = half(flat[12 * BLOCK : small_used]).reshape(heads_here, table_rows).T
-    qkv_out = grads[:3].transpose(1, 0, 2).reshape(256, 3 * BLOCK)
-    fc1_out = hidden_back(grads[4:8].transpose(1, 0, 2).reshape(256, 4 * BLOCK))
-    fc2_out = grads[8:].reshape(1024, BLOCK)
-    return (
-        block_out, tokens_grad, n1g, n1b, qkv_out, qb, vb, table_out, grads[3], pb, n2g, n2b,
-        fc1_out, f1b, fc2_out, f2b,
-    )
+    grads, small = sum_grads(run_grads(acts), small)
+    outs = finish(grads.reshape(12, 256, BLOCK), small, table_rows, heads_here)
+    return (block_out, tokens_grad, *outs)
 
 
 def solution(mesh):

time: 219 us -> 201 us (0.918)
  local copies, waits for them, and re-layouts: 44.1 us -> 18.4 us
  Pallas kernels: 167 us -> 180 us
  other arithmetic: 3.55 us -> 0 us
    reshape x13 -> x0, local copies, waits for them, and re-layouts: 13.6 us -> none  [the longest x1 3.34 us: local(): weights.reshape(2, 12, 256, BLOCK).transpose(1, 0, 2, 3)]
    another operation x2 -> x0, local copies, waits for them, and re-layouts: 7.77 us -> none  [hidden_back(): return values.reshape(-1, 4, 2, 256).transpose(0, 2, 1, 3).reshape(-1, 2048)]
    pallas_call x1, Pallas kernels: 69.5 us -> 75.8 us  [run_layer(): pl.pallas_call(partial(layer_kernel, heads), grid=(images,), in_specs=[pl...]
    unnamed x30 -> x41, local copies, waits for them, and re-layouts: 12.4 us -> 18.4 us
    add x3 -> x0, local copies, waits for them, and re-layouts: 4.57 us -> none  [score_bias(): return (bias[None] + mask[:, :, None, :]).reshape(4, WPAD, heads * WPAD)]
    pallas_call x1, Pallas kernels: 29.1 us -> 33.2 us  [gather_weights(): pl.pallas_call(gather_kernel, in_specs=[pl.BlockSpec(memory_space=pl.ANY)...]
    pallas_call x0 -> x1, Pallas kernels: none -> 3.43 us  [finish(): pl.pallas_call(finish_kernel, in_specs=[vmem, vmem], out_specs=[spec for...]
    dynamic_slice x6 -> x0, local copies, waits for them, and re-layouts: 2.96 us -> none  [half(): return lax.dynamic_slice(values, (hi * size,), (size,))]
where the time goes in v2:
time: 201 us; the launch traced here: 200 us
  Pallas kernels  180 us (90%)
  local copies, waits for them, and re-layouts  18.4 us (9%)
    pallas_call x1, Pallas kernels, run_layer(): pl.pallas_call(partial(layer_kernel, heads), grid=(images,), in_specs=[pl...  75.8 us
    pallas_call x1, Pallas kernels, sum_grads(): pl.pallas_call(sum_kernel, in_specs=[vmem, vmem], out_specs=[vmem, vmem],...  50.8 us
    pallas_call x1, Pallas kernels, gather_weights(): pl.pallas_call(gather_kernel, in_specs=[pl.BlockSpec(memory_space=pl.ANY)...  33.2 us
    unnamed x41, local copies, waits for them, and re-layouts  18.4 us
    pallas_call x1, Pallas kernels, run_grads(): pl.pallas_call(grads_kernel, grid=(12,), in_specs=[pl.BlockSpec((rows, BL...  16.7 us

profile of v2, /device:TPU:1, one launch (start us, length us, event | category | flops | bytes accessed | tf_op | source)
XLA Modules:
  0.0 199.8 jit_solution(11587426459168442542)
XLA Ops:
  1.3 0.8 copy.38.refs_9_
  2.1 0.9 copy.39.refs_11_
  3.0 0.0 copy-start.2
  3.0 1.2 copy-done.2
  4.2 0.0 copy-start.3
  4.3 1.2 copy-done.3
  5.5 0.0 copy-start.4
  5.5 1.1 copy-done.4
  6.6 0.0 copy-start.5
  6.6 0.9 copy-done.5
  7.6 0.0 copy-start.8
  7.6 0.7 copy-done.8
  8.3 0.0 copy-start.10
  8.3 0.7 copy-done.10
  9.0 0.0 copy-start.11
  9.0 0.7 copy-done.11
  9.6 0.0 copy-start.12
  9.6 0.7 copy-done.12
  10.3 0.0 copy-start.13
  10.3 0.7 copy-done.13
  11.0 0.0 copy-start.14
  11.0 0.7 copy-done.14
  11.6 0.0 copy-start.15
  11.6 0.7 copy-done.15
  12.3 0.0 copy-start.16
  12.3 0.7 copy-done.16
  12.9 0.0 copy-start.17
  12.9 0.7 copy-done.17
  13.6 0.0 copy-start.18
  13.6 0.7 copy-done.18
  14.2 33.2 %gather_weights.1 = (bf16[2,3072,512]{2,1,0:T(8,128)(2,1)S(1)}, f32[2,24,256]{2,1,0:T(8,128)S(1)}, f32[4,64,1024]{2,1,0:T(8,128)S(1)}, f32[32,128]{1,0:T(8,128)S(1)}) custom-call(bf16[256,1536]{1,0:T(8,128)(2,1)S(1)} %copy-done.4, bf16[256,512]{1,0:T(8,128)(2,1)S(1)} %copy-done.5, bf16[256,2048]{1,0:T(8,128)(2,1)S(1)} %copy-done.2, ...), custom_call_target="tpu_custom_call" | custom-call | tf_op jit(solution)/shard_map/gather_weights/pallas_call | solution.py:543
  47.5 0.0 copy-start
  47.5 2.7 %copy-done = bf16[2,3072,512]{2,1,0:T(8,128)(2,1)} copy-done((bf16[2,3072,512]{2,1,0:T(8,128)(2,1)}, bf16[2,3072,512]{2,1,0:T(8,128)(2,1)S(1)}, u32[]{:S(2)}) %copy-start) | copy-done | bytes 6291480
  50.2 0.0 copy-start.1
  50.2 1.0 copy-done.1
  51.1 0.0 copy-start.7
  51.1 0.6 copy-done.7
  51.7 0.0 copy-start.9
  51.7 0.6 copy-done.9
  52.3 75.8 %layer.1 = (bf16[6,196,512]{2,1,0:T(8,128)(2,1)}, f32[6,196,512]{2,1,0:T(8,128)}, bf16[6,224,8192]{2,1,0:T(8,128)(2,1)}, f32[24,512]{1,0:T(8,128)}) custom-call(s32[1]{0:T(128)S(6)} %copy.41.count_ref, bf16[6,196,512]{2,1,0:T(8,128)(2,1)} %tok_ref.1, bf16[6,196,512]{2,1,0:T(8,128)(2,1)} %up_ref.1, bf16[224,196]{1,0:T(8,128)(2,1)} %constant.6.clone.place_ref, ...), custom_call_target="tpu_custom_call" | custom-call | tf_op jit(solution)/shard_map/layer/pallas_call | solution.py:309
  128.1 0.0 copy-start.6
  128.1 16.7 %weight_grads.1 = bf16[12,512,512]{2,1,0:T(8,128)(2,1)S(1)} custom-call(bf16[1344,8192]{1,0:T(8,128)(2,1)} %bitcast.5, bf16[1344,8192]{1,0:T(8,128)(2,1)} %bitcast.6), custom_call_target="tpu_custom_call" | custom-call | tf_op jit(solution)/shard_map/weight_grads/pallas_call | solution.py:361
  144.8 0.0 copy-done.6
  144.8 50.8 %sum_grads.1 = (bf16[3,1024,512]{2,1,0:T(8,128)(2,1)S(1)}, f32[24,256]{1,0:T(8,128)S(1)}) custom-call(bf16[6144,512]{1,0:T(8,128)(2,1)S(1)} %bitcast.3, f32[24,512]{1,0:T(8,128)S(1)} %copy-done.6), custom_call_target="tpu_custom_call" | custom-call | tf_op jit(solution)/shard_map/sum_grads/pallas_call | solution.py:720
  195.7 3.4 %finish.1 = (f32[256]{0:T(256)}, f32[256]{0:T(256)}, f32[256,1536]{1,0:T(8,128)}, f32[256]{0:T(256)}, f32[256]{0:T(256)}, /*index=5*/f32[169,8]{1,0:T(8,128)S(1)...) custom-call(bf16[12,256,512]{2,1,0:T(8,128)(2,1)S(1)} %bitcast.4, ...), custom_call_target="tpu_custom_call" | custom-call | tf_op jit(solution)/shard_map/finish/pallas_call | solution.py:796
  199.1 0.7 copy.40
Async XLA Ops:
  3.0 1.2 copy-start.2
  4.2 1.2 copy-start.3
  5.5 1.1 copy-start.4
  6.6 0.9 copy-start.5
  7.6 0.7 copy-start.8
  8.3 0.7 copy-start.10
  9.0 0.7 copy-start.11
  9.6 0.7 copy-start.12
  10.3 0.7 copy-start.13
  11.0 0.7 copy-start.14
  11.6 0.7 copy-start.15
  12.3 0.7 copy-start.16
  12.9 0.7 copy-start.17
  13.6 0.7 copy-start.18
  47.5 2.7 %copy-start = (bf16[2,3072,512]{2,1,0:T(8,128)(2,1)}, bf16[2,3072,512]{2,1,0:T(8,128)(2,1)S(1)}, u32[]{:S(2)}) copy-start(bf16[2,3072,512]{2,1,0:T(8,128)(2,1)S(1)} %get-tuple-element.43.w_any) | copy-start | bytes 18874372
  50.2 1.0 copy-start.1
  51.1 0.6 copy-start.7
  51.7 0.6 copy-start.9
  128.1 16.7 %copy-start.6 = (f32[24,512]{1,0:T(8,128)S(1)}, f32[24,512]{1,0:T(8,128)}, u32[]{:S(2)}) copy-start(f32[24,512]{1,0:T(8,128)} %get-tuple-element.47.small_ref) | copy-start | bytes 147460

commit v3 on v0

v3 whole, which is shorter than its diff:
```python
from functools import partial

import jax
import jax.numpy as jnp
from jax import lax
from jax.experimental import pallas as pl
from jax.experimental.pallas import tpu as pltpu
from jax.sharding import PartitionSpec as P

WIN = 7
SIDE = 14
SHIFT = 3
EPSILON = 1e-05
MASKED = -1e30
WTOK = WIN * WIN
ROWS = 56
WPAD = 64
BLOCK = 512
F32 = jnp.float32
BF16 = jnp.bfloat16


def nn(left, right):
    return jnp.dot(left, right, preferred_element_type=F32)


def nt(left, right):
    return lax.dot_general(left, right, (((1,), (1,)), ((), ())), preferred_element_type=F32)


def tn(left, right):
    return lax.dot_general(left, right, (((0,), (0,)), ((), ())), preferred_element_type=F32)


def normalize(values):
    center = values - jnp.mean(values, -1, keepdims=True)
    rate = lax.rsqrt(jnp.mean(center * center, -1, keepdims=True) + EPSILON)
    return center * rate, rate


def norm_back(grad, unit, rate, gain):
    scaled = grad * gain
    return rate * (
        scaled
        - jnp.mean(scaled, -1, keepdims=True)
        - unit * jnp.mean(scaled * unit, -1, keepdims=True)
    )


def normal_parts(v):
    size = jnp.abs(v) * 0.7071067811865476
    bell = jnp.exp(-0.5 * v * v)
    t = 1.0 / (1.0 + 0.3275911 * size)
    tail = t * (
        0.254829592
        + t * (-0.284496736 + t * (1.421413741 + t * (-1.453152027 + t * 1.061405429)))
    )
    half = 0.5 * tail * bell
    return jnp.where(v < 0, half, 1.0 - half), 0.3989422804014327 * bell


def col_sum(values):
    return jnp.sum(values, 0, keepdims=True)


MESH = pl.DeviceIdType.MESH
SIDE_CHIPS = 4


class Place:
    def __init__(self):
        replica = lax.axis_index("replica")
        self.hi = lax.axis_index("shard")
        self.core = lax.rem(replica, 2)
        self.at = {
            "x": self.hi * 2 + lax.rem(replica // 2, 2),
            "z": lax.rem(replica // 4, SIDE_CHIPS),
            "y": replica // 16,
        }
        self.lo = lax.rem(replica // 2, 2)

    def id_of(self, core=None, **at):
        place = dict(self.at, **at)
        core = self.core if core is None else core
        lo, hi = lax.rem(place["x"], 2), place["x"] // 2
        return (((place["y"] * SIDE_CHIPS + place["z"]) * 2 + lo) * 2 + core, hi)

    def other_core(self):
        return self.id_of(core=1 - self.core)

    def along(self, axis, step):
        return self.id_of(**{axis: lax.rem(self.at[axis] + step, SIDE_CHIPS)})


def greet(devices):
    barrier = pltpu.get_barrier_semaphore()
    for device in devices:
        pl.semaphore_signal(barrier, inc=1, device_id=device, device_id_type=MESH)
    pl.semaphore_wait(barrier, len(devices))


def pad_window(values):
    return jnp.concatenate([values, jnp.zeros((WPAD - ROWS, values.shape[1]), F32)], 0)


def source_of(row):
    window = jnp.floor((row + 0.5) / ROWS)
    cell = row - window * ROWS
    across = jnp.floor((window + 0.5) / 2)
    down = jnp.floor((cell + 0.5) / WIN)
    i = across * WIN + down + SHIFT
    j = (window - 2 * across) * WIN + (cell - down * WIN) + SHIFT
    i = jnp.where(i >= SIDE, i - SIDE, i)
    j = jnp.where(j >= SIDE, j - SIDE, j)
    return jnp.where(cell < WTOK, i * SIDE + j, -1.0)


def iota(shape, axis):
    return lax.broadcasted_iota(jnp.int32, shape, axis).astype(F32)


def place_matrix():
    rows, tokens = 4 * ROWS, SIDE * SIDE
    return jnp.where(source_of(iota((rows, tokens), 0)) == iota((rows, tokens), 1), 1.0, 0.0)


def back_matrix():
    rows, tokens = 4 * ROWS, SIDE * SIDE
    return jnp.where(source_of(iota((tokens, rows), 1)) == iota((tokens, rows), 0), 1.0, 0.0)


def head_mask():
    shape = (4 * WPAD, 128)
    row, lane = iota(shape, 0), iota(shape, 1)
    return jnp.where(jnp.floor((row + 0.5) / WPAD) == jnp.floor((lane + 0.5) / 32), 1.0, 0.0)


def pair_rows(rel_ref, j):
    return jnp.where(iota((256, 128), 0) == rel_ref[pl.ds(j, 1), :], 1.0, 0.0).astype(BF16)


def spread(part, hmask):
    return jnp.concatenate([part] * 4, 0) * hmask


def fold(full, hmask):
    full = full * hmask.astype(F32)
    total = full[:WPAD]
    for h in range(1, 4):
        total = total + full[h * WPAD : (h + 1) * WPAD]
    return total[:ROWS]


def both_halves(vec_ref, row):
    return jnp.concatenate([vec_ref[0, row : row + 1, :], vec_ref[1, row : row + 1, :]], 1)


def remote(source, target, send_sem, recv_sem, number, device):
    return pltpu.make_async_remote_copy(
        src_ref=source,
        dst_ref=target,
        send_sem=send_sem.at[number],
        recv_sem=recv_sem.at[number],
        device_id=device,
        device_id_type=MESH,
    )


def start(copies):
    for copy in copies:
        copy.start()


def arrived(copies):
    for copy in copies:
        copy.wait_recv()


def sent(copies):
    for copy in copies:
        copy.wait_send()


class Gather:
    SEMAPHORES = 33

    def __init__(self, me, w_ref, v_ref, send_sem, recv_sem):
        self.me, self.w, self.v = me, w_ref, v_ref
        self.sems = (send_sem, recv_sem)

    def flows(self, group):
        count = 1 + group
        for flow, (first, second) in enumerate((("z", "y"), ("y", "z"))):
            block = 4 * group + 2 * count * flow + self.me.core * count
            yield 16 * group + 8 * flow, pl.ds(block, count), first, second

    def copy(self, number, part, device):
        return remote(part, part, *self.sems, number, device)

    def facing(self):
        return self.me.id_of(x=3 - self.me.at["x"])

    def cross(self, group):
        me = self.me
        return [
            self.copy(
                number,
                self.w.at[blocks, me.hi, pl.ds(me.at[second] * 64 + me.at[first] * 16, 16)],
                self.facing(),
            )
            for number, blocks, first, second in self.flows(group)
        ]

    def vectors(self):
        return [self.copy(32, self.v.at[self.me.hi], self.facing())]

    def first(self, group):
        me = self.me
        return [
            self.copy(
                number + step,
                self.w.at[blocks, 1 - me.hi, pl.ds(me.at[second] * 64 + me.at[first] * 16, 16)],
                me.along(first, step),
            )
            for number, blocks, first, second in self.flows(group)
            for step in (1, 2, 3)
        ]

    def second(self, group):
        me = self.me
        return [
            self.copy(
                number + 3 + step,
                self.w.at[blocks, 1 - me.hi, pl.ds(me.at[second] * 64, 64)],
                me.along(second, step),
            )
            for number, blocks, first, second in self.flows(group)
            for step in (1, 2, 3)
        ]

    def last(self, group):
        return [
            self.copy(number + 7, self.w.at[blocks, 1 - self.me.hi], self.me.other_core())
            for number, blocks, _, _ in self.flows(group)
        ]


def front_kernel(
    images,
    count_ref,
    qkv_w, proj_w, fc1_w, fc2_w, n1g, n1b, qb, vb, pb, n2g, n2b, f2b, f1b, table_w, index_w, mask_w,
    tok_ref, up_ref,
    qkv_ref, prob_ref, att_ref, out_ref, gmid_ref, fc_ref, small_ref, vec_out, rel_ref, low_ref,
    vec_ref, w_ref, acts, bias_ref, place_ref, back_ref, hmask_ref, att_s,
    v0, v1, v2, v3, v4, v5, v6, v7, v8, table_v, index_v, mask_v, square, square_mask, pairs,
    w_sem, in_sem, low_sem, send_sem, recv_sem,
):
    step = pl.program_id(0)
    me = Place()
    hi = me.hi
    gather = Gather(me, w_ref, vec_ref, send_sem, recv_sem)
    heads = table_w.shape[1] * 2
    scale = (tok_ref.shape[2] // heads) ** (-0.5)

    def own_weights(group):
        pairs = []
        if group == 0:
            for n in range(3):
                pairs.append((qkv_w.at[:, pl.ds(n * BLOCK, BLOCK)], w_ref.at[n, hi]))
            pairs.append((proj_w, w_ref.at[3, hi]))
        else:
            for m in range(4):
                for half in range(2):
                    pairs.append(
                        (
                            fc1_w.at[:, pl.ds(half * 1024 + m * 256, 256)],
                            w_ref.at[4 + m, hi, :, pl.ds(half * 256, 256)],
                        )
                    )
                pairs.append((fc2_w.at[pl.ds(m * 256, 256)], w_ref.at[8 + m, hi]))
        return [
            pltpu.make_async_copy(source, target, w_sem.at[4 * group + i])
            for i, (source, target) in enumerate(pairs)
        ]

    def own_small():
        sources = (n1g, n1b, qb, vb, pb, n2g, n2b, f2b, f1b, table_w, index_w, mask_w)
        targets = (v0, v1, v2, v3, v4, v5, v6, v7, v8, table_v, index_v, mask_v)
        return [
            pltpu.make_async_copy(source, target, in_sem.at[i])
            for i, (source, target) in enumerate(zip(sources, targets))
        ]

    def low_copy():
        return pltpu.make_async_copy(w_ref.at[pl.ds(0, 4)], low_ref, low_sem.at[0])

    def weight(n):
        return w_ref[n].reshape(BLOCK, BLOCK)

    def vec(row):
        return both_halves(vec_ref, row)

    def note(row, values):
        small_ref[row : row + 1, :] += col_sum(values)

    @pl.when(step == 0)
    def _():
        small_copies = own_small()
        start(own_weights(0))
        start(small_copies)
        start(own_weights(1))
        peers = [gather.facing(), me.other_core()]
        peers += [me.along(axis, s) for axis in ("y", "z") for s in (1, 2, 3)]
        greet(peers)
        for copy in own_weights(0):
            copy.wait()
        start(gather.cross(0))
        for copy in small_copies:
            copy.wait()
        rows = [ref[...].astype(F32).reshape(1, 256) for ref in (v0, v1, v2, v3, v4, v5, v6, v7)]
        rows += [v8[pl.ds(m * 256, 256)].astype(F32).reshape(1, 256) for m in range(4)]
        rows.append(jnp.zeros((4, 256), F32))
        vec_ref[pl.ds(hi, 1), 0:16] = jnp.concatenate(rows, 0)[None]
        table_rows, heads_here = table_v.shape
        square[...] = jnp.zeros_like(square)
        square[0:table_rows, 0:heads_here] = table_v[...].astype(F32)
        vec_ref[pl.ds(hi, 1), 16:24] = jnp.concatenate(
            [square[0:128].T, square[128:256].T], 1
        )[None, 0:8]
        start(gather.vectors())
        for copy in own_weights(1):
            copy.wait()
        arrived(gather.cross(0))
        start(gather.first(0))
        start(gather.cross(1))
        square[0:128] = jnp.full((128, 128), -1.0, F32)
        square[0:WTOK, 0:WTOK] = index_v[...].astype(F32)
        turned = square[0:128].T
        half = WPAD // 2
        rel_ref[...] = jnp.concatenate([turned[:half, :WPAD], turned[half:WPAD, :WPAD]], 1)
        for w in range(4):
            square_mask[w] = jnp.where(iota((WPAD, WPAD), 0) < WTOK, 0.0, MASKED)
            square_mask[w, 0:WTOK, 0:WTOK] = jnp.where(mask_v[w] == 1, 0.0, -100.0)
        place_ref[...] = place_matrix().astype(BF16)
        back_ref[...] = back_matrix().astype(BF16)
        hmask_ref[...] = head_mask().astype(BF16)
        small_ref[...] = jnp.zeros_like(small_ref)
        arrived(gather.first(0))
        start(gather.second(0))
        arrived(gather.vectors())
        table = jnp.concatenate([vec_ref[0, 16:24], vec_ref[1, 16:24]], 0).astype(BF16)

        def body(j, carry):
            pairs[pl.ds(pl.multiple_of(j * heads, heads), heads), :] = nn(table, pair_rows(rel_ref, j))
            return carry

        lax.fori_loop(0, half, body, 0)
        for h in range(heads):
            at = slice(h * WPAD, (h + 1) * WPAD)
            both = pairs[pl.ds(h, half, stride=heads), :]
            for w in range(4):
                bias_ref[w, :half, at] = both[:, :WPAD] + square_mask[w, :half]
                bias_ref[w, half:, at] = both[:, WPAD:] + square_mask[w, half:]
        arrived(gather.second(0))
        start(gather.last(0))
        arrived(gather.cross(1))
        start(gather.first(1))
        vec_out[...] = vec_ref[...]
        arrived(gather.last(0))
        low_copy().start()

    @pl.when(step == 1)
    def _():
        arrived(gather.first(1))
        start(gather.second(1))

    @pl.when(step == SECOND_STEP)
    def _():
        arrived(gather.second(1))
        start(gather.last(1))

    @pl.when(step == images)
    def _():
        arrived(gather.last(1))

    @pl.when(step < images)
    def _():
        hmask = hmask_ref[...]
        unit, _ = normalize(nn(place_ref[...], tok_ref[0]))
        normed = (unit * vec(0) + vec(1)).astype(BF16)
        for n in range(3):
            part = nn(normed, weight(n))
            if n == 0:
                part = (part + vec(2)) * scale
            if n == 2:
                part = part + vec(3)
            for w in range(4):
                qkv_ref[0, w, :, n * BLOCK : (n + 1) * BLOCK] = pad_window(
                    part[w * ROWS : (w + 1) * ROWS]
                ).astype(BF16)
        for w in range(4):
            for g in range(heads // 4):
                at = slice(g * 128, (g + 1) * 128)
                wide = slice(g * 4 * WPAD, (g + 1) * 4 * WPAD)
                q = qkv_ref[0, w, :, g * 128 : (g + 1) * 128]
                k = qkv_ref[0, w, :, BLOCK + g * 128 : BLOCK + (g + 1) * 128]
                v = qkv_ref[0, w, :, 2 * BLOCK + g * 128 : 2 * BLOCK + (g + 1) * 128]
                scores = nt(k, spread(q, hmask)) + bias_ref[w, :, wide]
                raised = jnp.exp(scores - jnp.max(scores, 0, keepdims=True))
                probs = raised * (1.0 / jnp.sum(raised, 0, keepdims=True))
                prob_ref[0, w, :, wide] = probs
                att_s[w * ROWS : (w + 1) * ROWS, at] = fold(tn(probs.astype(BF16), v), hmask)
        att_ref[step] = att_s[...].astype(BF16)

    @pl.when((step >= images) & (step < 2 * images))
    def _():
        image = step - images
        valid = (image < count_ref[0]).astype(F32)
        rows = pl.ds(pl.multiple_of(image * (4 * ROWS), 16), 4 * ROWS)

        def keep(block, values):
            acts[block, rows, :] = values

        middle = nn(place_ref[...], tok_ref[0]) + (nn(att_ref[image], weight(3)) + vec(4))
        unit, rate = normalize(middle)
        normed = (unit * vec(5) + vec(6)).astype(BF16)
        keep(0, normed)
        upstream = nn(place_ref[...], up_ref[0]) * valid
        up_low = upstream.astype(BF16)
        keep(9, up_low)
        note(7, upstream)
        branch = None
        grad = None
        for c in range(4):
            pre = nn(normed, weight(4 + c)) + vec(8 + c)
            below, density = normal_parts(pre)
            act = (pre * below).astype(BF16)
            keep(5 + c, act)
            grad_pre = nt(up_low, weight(8 + c)) * (below + pre * density)
            note(8 + c, grad_pre)
            pre_low = grad_pre.astype(BF16)
            keep(1 + c, pre_low)
            first = nn(act, weight(8 + c))
            second = nt(pre_low, weight(4 + c))
            branch = first if c == 0 else branch + first
            grad = second if c == 0 else grad + second
        result = middle + (branch + vec(7))
        out_ref[0] = nn(back_ref[...], (result * valid).astype(BF16)).astype(BF16)
        note(5, grad * unit)
        note(6, grad)
        grad_middle = upstream + norm_back(grad, unit, rate, vec(5))
        note(4, grad_middle)
        gmid_ref[0] = grad_middle

    @pl.when(step >= 2 * images)
    def _():
        block = step - 2 * images
        left = jnp.where(block < 4, 0, block + 1)
        right = jnp.where(block < 4, block + 1, 9)
        fc_ref[0] = tn(acts[left], acts[right]).astype(BF16)

    @pl.when(step == pl.num_programs(0) - 1)
    def _():
        for group in range(2):
            for copies in (gather.cross, gather.first, gather.second, gather.last):
                sent(copies(group))
        sent(gather.vectors())
        low_copy().wait()


SECOND_STEP = 3


def run_front(matrices, vectors, hidden_bias, table, rel_index, shift_mask, tokens, out_grad, count):
    images, tokens_image, width = tokens.shape
    heads = table.shape[1] * 2
    rows = 4 * ROWS
    far = pl.BlockSpec(memory_space=pltpu.HBM)
    small = vectors + [hidden_bias, table, rel_index, shift_mask]

    def per_image(shape, index):
        return pl.BlockSpec((1,) + shape, lambda b: (index(b),) + (0,) * len(shape))

    def whole(shape):
        return pl.BlockSpec(shape, lambda b: (0,) * len(shape), pipeline_mode=pl.Buffered(1))

    def early(b):
        return jnp.minimum(b, images - 1)

    def late(b):
        return jnp.clip(b - images, 0, images - 1)

    def twice(b):
        return jnp.where(b < images, b, late(b))

    return pl.pallas_call(
        partial(front_kernel, images),
        grid=(2 * images + 8,),
        in_specs=[pl.BlockSpec(memory_space=pltpu.SMEM)]
        + [far] * (4 + len(small))
        + [per_image((tokens_image, width), twice), per_image((tokens_image, width), late)],
        out_specs=[
            per_image((4, WPAD, 3 * BLOCK), early),
            per_image((4, WPAD, heads * WPAD), early),
            whole((images, rows, width)),
            per_image((tokens_image, width), late),
            per_image((rows, width), late),
            per_image((BLOCK, BLOCK), lambda b: jnp.maximum(b - 2 * images, 0)),
            whole((24, BLOCK)),
            whole((2, 24, 256)),
            whole((WPAD // 2, 2 * WPAD)),
            far,
        ],
        out_shape=[
            jax.ShapeDtypeStruct((images, 4, WPAD, 3 * BLOCK), BF16),
            jax.ShapeDtypeStruct((images, 4, WPAD, heads * WPAD), F32),
            jax.ShapeDtypeStruct((images, rows, width), BF16),
            jax.ShapeDtypeStruct(tokens.shape, BF16),
            jax.ShapeDtypeStruct((images, rows, width), F32),
            jax.ShapeDtypeStruct((8, BLOCK, BLOCK), BF16),
            jax.ShapeDtypeStruct((24, BLOCK), F32),
            jax.ShapeDtypeStruct((2, 24, 256), F32),
            jax.ShapeDtypeStruct((WPAD // 2, 2 * WPAD), F32),
            jax.ShapeDtypeStruct((4, 2, 256, BLOCK), BF16),
        ],
        scratch_shapes=[
            pltpu.VMEM((2, 24, 256), F32),
            pltpu.VMEM((12, 2, 256, BLOCK), BF16),
            pltpu.VMEM((10, images * rows, BLOCK), BF16),
            pltpu.VMEM((4, WPAD, heads * WPAD), F32),
            pltpu.VMEM((rows, tokens_image), BF16),
            pltpu.VMEM((tokens_image, rows), BF16),
            pltpu.VMEM((4 * WPAD, 128), BF16),
            pltpu.VMEM((rows, BLOCK), F32),
        ]
        + [pltpu.VMEM(item.shape, item.dtype) for item in small]
        + [
            pltpu.VMEM((256, 128), F32),
            pltpu.VMEM((4, WPAD, WPAD), F32),
            pltpu.VMEM((heads * WPAD // 2, 2 * WPAD), F32),
            pltpu.SemaphoreType.DMA((16,)),
            pltpu.SemaphoreType.DMA((len(small),)),
            pltpu.SemaphoreType.DMA((1,)),
            pltpu.SemaphoreType.DMA((Gather.SEMAPHORES,)),
            pltpu.SemaphoreType.DMA((Gather.SEMAPHORES,)),
        ],
        compiler_params=pltpu.CompilerParams(
            collective_id=0, has_side_effects=True, vmem_limit_bytes=56 * 1024 * 1024
        ),
        name="front",
    )(count, *matrices, *small, tokens, out_grad)


class Reduce:
    SEMAPHORES = 36

    def __init__(self, me, source, own, pair, sums, got, sum_one, got_one, sum_two, got_two, f_ref, first_block, sems, base):
        self.me, self.source, self.own, self.pair, self.sums = me, source, own, pair, sums
        self.got, self.sum_one, self.got_one = got, sum_one, got_one
        self.sum_two, self.got_two, self.f_ref = sum_two, got_two, f_ref
        self.first_block, self.sems, self.base = first_block, sems, base
        self.count = pair.shape[1]

    def axes(self, p):
        return (("y", "z"), ("z", "y"))[p]

    def copy(self, p, number, source, target, device):
        return remote(source, target, *self.sems, self.base + 18 * p + number, device)

    def blocks(self, p, core):
        return pl.ds((2 * p + core) * self.count, self.count)

    def target(self, p):
        return pl.ds(self.first_block + (2 * p + self.me.core) * self.count, self.count)

    def cores(self, p):
        return [
            self.copy(
                p, 0, self.source.at[self.blocks(p, 1 - self.me.core)], self.pair.at[p], self.me.other_core()
            )
        ]

    def add_cores(self, p):
        arrived(self.cores(p))
        for b in range(self.count):
            for half in range(2):
                if self.own is None:
                    block = self.source[pl.ds((2 * p + self.me.core) * self.count + b, 1), half][0]
                else:
                    block = self.own[p, b, half]
                total = block.astype(F32) + self.pair[p, b, half].astype(F32)
                self.sums[p, b, half] = total.astype(BF16)

    def scatter(self, p, stage):
        me, axis = self.me, self.axes(p)[stage]
        rows = (64, 16)[stage]
        source, target = ((self.sums, self.got), (self.sum_one, self.got_one))[stage]
        return [
            self.copy(
                p,
                1 + 3 * stage + s - 1,
                source.at[p, :, :, pl.ds(lax.rem(me.at[axis] + s, SIDE_CHIPS) * rows, rows)],
                target.at[p, s - 1],
                me.along(axis, s),
            )
            for s in (1, 2, 3)
        ]

    def add(self, p, stage):
        arrived(self.scatter(p, stage))
        rows = (64, 16)[stage]
        source, got, target = (
            (self.sums, self.got, self.sum_one),
            (self.sum_one, self.got_one, self.sum_two),
        )[stage]
        at = pl.ds(pl.multiple_of(self.me.at[self.axes(p)[stage]] * rows, 16), rows)
        for b in range(self.count):
            for half in range(2):
                total = source[p, b, half, at, :].astype(F32)
                for s in range(3):
                    total = total + got[p, s, b, half].astype(F32)
                target[p, b, half] = total.astype(BF16)

    def across(self, p):
        me = self.me
        copies = []
        for s in (1, 2, 3):
            peer = lax.rem(me.at["x"] + s, SIDE_CHIPS)
            copies.append(
                self.copy(
                    p, 6 + s, self.sum_two.at[p, :, peer // 2], self.got_two.at[p, me.at["x"]], me.along("x", s)
                )
            )
        return copies

    def keep_own(self, p):
        for b in range(self.count):
            self.got_two[p, pl.ds(self.me.at["x"], 1), b] = self.sum_two[p, b, pl.ds(self.me.hi, 1)]

    def place(self, p):
        first, second = self.axes(p)
        return self.me.at[first] * 64, self.me.at[first] * 64 + self.me.at[second] * 16

    def add_across(self, p):
        arrived(self.across(p))
        _, row = self.place(p)
        at = pl.ds(pl.multiple_of(row, 16), 16)
        for b in range(self.count):
            parts = [self.got_two[p, x, b].astype(F32) for x in range(4)]
            total = (parts[0] + parts[1]) + (parts[2] + parts[3])
            block = self.first_block + (2 * p + self.me.core) * self.count + b
            self.f_ref[pl.ds(block, 1), at] = total.astype(BF16)[None]

    def back(self, p, stage):
        outer, inner = self.place(p)
        axis = self.axes(p)[stage]
        at = pl.ds(outer, 64) if stage == 0 else pl.ds(inner, 16)
        part = self.f_ref.at[self.target(p), at]
        return [
            self.copy(p, 10 + 3 * (1 - stage) + s - 1, part, part, self.me.along(axis, s)) for s in (1, 2, 3)
        ]

    def last(self, p):
        part = self.f_ref.at[self.target(p)]
        return [self.copy(p, 16, part, part, self.me.other_core())]

    def step(self, number):
        for p in range(2):
            if number == 0:
                start(self.cores(p))
            elif number == 1:
                self.add_cores(p)
                start(self.scatter(p, 0))
            elif number == 2:
                self.add(p, 0)
                start(self.scatter(p, 1))
            elif number == 3:
                self.add(p, 1)
                start(self.across(p))
                self.keep_own(p)
            elif number == 4:
                self.add_across(p)
                start(self.back(p, 1))
            elif number == 5:
                arrived(self.back(p, 1))
                start(self.back(p, 0))
            elif number == 6:
                arrived(self.back(p, 0))
                start(self.last(p))
            else:
                arrived(self.last(p))

    def all_sent(self):
        for p in range(2):
            sent(self.cores(p))
            for stage in range(2):
                sent(self.scatter(p, stage))
                sent(self.back(p, stage))
            sent(self.across(p))
            sent(self.last(p))


def back_kernel(
    images,
    heads,
    qkv_ref, prob_ref, att_ref, gmid_ref, tok_ref, w_ref, vec_ref, rel_ref, small_in, fc_ref,
    tg_ref, f_out, small_out,
    f_ref, place_ref, back_ref, hmask_ref, small_ref, pair_ref, fold_s, gatt_s, dqkv_s, acts, low_ref,
    fc_own, fc_pair, fc_sums, fc_got, fc_sum_one, fc_got_one, fc_sum_two, fc_got_two,
    lo_pair, lo_sums, lo_got, lo_sum_one, lo_got_one, lo_sum_two, lo_got_two,
    small_pair, small_x, small_y, small_z, own_sem, out_sem, send_sem, recv_sem,
):
    step = pl.program_id(0)
    me = Place()
    scale = (tok_ref.shape[2] // heads) ** (-0.5)
    sems = (send_sem, recv_sem)
    high = Reduce(
        me, fc_ref, fc_own, fc_pair, fc_sums, fc_got, fc_sum_one, fc_got_one, fc_sum_two, fc_got_two, f_ref, 4, sems, 0
    )
    low = Reduce(
        me, low_ref, None, lo_pair, lo_sums, lo_got, lo_sum_one, lo_got_one, lo_sum_two, lo_got_two, f_ref, 0, sems, 36
    )

    def own_copies():
        return [
            pltpu.make_async_copy(fc_ref.at[high.blocks(p, me.core)], fc_own.at[p], own_sem.at[p])
            for p in range(2)
        ]

    def weight(n):
        return w_ref[n].reshape(BLOCK, BLOCK)

    def vec(row):
        return both_halves(vec_ref, row)

    def note(row, values):
        small_ref[row : row + 1, :] += col_sum(values)

    @pl.when(step == 0)
    def _():
        start(own_copies())
        peers = [me.other_core()]
        peers += [me.along(axis, s) for axis in ("x", "y", "z") for s in (1, 2, 3)]
        greet(peers)
        high.step(0)
        place_ref[...] = place_matrix().astype(BF16)
        back_ref[...] = back_matrix().astype(BF16)
        hmask_ref[...] = head_mask().astype(BF16)
        small_ref[...] = small_in[...]
        pair_ref[...] = jnp.zeros_like(pair_ref)

    @pl.when(step == 1)
    def _():
        for copy in own_copies():
            copy.wait()
        high.step(1)

    for number, at_step in HIGH_STEPS:
        @pl.when(step == at_step)
        def _(number=number):
            high.step(number)

    @pl.when(step < images)
    def _():
        hmask = hmask_ref[...]
        rows = pl.ds(pl.multiple_of(step * (4 * ROWS), 16), 4 * ROWS)

        def keep(block, values):
            acts[block, rows, :] = values

        keep(4, att_ref[0])
        unit, rate = normalize(nn(place_ref[...], tok_ref[0]))
        keep(0, (unit * vec(0) + vec(1)).astype(BF16))
        grad_middle = gmid_ref[0]
        proj_low = grad_middle.astype(BF16)
        keep(5, proj_low)
        grad_att = nt(proj_low, weight(3))
        for w in range(4):
            gatt_s[w] = pad_window(grad_att[w * ROWS : (w + 1) * ROWS]).astype(BF16)
        for w in range(4):
            here = slice(w * ROWS, (w + 1) * ROWS)
            for g in range(heads // 4):
                at = slice(g * 128, (g + 1) * 128)
                wide = slice(g * 4 * WPAD, (g + 1) * 4 * WPAD)
                q = qkv_ref[0, w, :, g * 128 : (g + 1) * 128]
                k = qkv_ref[0, w, :, BLOCK + g * 128 : BLOCK + (g + 1) * 128]
                v = qkv_ref[0, w, :, 2 * BLOCK + g * 128 : 2 * BLOCK + (g + 1) * 128]
                probs = prob_ref[0, w, :, wide]
                spread_grad = spread(gatt_s[w, :, at], hmask)
                grad_v = nn(probs.astype(BF16), spread_grad)
                grad_probs = nt(v, spread_grad)
                weighted = probs * grad_probs
                grad_scores = weighted - probs * jnp.sum(weighted, 0, keepdims=True)
                pair_ref[:, wide] += grad_scores
                scores_low = grad_scores.astype(BF16)
                grad_k = nn(scores_low, spread(q, hmask))
                grad_q = fold(tn(scores_low, k), hmask) * scale
                dqkv_s[here, g * 128 : (g + 1) * 128] = grad_q
                dqkv_s[here, BLOCK + g * 128 : BLOCK + (g + 1) * 128] = grad_k[:ROWS]
                dqkv_s[here, 2 * BLOCK + g * 128 : 2 * BLOCK + (g + 1) * 128] = grad_v[:ROWS]
        grad = None
        for n in range(3):
            part = dqkv_s[:, n * BLOCK : (n + 1) * BLOCK]
            if n == 0:
                note(2, part)
            if n == 2:
                note(3, part)
            part = part.astype(BF16)
            keep(1 + n, part)
            term = nt(part, weight(n))
            grad = term if n == 0 else grad + term
        note(0, grad * unit)
        note(1, grad)
        total = grad_middle + norm_back(grad, unit, rate, vec(0))
        upper = total.astype(BF16)
        rest = (total - upper.astype(F32)).astype(BF16)
        tg_ref[0] = nn(back_ref[...], upper) + nn(back_ref[...], rest)

    small_bufs = {"x": small_x, "y": small_y, "z": small_z}
    small_base = 72

    def small_cores():
        part = small_pair.at[me.core]
        return [remote(part, part, *sems, small_base, me.other_core())]

    def small_copies(axis):
        part = small_bufs[axis].at[me.at[axis]]
        first = small_base + 1 + 3 * "xyz".index(axis)
        return [remote(part, part, *sems, first + s - 1, me.along(axis, s)) for s in (1, 2, 3)]

    def small_start(axis, values):
        small_bufs[axis][pl.ds(me.at[axis], 1)] = values[None]
        start(small_copies(axis))

    def small_sum(axis):
        arrived(small_copies(axis))
        buf = small_bufs[axis]
        return (buf[0] + buf[1]) + (buf[2] + buf[3])

    @pl.when(step == images)
    def _():
        for p in range(2):
            for n in (2 * p, 2 * p + 1):
                left, right = ((0, 1), (0, 2), (0, 3), (4, 5))[n]
                low_ref[n] = tn(acts[left], acts[right]).astype(BF16).reshape(2, 256, BLOCK)
            start(low.cores(p))
        half = WPAD // 2
        for h in range(heads):
            at = slice(h * WPAD, (h + 1) * WPAD)
            both = jnp.concatenate([pair_ref[:half, at], pair_ref[half:, at]], 1)
            fold_s[pl.ds(h, half, stride=heads), :] = both

        def body(j, total):
            values = fold_s[pl.ds(pl.multiple_of(j * heads, heads), heads), :]
            upper = values.astype(BF16)
            rest = (values - upper.astype(F32)).astype(BF16)
            return total + nt(jnp.concatenate([upper, rest], 0), pair_rows(rel_ref, j))

        total = lax.fori_loop(0, half, body, jnp.zeros((2 * heads, 256), F32))
        table = total[:heads] + total[heads:]
        small_ref[12 : 12 + heads // 2, :256] = table[: heads // 2]
        small_ref[12 : 12 + heads // 2, 256:] = table[heads // 2 :]
        small_pair[pl.ds(me.core, 1)] = small_ref[...][None]
        start(small_cores())
        low.step(1)
        for number in TAIL_HIGH[0]:
            high.step(number)
        arrived(small_cores())
        small_start("x", small_pair[0] + small_pair[1])
        low.step(2)
        for number in TAIL_HIGH[1]:
            high.step(number)
        small_start("y", small_sum("x"))
        low.step(3)
        for number in TAIL_HIGH[2]:
            high.step(number)
        small_start("z", small_sum("y"))
        high_out = pltpu.make_async_copy(f_ref.at[pl.ds(4, 8)], f_out.at[pl.ds(4, 8)], out_sem.at[0])
        high_out.start()
        low.step(4)
        low.step(5)
        small_total = small_sum("z")
        small_out[...] = jnp.where(me.hi == 0, small_total[:, :256], small_total[:, 256:])
        low.step(6)
        low.step(7)
        low_out = pltpu.make_async_copy(f_ref.at[pl.ds(0, 4)], f_out.at[pl.ds(0, 4)], out_sem.at[1])
        low_out.start()
        high_out.wait()
        low_out.wait()
        high.all_sent()
        low.all_sent()
        sent(small_cores())
        for axis in "xyz":
            sent(small_copies(axis))


HIGH_STEPS = ((2, 3), (3, 4), (4, 5))
TAIL_HIGH = ((5,), (6,), (7,))


def run_back(qkv, prob, att, gmid, tokens, weights, vecs, rel_rows, small, fc):
    images, tokens_image, width = tokens.shape
    heads = prob.shape[3] // WPAD
    rows = 4 * ROWS
    vmem = pl.BlockSpec(memory_space=pltpu.VMEM)
    far = pl.BlockSpec(memory_space=pltpu.HBM)

    def per_image(shape):
        return pl.BlockSpec(
            (1,) + shape, lambda b: (jnp.minimum(b, images - 1),) + (0,) * len(shape)
        )

    def whole(array):
        return pl.BlockSpec(array.shape, lambda b: (0,) * array.ndim, pipeline_mode=pl.Buffered(1))

    def reduce_scratch(count):
        return [
            pltpu.VMEM((2, count, 2, 256, BLOCK), BF16),
            pltpu.VMEM((2, count, 2, 256, BLOCK), BF16),
            pltpu.VMEM((2, 3, count, 2, 64, BLOCK), BF16),
            pltpu.VMEM((2, count, 2, 64, BLOCK), BF16),
            pltpu.VMEM((2, 3, count, 2, 16, BLOCK), BF16),
            pltpu.VMEM((2, count, 2, 16, BLOCK), BF16),
            pltpu.VMEM((2, 4, count, 16, BLOCK), BF16),
        ]

    return pl.pallas_call(
        partial(back_kernel, images, heads),
        grid=(images + 1,),
        in_specs=[
            per_image(qkv.shape[1:]),
            per_image(prob.shape[1:]),
            per_image(att.shape[1:]),
            per_image(gmid.shape[1:]),
            per_image((tokens_image, width)),
            whole(weights),
            whole(vecs),
            whole(rel_rows),
            whole(small),
            far,
        ],
        out_specs=[per_image((tokens_image, width)), far, vmem],
        out_shape=[
            jax.ShapeDtypeStruct(tokens.shape, F32),
            jax.ShapeDtypeStruct((12, 256, BLOCK), BF16),
            jax.ShapeDtypeStruct((24, 256), F32),
        ],
        scratch_shapes=[
            pltpu.VMEM((12, 256, BLOCK), BF16),
            pltpu.VMEM((rows, tokens_image), BF16),
            pltpu.VMEM((tokens_image, rows), BF16),
            pltpu.VMEM((4 * WPAD, 128), BF16),
            pltpu.VMEM((24, BLOCK), F32),
            pltpu.VMEM((WPAD, heads * WPAD), F32),
            pltpu.VMEM((heads * WPAD // 2, 128), F32),
            pltpu.VMEM((4, WPAD, BLOCK), BF16),
            pltpu.VMEM((rows, 3 * BLOCK), F32),
            pltpu.VMEM((6, images * rows, BLOCK), BF16),
            pltpu.VMEM((4, 2, 256, BLOCK), BF16),
            pltpu.VMEM((2, 2, 2, 256, BLOCK), BF16),
        ]
        + reduce_scratch(2)
        + reduce_scratch(1)
        + [
            pltpu.VMEM((2, 24, BLOCK), F32),
            pltpu.VMEM((4, 24, BLOCK), F32),
            pltpu.VMEM((4, 24, BLOCK), F32),
            pltpu.VMEM((4, 24, BLOCK), F32),
            pltpu.SemaphoreType.DMA((2,)),
            pltpu.SemaphoreType.DMA((2,)),
            pltpu.SemaphoreType.DMA((82,)),
            pltpu.SemaphoreType.DMA((82,)),
        ],
        compiler_params=pltpu.CompilerParams(
            collective_id=1, has_side_effects=True, vmem_limit_bytes=56 * 1024 * 1024
        ),
        name="back",
    )(qkv, prob, att, gmid, tokens, weights, vecs, rel_rows, small, fc)


def finish_kernel(
    f_ref, small_ref, n1g, n1b, qkv, qb, vb, table, proj, pb, n2g, n2b, fc1, f1b, fc2, f2b, wide, turn, sem
):
    copies = []

    def store(source, target):
        copy = pltpu.make_async_copy(source, target, sem.at[len(copies)])
        copy.start()
        copies.append(copy)

    for n in range(12):
        wide[n] = f_ref[n].astype(F32)
        if n < 3:
            store(wide.at[n], qkv.at[:, pl.ds(n * BLOCK, BLOCK)])
        elif n == 3:
            store(wide.at[n], proj)
        elif n < 8:
            for half in range(2):
                store(
                    wide.at[n, :, pl.ds(half * 256, 256)],
                    fc1.at[:, pl.ds(half * 1024 + (n - 4) * 256, 256)],
                )
        else:
            store(wide.at[n], fc2.at[pl.ds((n - 8) * 256, 256)])
    for row, ref in enumerate((n1g, n1b, qb, vb, pb, n2g, n2b, f2b)):
        ref[...] = small_ref[row : row + 1, :].reshape(256)
    for m in range(4):
        f1b[pl.ds(m * 256, 256)] = small_ref[8 + m : 9 + m, :].reshape(256)
    turn[...] = jnp.zeros_like(turn)
    turn[0:8, :] = small_ref[12:20, :]
    table[...] = jnp.concatenate([turn[:, 0:128].T, turn[:, 128:256].T], 0)[
        : table.shape[0], : table.shape[1]
    ]
    for copy in copies:
        copy.wait()


def finish(grads, small, table_rows, heads_here):
    vmem = pl.BlockSpec(memory_space=pltpu.VMEM)
    far = pl.BlockSpec(memory_space=pl.ANY)
    vector, hidden = ((256,), vmem), ((1024,), vmem)
    outs = [
        vector, vector, ((256, 3 * BLOCK), far), vector, vector, ((table_rows, heads_here), vmem),
        ((256, BLOCK), far), vector, vector, vector, ((256, 4 * BLOCK), far), hidden,
        ((1024, BLOCK), far), vector,
    ]
    return pl.pallas_call(
        finish_kernel,
        in_specs=[vmem, vmem],
        out_specs=[spec for _, spec in outs],
        out_shape=[jax.ShapeDtypeStruct(shape, F32) for shape, _ in outs],
        scratch_shapes=[
            pltpu.VMEM((12, 256, BLOCK), F32),
            pltpu.VMEM((128, 256), F32),
            pltpu.SemaphoreType.DMA((16,)),
        ],
        compiler_params=pltpu.CompilerParams(vmem_limit_bytes=30 * 1024 * 1024),
        name="finish",
    )(grads, small)


def local(
    tokens, image_counts, shift_mask, rel_index, norm1_gain, norm1_bias, qkv_weight, q_bias, v_bias,
    rel_table, proj_weight, proj_bias, norm2_gain, norm2_bias, fc1_weight, fc1_bias, fc2_weight,
    fc2_bias, out_grad,
):
    table_rows, heads_here = rel_table.shape
    qkv, prob, att, block_out, gmid, fc, small, vecs, rel_rows, low_weights = run_front(
        [qkv_weight, proj_weight, fc1_weight, fc2_weight],
        [norm1_gain, norm1_bias, q_bias, v_bias, proj_bias, norm2_gain, norm2_bias, fc2_bias],
        fc1_bias, rel_table, rel_index, shift_mask, tokens, out_grad, image_counts,
    )
    tokens_grad, grads, small = run_back(
        qkv, prob, att, gmid, tokens, low_weights, vecs, rel_rows, small, fc.reshape(8, 2, 256, BLOCK)
    )
    outs = finish(grads, small, table_rows, heads_here)
    return (block_out, tokens_grad, *outs)


def solution(mesh):
    split = P(("replica", "shard"), None, None)
    vector, matrix, table = P("shard"), P("shard", None), P(None, "shard")
    return jax.shard_map(
        local,
        mesh=mesh,
        in_specs=(
            split, P(("replica", "shard")), P(), P(), vector, vector, matrix, vector, vector, table,
            matrix, vector, vector, vector, matrix, vector, matrix, vector, split,
        ),
        out_specs=(
            split, split, vector, vector, matrix, vector, vector, table, matrix, vector, vector,
            vector, matrix, vector, matrix, vector,
        ),
        check_vma=False,
    )
```

time: 782 us -> 178 us (0.23); the launches traced: 770 us -> 178 us
  blocking collectives: 398 us -> 0 us
  Pallas kernels: 0 us -> 167 us
  local copies, waits for them, and re-layouts: 154 us -> 10.1 us
  matrix products: 132 us -> 0 us
  other arithmetic: 51.3 us -> 0 us
  waiting for transfers between devices: 16.5 us -> 0 us
  between operations: 17.5 us -> 1.33 us
    psum x1 -> x0, blocking collectives: 326 us -> none  [local(): lax.psum((all_share[0], all_share[1], all_share[2], all_share[3], all_sha...]
    pallas_call x0 -> x3, Pallas kernels: none -> 167 us  [the longest x1 83.9 us: run_back(): pl.pallas_call(partial(back_kernel, images, heads), grid=(images + 1,), i...]
    dot_general x20 -> x0, matrix products: 132 us -> none  [the longest x1 26.9 us: local(): jnp.dot(normed_two, gathered[10], preferred_element_type=jnp.float32)]
    all_gather x11 -> x0, blocking collectives: 64 us -> none  [the longest x1 15.3 us: local(): lax.all_gather(proj_weight, 'shard', axis=0, tiled=True)]
    reshape x19 -> x0, local copies, waits for them, and re-layouts: 53.1 us -> none  [the longest x2 11.9 us: local(): grad_att = back_product(proj_low, back_params[6]).astype(jnp.bfloat16).re...]
    concatenate x9 -> x0, local copies, waits for them, and re-layouts: 52.2 us -> none  [local(): jnp.concatenate([grad_queries, grad_keys, grad_values], -1)]
    reduce_sum x15 -> x0, other arithmetic: 34.8 us -> none  [the longest x3 9.46 us: row_sum(): return jnp.sum(values.reshape(-1, values.shape[-1]), 0)]
    another operation x6 -> x0, local copies, waits for them, and re-layouts: 17.9 us -> none
  transfers between devices with their start and end apart: 8 -> 0, of which waited for: 1 -> 0; matrix products, arithmetic and copies ran while one was open for 31% -> 0% of each run, Pallas kernels for 0% -> 0%
where the time goes in v3:
time: 178 us
  Pallas kernels  167 us (94%)
  local copies, waits for them, and re-layouts  10.1 us (6%)
    pallas_call x1, Pallas kernels, run_back(): pl.pallas_call(partial(back_kernel, images, heads), grid=(images + 1,), i...  83.9 us
    pallas_call x1, Pallas kernels, run_front(): pl.pallas_call(partial(front_kernel, images), grid=(2 * images + 8,), in_...  79 us
    unnamed x11, local copies, waits for them, and re-layouts  10.1 us
    pallas_call x1, Pallas kernels, finish(): pl.pallas_call(finish_kernel, in_specs=[vmem, vmem], out_specs=[spec for...  3.64 us

profile of v3, /device:TPU:1, one launch (start us, length us, event | category | flops | bytes accessed | tf_op | source)
XLA Modules:
  0.0 177.9 jit_solution(6831397572838854289)
XLA Ops:
  1.3 1.4 copy.35.table_w
  2.7 1.5 copy.36.mask_w
  4.3 79.0 %front.1 = (bf16[6,4,64,1536]{3,2,1,0:T(8,128)(2,1)}, f32[6,4,64,1024]{3,2,1,0:T(8,128)}, bf16[6,224,512]{2,1,0:T(8,128)(2,1)}, bf16[6,196,512]{2,1,0:T(8,128)(2...) custom-call(s32[1]{0:T(128)S(6)} %copy.40.count_ref, ...), custom_call_target="tpu_custom_call" | custom-call | tf_op jit(solution)/shard_map/front/pallas_call | solution.py:496
  83.2 83.9 %back.1 = (f32[6,196,512]{2,1,0:T(8,128)}, bf16[12,256,512]{2,1,0:T(8,128)(2,1)}, f32[24,256]{1,0:T(8,128)}) custom-call(bf16[6,4,64,1536]{3,2,1,0:T(8,128)(2,1)} %get-tuple-element.44.qkv_ref, f32[6,4,64,1024]{3,2,1,0:T(8,128)} %get-tuple-element.45.prob_ref, bf16[6,224,512]{2,1,0:T(8,128)(2,1)} %get-tuple-element.46.att_ref, ...), custom_call_target="tpu_custom_call" | custom-call | tf_op jit(solution)/shard_map/back/pallas_call | solution.py:927
  167.2 0.0 copy-start
  167.2 1.9 %copy-done = bf16[12,256,512]{2,1,0:T(8,128)(2,1)S(1)} copy-done((bf16[12,256,512]{2,1,0:T(8,128)(2,1)S(1)}, bf16[12,256,512]{2,1,0:T(8,128)(2,1)}, u32[]{:S(2)}) %copy-start) | copy-done | bytes 3145752
  169.0 0.0 copy-start.1
  169.1 0.7 copy-done.1
  169.8 0.0 copy-start.2
  169.8 3.6 %finish.1 = (f32[256]{0:T(256)}, f32[256]{0:T(256)}, f32[256,1536]{1,0:T(8,128)}, f32[256]{0:T(256)}, f32[256]{0:T(256)}, /*index=5*/f32[169,8]{1,0:T(8,128)S(1)...) custom-call(bf16[12,256,512]{2,1,0:T(8,128)(2,1)S(1)} %copy-done, ...), custom_call_target="tpu_custom_call" | custom-call | tf_op jit(solution)/shard_map/finish/pallas_call | solution.py:1027
  173.4 0.7 copy.37
  174.1 2.4 %copy.41 = bf16[6,196,512]{2,1,0:T(8,128)(2,1)} copy(bf16[6,196,512]{2,1,0:T(8,128)(2,1)} %get-tuple-element.102) | data formatting | bytes 2408448
  176.5 0.0 copy-done.2
  176.5 1.4 copy.42
Async XLA Ops:
  167.2 1.9 %copy-start = (bf16[12,256,512]{2,1,0:T(8,128)(2,1)S(1)}, bf16[12,256,512]{2,1,0:T(8,128)(2,1)}, u32[]{:S(2)}) copy-start(bf16[12,256,512]{2,1,0:T(8,128)(2,1)} %get-tuple-element.54.f_ref) | copy-start | bytes 9437188
  169.0 0.7 copy-start.1
  169.8 6.7 %copy-start.2 = (f32[6,196,512]{2,1,0:T(8,128)S(1)}, f32[6,196,512]{2,1,0:T(8,128)}, u32[]{:S(2)}) copy-start(f32[6,196,512]{2,1,0:T(8,128)} %get-tuple-element.103) | copy-start | bytes 7225348

commit v4 on v3

--- a/solution.py
+++ b/solution.py
@@ -250,8 +250,8 @@
     count_ref,
     qkv_w, proj_w, fc1_w, fc2_w, n1g, n1b, qb, vb, pb, n2g, n2b, f2b, f1b, table_w, index_w, mask_w,
     tok_ref, up_ref,
-    qkv_ref, prob_ref, att_ref, out_ref, gmid_ref, fc_ref, small_ref, vec_out, rel_ref, low_ref,
-    vec_ref, w_ref, acts, bias_ref, place_ref, back_ref, hmask_ref, att_s,
+    qkv_ref, prob_ref, normed_ref, att_ref, out_ref, gmid_ref, fc_ref, small_ref, vec_out, rel_ref, low_ref,
+    vec_ref, w_ref, acts, bias_ref, place_ref, hmask_ref, att_s, qkv_s, prob_s, acts_s,
     v0, v1, v2, v3, v4, v5, v6, v7, v8, table_v, index_v, mask_v, square, square_mask, pairs,
     w_sem, in_sem, low_sem, send_sem, recv_sem,
 ):
@@ -259,7 +259,7 @@
     me = Place()
     hi = me.hi
     gather = Gather(me, w_ref, vec_ref, send_sem, recv_sem)
-    heads = table_w.shape[1] * 2
+    heads = table_w.shape[0] * 2
     scale = (tok_ref.shape[2] // heads) ** (-0.5)
 
     def own_weights(group):
@@ -321,58 +321,51 @@
         rows += [v8[pl.ds(m * 256, 256)].astype(F32).reshape(1, 256) for m in range(4)]
         rows.append(jnp.zeros((4, 256), F32))
         vec_ref[pl.ds(hi, 1), 0:16] = jnp.concatenate(rows, 0)[None]
-        table_rows, heads_here = table_v.shape
-        square[...] = jnp.zeros_like(square)
-        square[0:table_rows, 0:heads_here] = table_v[...].astype(F32)
-        vec_ref[pl.ds(hi, 1), 16:24] = jnp.concatenate(
-            [square[0:128].T, square[128:256].T], 1
-        )[None, 0:8]
+        heads_here, table_rows = table_v.shape
+        vec_ref[pl.ds(hi, 1), 16:24] = jnp.zeros((1, 8, 256), F32)
+        vec_ref[pl.ds(hi, 1), 16:24, 0:table_rows] = table_v[...].astype(F32)[None]
         start(gather.vectors())
         for copy in own_weights(1):
             copy.wait()
+        start(gather.cross(1))
         arrived(gather.cross(0))
         start(gather.first(0))
-        start(gather.cross(1))
-        square[0:128] = jnp.full((128, 128), -1.0, F32)
+        arrived(gather.cross(1))
+        start(gather.first(1))
+        square[...] = jnp.full((128, 128), -1.0, F32)
         square[0:WTOK, 0:WTOK] = index_v[...].astype(F32)
-        turned = square[0:128].T
+        turned = square[...].T
         half = WPAD // 2
         rel_ref[...] = jnp.concatenate([turned[:half, :WPAD], turned[half:WPAD, :WPAD]], 1)
         for w in range(4):
             square_mask[w] = jnp.where(iota((WPAD, WPAD), 0) < WTOK, 0.0, MASKED)
-            square_mask[w, 0:WTOK, 0:WTOK] = jnp.where(mask_v[w] == 1, 0.0, -100.0)
+            square_mask[w, 0:WTOK, 0:WTOK] = jnp.where(mask_v[:, w, :] == 1, 0.0, -100.0)
         place_ref[...] = place_matrix().astype(BF16)
-        back_ref[...] = back_matrix().astype(BF16)
         hmask_ref[...] = head_mask().astype(BF16)
         small_ref[...] = jnp.zeros_like(small_ref)
         arrived(gather.first(0))
         start(gather.second(0))
+        arrived(gather.first(1))
+        start(gather.second(1))
         arrived(gather.vectors())
+        vec_out[...] = vec_ref[...]
         table = jnp.concatenate([vec_ref[0, 16:24], vec_ref[1, 16:24]], 0).astype(BF16)
 
         def body(j, carry):
             pairs[pl.ds(pl.multiple_of(j * heads, heads), heads), :] = nn(table, pair_rows(rel_ref, j))
             return carry
 
-        lax.fori_loop(0, half, body, 0)
+        lax.fori_loop(0, half, body, 0, unroll=4)
+        arrived(gather.second(0))
+        start(gather.last(0))
         for h in range(heads):
             at = slice(h * WPAD, (h + 1) * WPAD)
             both = pairs[pl.ds(h, half, stride=heads), :]
             for w in range(4):
                 bias_ref[w, :half, at] = both[:, :WPAD] + square_mask[w, :half]
                 bias_ref[w, half:, at] = both[:, WPAD:] + square_mask[w, half:]
-        arrived(gather.second(0))
-        start(gather.last(0))
-        arrived(gather.cross(1))
-        start(gather.first(1))
-        vec_out[...] = vec_ref[...]
         arrived(gather.last(0))
         low_copy().start()
-
-    @pl.when(step == 1)
-    def _():
-        arrived(gather.first(1))
-        start(gather.second(1))
 
     @pl.when(step == SECOND_STEP)
     def _():
@@ -395,22 +388,25 @@
             if n == 2:
                 part = part + vec(3)
             for w in range(4):
-                qkv_ref[0, w, :, n * BLOCK : (n + 1) * BLOCK] = pad_window(
+                qkv_s[w, :, n * BLOCK : (n + 1) * BLOCK] = pad_window(
                     part[w * ROWS : (w + 1) * ROWS]
                 ).astype(BF16)
         for w in range(4):
             for g in range(heads // 4):
                 at = slice(g * 128, (g + 1) * 128)
                 wide = slice(g * 4 * WPAD, (g + 1) * 4 * WPAD)
-                q = qkv_ref[0, w, :, g * 128 : (g + 1) * 128]
-                k = qkv_ref[0, w, :, BLOCK + g * 128 : BLOCK + (g + 1) * 128]
-                v = qkv_ref[0, w, :, 2 * BLOCK + g * 128 : 2 * BLOCK + (g + 1) * 128]
+                q = qkv_s[w, :, g * 128 : (g + 1) * 128]
+                k = qkv_s[w, :, BLOCK + g * 128 : BLOCK + (g + 1) * 128]
+                v = qkv_s[w, :, 2 * BLOCK + g * 128 : 2 * BLOCK + (g + 1) * 128]
                 scores = nt(k, spread(q, hmask)) + bias_ref[w, :, wide]
                 raised = jnp.exp(scores - jnp.max(scores, 0, keepdims=True))
                 probs = raised * (1.0 / jnp.sum(raised, 0, keepdims=True))
-                prob_ref[0, w, :, wide] = probs
+                prob_s[w, :, wide] = probs
                 att_s[w * ROWS : (w + 1) * ROWS, at] = fold(tn(probs.astype(BF16), v), hmask)
         att_ref[step] = att_s[...].astype(BF16)
+        normed_ref[0] = normed
+        qkv_ref[0] = qkv_s[...]
+        prob_ref[0] = prob_s[...]
 
     @pl.when((step >= images) & (step < 2 * images))
     def _():
@@ -419,7 +415,7 @@
         rows = pl.ds(pl.multiple_of(image * (4 * ROWS), 16), 4 * ROWS)
 
         def keep(block, values):
-            acts[block, rows, :] = values
+            acts_s[block] = values
 
         middle = nn(place_ref[...], tok_ref[0]) + (nn(att_ref[image], weight(3)) + vec(4))
         unit, rate = normalize(middle)
@@ -445,12 +441,14 @@
             branch = first if c == 0 else branch + first
             grad = second if c == 0 else grad + second
         result = middle + (branch + vec(7))
-        out_ref[0] = nn(back_ref[...], (result * valid).astype(BF16)).astype(BF16)
         note(5, grad * unit)
         note(6, grad)
         grad_middle = upstream + norm_back(grad, unit, rate, vec(5))
         note(4, grad_middle)
         gmid_ref[0] = grad_middle
+        out_ref[0] = (result * valid).astype(BF16)
+        for block in range(10):
+            acts[block, rows, :] = acts_s[block]
 
     @pl.when(step >= 2 * images)
     def _():
@@ -473,7 +471,7 @@
 
 def run_front(matrices, vectors, hidden_bias, table, rel_index, shift_mask, tokens, out_grad, count):
     images, tokens_image, width = tokens.shape
-    heads = table.shape[1] * 2
+    heads = table.shape[0] * 2
     rows = 4 * ROWS
     far = pl.BlockSpec(memory_space=pltpu.HBM)
     small = vectors + [hidden_bias, table, rel_index, shift_mask]
@@ -502,8 +500,9 @@
         out_specs=[
             per_image((4, WPAD, 3 * BLOCK), early),
             per_image((4, WPAD, heads * WPAD), early),
+            per_image((rows, width), early),
             whole((images, rows, width)),
-            per_image((tokens_image, width), late),
+            per_image((rows, width), late),
             per_image((rows, width), late),
             per_image((BLOCK, BLOCK), lambda b: jnp.maximum(b - 2 * images, 0)),
             whole((24, BLOCK)),
@@ -515,7 +514,8 @@
             jax.ShapeDtypeStruct((images, 4, WPAD, 3 * BLOCK), BF16),
             jax.ShapeDtypeStruct((images, 4, WPAD, heads * WPAD), F32),
             jax.ShapeDtypeStruct((images, rows, width), BF16),
-            jax.ShapeDtypeStruct(tokens.shape, BF16),
+            jax.ShapeDtypeStruct((images, rows, width), BF16),
+            jax.ShapeDtypeStruct((images, rows, width), BF16),
             jax.ShapeDtypeStruct((images, rows, width), F32),
             jax.ShapeDtypeStruct((8, BLOCK, BLOCK), BF16),
             jax.ShapeDtypeStruct((24, BLOCK), F32),
@@ -529,13 +529,15 @@
             pltpu.VMEM((10, images * rows, BLOCK), BF16),
             pltpu.VMEM((4, WPAD, heads * WPAD), F32),
             pltpu.VMEM((rows, tokens_image), BF16),
-            pltpu.VMEM((tokens_image, rows), BF16),
             pltpu.VMEM((4 * WPAD, 128), BF16),
             pltpu.VMEM((rows, BLOCK), F32),
+            pltpu.VMEM((4, WPAD, 3 * BLOCK), BF16),
+            pltpu.VMEM((4, WPAD, heads * WPAD), F32),
+            pltpu.VMEM((10, rows, BLOCK), BF16),
         ]
         + [pltpu.VMEM(item.shape, item.dtype) for item in small]
         + [
-            pltpu.VMEM((256, 128), F32),
+            pltpu.VMEM((128, 128), F32),
             pltpu.VMEM((4, WPAD, WPAD), F32),
             pltpu.VMEM((heads * WPAD // 2, 2 * WPAD), F32),
             pltpu.SemaphoreType.DMA((16,)),
@@ -703,12 +705,12 @@
 def back_kernel(
     images,
     heads,
-    qkv_ref, prob_ref, att_ref, gmid_ref, tok_ref, w_ref, vec_ref, rel_ref, small_in, fc_ref,
+    qkv_ref, prob_ref, normed_ref, att_ref, gmid_ref, tok_ref, w_ref, vec_ref, rel_ref, small_in, fc_ref,
     tg_ref, f_out, small_out,
-    f_ref, place_ref, back_ref, hmask_ref, small_ref, pair_ref, fold_s, gatt_s, dqkv_s, acts, low_ref,
+    qkv_s, prob_s, gmid_s, acts_s, f_ref, place_ref, hmask_ref, small_ref, pair_ref, fold_s, gatt_s, dqkv_s, acts, low_ref,
     fc_own, fc_pair, fc_sums, fc_got, fc_sum_one, fc_got_one, fc_sum_two, fc_got_two,
     lo_pair, lo_sums, lo_got, lo_sum_one, lo_got_one, lo_sum_two, lo_got_two,
-    small_pair, small_x, small_y, small_z, own_sem, out_sem, send_sem, recv_sem,
+    small_pair, small_halves, small_x, small_y, small_z, own_sem, out_sem, send_sem, recv_sem,
 ):
     step = pl.program_id(0)
     me = Place()
@@ -744,7 +746,6 @@
         greet(peers)
         high.step(0)
         place_ref[...] = place_matrix().astype(BF16)
-        back_ref[...] = back_matrix().astype(BF16)
         hmask_ref[...] = head_mask().astype(BF16)
         small_ref[...] = small_in[...]
         pair_ref[...] = jnp.zeros_like(pair_ref)
@@ -753,12 +754,12 @@
     def _():
         for copy in own_copies():
             copy.wait()
-        high.step(1)
-
-    for number, at_step in HIGH_STEPS:
+
+    for at_step, moves in PLAN:
         @pl.when(step == at_step)
-        def _(number=number):
-            high.step(number)
+        def _(moves=moves):
+            for group, number in moves:
+                (high if group == "high" else low).step(number)
 
     @pl.when(step < images)
     def _():
@@ -766,55 +767,65 @@
         rows = pl.ds(pl.multiple_of(step * (4 * ROWS), 16), 4 * ROWS)
 
         def keep(block, values):
-            acts[block, rows, :] = values
-
+            acts_s[block] = values
+
+        qkv_s[...] = qkv_ref[0]
+        prob_s[...] = prob_ref[0]
+        gmid_s[...] = gmid_ref[0]
         keep(4, att_ref[0])
-        unit, rate = normalize(nn(place_ref[...], tok_ref[0]))
-        keep(0, (unit * vec(0) + vec(1)).astype(BF16))
-        grad_middle = gmid_ref[0]
+        keep(0, normed_ref[0])
+        grad_middle = gmid_s[...]
         proj_low = grad_middle.astype(BF16)
         keep(5, proj_low)
         grad_att = nt(proj_low, weight(3))
         for w in range(4):
             gatt_s[w] = pad_window(grad_att[w * ROWS : (w + 1) * ROWS]).astype(BF16)
+        groups = range(heads // 4)
+        ats = [slice(g * 128, (g + 1) * 128) for g in groups]
+        wides = [slice(g * 4 * WPAD, (g + 1) * 4 * WPAD) for g in groups]
         for w in range(4):
             here = slice(w * ROWS, (w + 1) * ROWS)
-            for g in range(heads // 4):
-                at = slice(g * 128, (g + 1) * 128)
-                wide = slice(g * 4 * WPAD, (g + 1) * 4 * WPAD)
-                q = qkv_ref[0, w, :, g * 128 : (g + 1) * 128]
-                k = qkv_ref[0, w, :, BLOCK + g * 128 : BLOCK + (g + 1) * 128]
-                v = qkv_ref[0, w, :, 2 * BLOCK + g * 128 : 2 * BLOCK + (g + 1) * 128]
-                probs = prob_ref[0, w, :, wide]
-                spread_grad = spread(gatt_s[w, :, at], hmask)
-                grad_v = nn(probs.astype(BF16), spread_grad)
-                grad_probs = nt(v, spread_grad)
-                weighted = probs * grad_probs
+
+            def part(n, g, w=w):
+                return qkv_s[w, :, n * BLOCK + g * 128 : n * BLOCK + (g + 1) * 128]
+
+            spread_grad = [spread(gatt_s[w, :, ats[g]], hmask) for g in groups]
+            grad_probs = [nt(part(2, g), spread_grad[g]) for g in groups]
+            grad_v = [nn(prob_s[w, :, wides[g]].astype(BF16), spread_grad[g]) for g in groups]
+            scores_low = []
+            for g in groups:
+                probs = prob_s[w, :, wides[g]]
+                weighted = probs * grad_probs[g]
                 grad_scores = weighted - probs * jnp.sum(weighted, 0, keepdims=True)
-                pair_ref[:, wide] += grad_scores
-                scores_low = grad_scores.astype(BF16)
-                grad_k = nn(scores_low, spread(q, hmask))
-                grad_q = fold(tn(scores_low, k), hmask) * scale
-                dqkv_s[here, g * 128 : (g + 1) * 128] = grad_q
-                dqkv_s[here, BLOCK + g * 128 : BLOCK + (g + 1) * 128] = grad_k[:ROWS]
-                dqkv_s[here, 2 * BLOCK + g * 128 : 2 * BLOCK + (g + 1) * 128] = grad_v[:ROWS]
-        grad = None
+                pair_ref[:, wides[g]] += grad_scores
+                scores_low.append(grad_scores.astype(BF16))
+            grad_k = [nn(scores_low[g], spread(part(0, g), hmask)) for g in groups]
+            grad_q = [tn(scores_low[g], part(1, g)) for g in groups]
+            for g in groups:
+                dqkv_s[here, 2 * BLOCK + g * 128 : 2 * BLOCK + (g + 1) * 128] = grad_v[g][:ROWS]
+                dqkv_s[here, BLOCK + g * 128 : BLOCK + (g + 1) * 128] = grad_k[g][:ROWS]
+                dqkv_s[here, g * 128 : (g + 1) * 128] = fold(grad_q[g], hmask) * scale
         for n in range(3):
             part = dqkv_s[:, n * BLOCK : (n + 1) * BLOCK]
             if n == 0:
                 note(2, part)
             if n == 2:
                 note(3, part)
-            part = part.astype(BF16)
-            keep(1 + n, part)
-            term = nt(part, weight(n))
+            keep(1 + n, part.astype(BF16))
+        for block in range(6):
+            acts[block, rows, :] = acts_s[block]
+
+    @pl.when(step > images)
+    def _():
+        rows = pl.ds(pl.multiple_of((step - images - 1) * (4 * ROWS), 16), 4 * ROWS)
+        unit, rate = normalize(nn(place_ref[...], tok_ref[0]))
+        grad = None
+        for n in range(3):
+            term = nt(acts[1 + n, rows, :], weight(n))
             grad = term if n == 0 else grad + term
         note(0, grad * unit)
         note(1, grad)
-        total = grad_middle + norm_back(grad, unit, rate, vec(0))
-        upper = total.astype(BF16)
-        rest = (total - upper.astype(F32)).astype(BF16)
-        tg_ref[0] = nn(back_ref[...], upper) + nn(back_ref[...], rest)
+        tg_ref[0] = gmid_ref[0] + norm_back(grad, unit, rate, vec(0))
 
     small_bufs = {"x": small_x, "y": small_y, "z": small_z}
     small_base = 72
@@ -828,12 +839,20 @@
         first = small_base + 1 + 3 * "xyz".index(axis)
         return [remote(part, part, *sems, first + s - 1, me.along(axis, s)) for s in (1, 2, 3)]
 
+    def small_across():
+        copies = []
+        for s in (1, 2, 3):
+            peer = lax.rem(me.at["x"] + s, SIDE_CHIPS)
+            source, target = small_halves.at[peer // 2], small_x.at[me.at["x"]]
+            copies.append(remote(source, target, *sems, small_base + s, me.along("x", s)))
+        return copies
+
     def small_start(axis, values):
         small_bufs[axis][pl.ds(me.at[axis], 1)] = values[None]
         start(small_copies(axis))
 
     def small_sum(axis):
-        arrived(small_copies(axis))
+        arrived(small_across() if axis == "x" else small_copies(axis))
         buf = small_bufs[axis]
         return (buf[0] + buf[1]) + (buf[2] + buf[3])
 
@@ -844,6 +863,9 @@
                 left, right = ((0, 1), (0, 2), (0, 3), (4, 5))[n]
                 low_ref[n] = tn(acts[left], acts[right]).astype(BF16).reshape(2, 256, BLOCK)
             start(low.cores(p))
+            if p == 0:
+                for number in DURING_GRADS:
+                    high.step(number)
         half = WPAD // 2
         for h in range(heads):
             at = slice(h * WPAD, (h + 1) * WPAD)
@@ -856,31 +878,31 @@
             rest = (values - upper.astype(F32)).astype(BF16)
             return total + nt(jnp.concatenate([upper, rest], 0), pair_rows(rel_ref, j))
 
-        total = lax.fori_loop(0, half, body, jnp.zeros((2 * heads, 256), F32))
+        total = lax.fori_loop(0, half, body, jnp.zeros((2 * heads, 256), F32), unroll=4)
         table = total[:heads] + total[heads:]
         small_ref[12 : 12 + heads // 2, :256] = table[: heads // 2]
         small_ref[12 : 12 + heads // 2, 256:] = table[heads // 2 :]
+
+    @pl.when(step == 2 * images)
+    def _():
         small_pair[pl.ds(me.core, 1)] = small_ref[...][None]
         start(small_cores())
-        low.step(1)
-        for number in TAIL_HIGH[0]:
-            high.step(number)
+        high.step(7)
+        high_out = pltpu.make_async_copy(f_ref.at[pl.ds(4, 8)], f_out.at[pl.ds(4, 8)], out_sem.at[0])
+        high_out.start()
         arrived(small_cores())
-        small_start("x", small_pair[0] + small_pair[1])
+        small_total = small_pair[0] + small_pair[1]
+        small_halves[0] = small_total[:, :256]
+        small_halves[1] = small_total[:, 256:]
+        start(small_across())
+        small_x[pl.ds(me.at["x"], 1)] = small_halves[pl.ds(me.hi, 1)]
         low.step(2)
-        for number in TAIL_HIGH[1]:
-            high.step(number)
         small_start("y", small_sum("x"))
         low.step(3)
-        for number in TAIL_HIGH[2]:
-            high.step(number)
         small_start("z", small_sum("y"))
-        high_out = pltpu.make_async_copy(f_ref.at[pl.ds(4, 8)], f_out.at[pl.ds(4, 8)], out_sem.at[0])
-        high_out.start()
         low.step(4)
+        small_out[...] = small_sum("z")
         low.step(5)
-        small_total = small_sum("z")
-        small_out[...] = jnp.where(me.hi == 0, small_total[:, :256], small_total[:, 256:])
         low.step(6)
         low.step(7)
         low_out = pltpu.make_async_copy(f_ref.at[pl.ds(0, 4)], f_out.at[pl.ds(0, 4)], out_sem.at[1])
@@ -890,25 +912,40 @@
         high.all_sent()
         low.all_sent()
         sent(small_cores())
-        for axis in "xyz":
-            sent(small_copies(axis))
-
-
-HIGH_STEPS = ((2, 3), (3, 4), (4, 5))
-TAIL_HIGH = ((5,), (6,), (7,))
-
-
-def run_back(qkv, prob, att, gmid, tokens, weights, vecs, rel_rows, small, fc):
+        sent(small_across())
+        sent(small_copies("y"))
+        sent(small_copies("z"))
+
+
+PLAN = (
+    (1, (("high", 1),)),
+    (4, (("high", 2),)),
+    (5, (("high", 3),)),
+    (6, (("high", 4),)),
+    (8, (("low", 1),)),
+    (9, (("high", 6),)),
+)
+DURING_GRADS = (5,)
+
+
+def run_back(qkv, prob, normed, att, gmid, tokens, weights, vecs, rel_rows, small, fc):
     images, tokens_image, width = tokens.shape
     heads = prob.shape[3] // WPAD
     rows = 4 * ROWS
     vmem = pl.BlockSpec(memory_space=pltpu.VMEM)
     far = pl.BlockSpec(memory_space=pltpu.HBM)
 
-    def per_image(shape):
-        return pl.BlockSpec(
-            (1,) + shape, lambda b: (jnp.minimum(b, images - 1),) + (0,) * len(shape)
-        )
+    def per_image(shape, index):
+        return pl.BlockSpec((1,) + shape, lambda b: (index(b),) + (0,) * len(shape))
+
+    def early(b):
+        return jnp.minimum(b, images - 1)
+
+    def late(b):
+        return jnp.maximum(b - images - 1, 0)
+
+    def twice(b):
+        return jnp.where(b < images, b, late(b))
 
     def whole(array):
         return pl.BlockSpec(array.shape, lambda b: (0,) * array.ndim, pipeline_mode=pl.Buffered(1))
@@ -926,29 +963,33 @@
 
     return pl.pallas_call(
         partial(back_kernel, images, heads),
-        grid=(images + 1,),
+        grid=(2 * images + 1,),
         in_specs=[
-            per_image(qkv.shape[1:]),
-            per_image(prob.shape[1:]),
-            per_image(att.shape[1:]),
-            per_image(gmid.shape[1:]),
-            per_image((tokens_image, width)),
+            per_image(qkv.shape[1:], early),
+            per_image(prob.shape[1:], early),
+            per_image(normed.shape[1:], early),
+            per_image(att.shape[1:], early),
+            per_image(gmid.shape[1:], twice),
+            per_image((tokens_image, width), late),
             whole(weights),
             whole(vecs),
             whole(rel_rows),
             whole(small),
             far,
         ],
-        out_specs=[per_image((tokens_image, width)), far, vmem],
+        out_specs=[per_image((rows, width), late), far, vmem],
         out_shape=[
-            jax.ShapeDtypeStruct(tokens.shape, F32),
+            jax.ShapeDtypeStruct((images, rows, width), F32),
             jax.ShapeDtypeStruct((12, 256, BLOCK), BF16),
             jax.ShapeDtypeStruct((24, 256), F32),
         ],
         scratch_shapes=[
+            pltpu.VMEM((4, WPAD, 3 * BLOCK), BF16),
+            pltpu.VMEM((4, WPAD, heads * WPAD), F32),
+            pltpu.VMEM((rows, width), F32),
+            pltpu.VMEM((6, rows, BLOCK), BF16),
             pltpu.VMEM((12, 256, BLOCK), BF16),
             pltpu.VMEM((rows, tokens_image), BF16),
-            pltpu.VMEM((tokens_image, rows), BF16),
             pltpu.VMEM((4 * WPAD, 128), BF16),
             pltpu.VMEM((24, BLOCK), F32),
             pltpu.VMEM((WPAD, heads * WPAD), F32),
@@ -963,9 +1004,10 @@
         + reduce_scratch(1)
         + [
             pltpu.VMEM((2, 24, BLOCK), F32),
-            pltpu.VMEM((4, 24, BLOCK), F32),
-            pltpu.VMEM((4, 24, BLOCK), F32),
-            pltpu.VMEM((4, 24, BLOCK), F32),
+            pltpu.VMEM((2, 24, 256), F32),
+            pltpu.VMEM((4, 24, 256), F32),
+            pltpu.VMEM((4, 24, 256), F32),
+            pltpu.VMEM((4, 24, 256), F32),
             pltpu.SemaphoreType.DMA((2,)),
             pltpu.SemaphoreType.DMA((2,)),
             pltpu.SemaphoreType.DMA((82,)),
@@ -975,68 +1017,104 @@
             collective_id=1, has_side_effects=True, vmem_limit_bytes=56 * 1024 * 1024
         ),
         name="back",
-    )(qkv, prob, att, gmid, tokens, weights, vecs, rel_rows, small, fc)
+    )(qkv, prob, normed, att, gmid, tokens, weights, vecs, rel_rows, small, fc)
 
 
 def finish_kernel(
-    f_ref, small_ref, n1g, n1b, qkv, qb, vb, table, proj, pb, n2g, n2b, fc1, f1b, fc2, f2b, wide, turn, sem
+    per_step,
+    out_win, tg_win, f_ref, small_ref,
+    out_ref, tg_ref, n1g, n1b, qkv, qb, vb, table, proj, pb, n2g, n2b, fc1, f1b, fc2, f2b,
+    back_ref, wide, sem,
 ):
-    copies = []
-
-    def store(source, target):
-        copy = pltpu.make_async_copy(source, target, sem.at[len(copies)])
-        copy.start()
-        copies.append(copy)
-
+    step = pl.program_id(0)
+    targets = []
     for n in range(12):
-        wide[n] = f_ref[n].astype(F32)
         if n < 3:
-            store(wide.at[n], qkv.at[:, pl.ds(n * BLOCK, BLOCK)])
+            targets.append([(slice(None), qkv.at[:, pl.ds(n * BLOCK, BLOCK)])])
         elif n == 3:
-            store(wide.at[n], proj)
+            targets.append([(slice(None), proj)])
         elif n < 8:
-            for half in range(2):
-                store(
-                    wide.at[n, :, pl.ds(half * 256, 256)],
-                    fc1.at[:, pl.ds(half * 1024 + (n - 4) * 256, 256)],
-                )
+            targets.append(
+                [
+                    (pl.ds(half * 256, 256), fc1.at[:, pl.ds(half * 1024 + (n - 4) * 256, 256)])
+                    for half in range(2)
+                ]
+            )
         else:
-            store(wide.at[n], fc2.at[pl.ds((n - 8) * 256, 256)])
-    for row, ref in enumerate((n1g, n1b, qb, vb, pb, n2g, n2b, f2b)):
-        ref[...] = small_ref[row : row + 1, :].reshape(256)
-    for m in range(4):
-        f1b[pl.ds(m * 256, 256)] = small_ref[8 + m : 9 + m, :].reshape(256)
-    turn[...] = jnp.zeros_like(turn)
-    turn[0:8, :] = small_ref[12:20, :]
-    table[...] = jnp.concatenate([turn[:, 0:128].T, turn[:, 128:256].T], 0)[
-        : table.shape[0], : table.shape[1]
-    ]
-    for copy in copies:
-        copy.wait()
-
-
-def finish(grads, small, table_rows, heads_here):
+            targets.append([(slice(None), fc2.at[pl.ds((n - 8) * 256, 256)])])
+
+    def stores(n):
+        return [
+            pltpu.make_async_copy(wide.at[n, :, lanes], target, sem.at[n, i])
+            for i, (lanes, target) in enumerate(targets[n])
+        ]
+
+    for n in range(12):
+        @pl.when(step == n // per_step)
+        def _(n=n):
+            wide[n] = f_ref[n % per_step].astype(F32)
+            start(stores(n))
+
+    @pl.when(step == 0)
+    def _():
+        back_ref[...] = back_matrix().astype(BF16)
+        for row, ref in enumerate((n1g, n1b, qb, vb, pb, n2g, n2b, f2b)):
+            ref[...] = small_ref[row : row + 1, :].reshape(256)
+        for m in range(4):
+            f1b[pl.ds(m * 256, 256)] = small_ref[8 + m : 9 + m, :].reshape(256)
+        table[...] = small_ref[12:20, 0 : table.shape[1]]
+
+    out_ref[0] = nn(back_ref[...], out_win[0]).astype(BF16)
+    total = tg_win[0]
+    upper = total.astype(BF16)
+    rest = (total - upper.astype(F32)).astype(BF16)
+    tg_ref[0] = nn(back_ref[...], upper) + nn(back_ref[...], rest)
+
+    @pl.when(step == pl.num_programs(0) - 1)
+    def _():
+        for n in range(12):
+            for copy in stores(n):
+                copy.wait()
+
+
+def finish(out_win, tg_win, grads, small, table_rows, heads_here):
+    images, rows, width = out_win.shape
+    tokens_image = SIDE * SIDE
+    per_step = -(-12 // images)
+    last_block = 12 // per_step - 1
     vmem = pl.BlockSpec(memory_space=pltpu.VMEM)
-    far = pl.BlockSpec(memory_space=pl.ANY)
+    far = pl.BlockSpec(memory_space=pltpu.HBM)
     vector, hidden = ((256,), vmem), ((1024,), vmem)
+    image = pl.BlockSpec((1, rows, width), lambda b: (b, 0, 0))
+    image_out = pl.BlockSpec((1, tokens_image, width), lambda b: (b, 0, 0))
     outs = [
-        vector, vector, ((256, 3 * BLOCK), far), vector, vector, ((table_rows, heads_here), vmem),
+        vector, vector, ((256, 3 * BLOCK), far), vector, vector, ((heads_here, table_rows), vmem),
         ((256, BLOCK), far), vector, vector, vector, ((256, 4 * BLOCK), far), hidden,
         ((1024, BLOCK), far), vector,
     ]
     return pl.pallas_call(
-        finish_kernel,
-        in_specs=[vmem, vmem],
-        out_specs=[spec for _, spec in outs],
-        out_shape=[jax.ShapeDtypeStruct(shape, F32) for shape, _ in outs],
+        partial(finish_kernel, per_step),
+        grid=(images,),
+        in_specs=[
+            image,
+            image,
+            pl.BlockSpec((per_step, 256, BLOCK), lambda b: (jnp.minimum(b, last_block), 0, 0)),
+            pl.BlockSpec(small.shape, lambda b: (0, 0)),
+        ],
+        out_specs=[image_out, image_out] + [spec for _, spec in outs],
+        out_shape=[
+            jax.ShapeDtypeStruct((images, tokens_image, width), BF16),
+            jax.ShapeDtypeStruct((images, tokens_image, width), F32),
+        ]
+        + [jax.ShapeDtypeStruct(shape, F32) for shape, _ in outs],
         scratch_shapes=[
+            pltpu.VMEM((tokens_image, rows), BF16),
             pltpu.VMEM((12, 256, BLOCK), F32),
-            pltpu.VMEM((128, 256), F32),
-            pltpu.SemaphoreType.DMA((16,)),
+            pltpu.SemaphoreType.DMA((12, 2)),
         ],
-        compiler_params=pltpu.CompilerParams(vmem_limit_bytes=30 * 1024 * 1024),
+        compiler_params=pltpu.CompilerParams(vmem_limit_bytes=40 * 1024 * 1024),
         name="finish",
-    )(grads, small)
+    )(out_win, tg_win, grads, small)
 
 
 def local(
@@ -1045,16 +1123,16 @@
     fc2_bias, out_grad,
 ):
     table_rows, heads_here = rel_table.shape
-    qkv, prob, att, block_out, gmid, fc, small, vecs, rel_rows, low_weights = run_front(
+    qkv, prob, normed, att, block_out, gmid, fc, small, vecs, rel_rows, low_weights = run_front(
         [qkv_weight, proj_weight, fc1_weight, fc2_weight],
         [norm1_gain, norm1_bias, q_bias, v_bias, proj_bias, norm2_gain, norm2_bias, fc2_bias],
-        fc1_bias, rel_table, rel_index, shift_mask, tokens, out_grad, image_counts,
+        fc1_bias, rel_table.T, rel_index, shift_mask.transpose(1, 0, 2), tokens, out_grad, image_counts,
     )
     tokens_grad, grads, small = run_back(
-        qkv, prob, att, gmid, tokens, low_weights, vecs, rel_rows, small, fc.reshape(8, 2, 256, BLOCK)
+        qkv, prob, normed, att, gmid, tokens, low_weights, vecs, rel_rows, small, fc.reshape(8, 2, 256, BLOCK)
     )
-    outs = finish(grads, small, table_rows, heads_here)
-    return (block_out, tokens_grad, *outs)
+    outs = finish(block_out, tokens_grad, grads, small, table_rows, heads_here)
+    return (*outs[:7], outs[7].T, *outs[8:])
 
 
 def solution(mesh):

time: 178 us -> 158 us (0.89)
  Pallas kernels: 167 us -> 152 us
  local copies, waits for them, and re-layouts: 10.1 us -> 4.4 us
    pallas_call x2, Pallas kernels: 87.6 us -> 75.9 us  [the longest x1 70.8 us: run_back(): pl.pallas_call(partial(back_kernel, images, heads), grid=(2 * images + 1,...]
    unnamed x11 -> x8, local copies, waits for them, and re-layouts: 10.1 us -> 4.4 us
    pallas_call x1, Pallas kernels: 79 us -> 76.3 us  [run_front(): pl.pallas_call(partial(front_kernel, images), grid=(2 * images + 8,), in_...]
where the time goes in v4:
time: 158 us
  Pallas kernels  152 us (96%)
  local copies, waits for them, and re-layouts  4.4 us (3%)
    pallas_call x1, Pallas kernels, run_front(): pl.pallas_call(partial(front_kernel, images), grid=(2 * images + 8,), in_...  76.3 us
    pallas_call x1, Pallas kernels, run_back(): pl.pallas_call(partial(back_kernel, images, heads), grid=(2 * images + 1,...  70.8 us
    pallas_call x1, Pallas kernels, finish(): pl.pallas_call(partial(finish_kernel, per_step), grid=(images,), in_specs...  5.17 us
    unnamed x8, local copies, waits for them, and re-layouts  4.4 us

profile of v4, /device:TPU:1, one launch (start us, length us, event | category | flops | bytes accessed | tf_op | source)
XLA Modules:
  0.0 158.1 jit_solution(3176346410525810947)
XLA Ops:
  1.3 76.3 %front.1 = (bf16[6,4,64,1536]{3,2,1,0:T(8,128)(2,1)}, f32[6,4,64,1024]{3,2,1,0:T(8,128)}, bf16[6,224,512]{2,1,0:T(8,128)(2,1)}, bf16[6,224,512]{2,1,0:T(8,128)(2...) custom-call(s32[1]{0:T(128)S(6)} %copy.35.count_ref, ...), custom_call_target="tpu_custom_call" | custom-call | tf_op jit(solution)/shard_map/front/pallas_call | solution.py:494
  77.6 0.0 copy-start.2
  77.6 70.8 %back.1 = (f32[6,224,512]{2,1,0:T(8,128)}, bf16[12,256,512]{2,1,0:T(8,128)(2,1)}, f32[24,256]{1,0:T(8,128)}) custom-call(bf16[6,4,64,1536]{3,2,1,0:T(8,128)(2,1)} %get-tuple-element.47.qkv_ref, f32[6,4,64,1024]{3,2,1,0:T(8,128)} %get-tuple-element.48.prob_ref, bf16[6,224,512]{2,1,0:T(8,128)(2,1)} %get-tuple-element.49.normed_ref, ...), custom_call_target="tpu_custom_call" | custom-call | tf_op jit(solution)/shard_map/back/pallas_call | solution.py:964
  148.4 0.0 copy-done.2
  148.4 0.0 copy-start
  148.4 1.9 %copy-done = bf16[12,256,512]{2,1,0:T(8,128)(2,1)S(1)} copy-done((bf16[12,256,512]{2,1,0:T(8,128)(2,1)S(1)}, bf16[12,256,512]{2,1,0:T(8,128)(2,1)}, u32[]{:S(2)}) %copy-start) | copy-done | bytes 3145752
  150.3 0.0 copy-start.1
  150.3 1.8 %copy-done.1 = f32[6,224,512]{2,1,0:T(8,128)S(1)} copy-done((f32[6,224,512]{2,1,0:T(8,128)S(1)}, f32[6,224,512]{2,1,0:T(8,128)}, u32[]{:S(2)}) %copy-start.1) | copy-done | bytes 2752536
  152.1 0.0 copy-start.3
  152.1 0.7 copy-done.3
  152.8 5.2 %finish.1 = (bf16[6,196,512]{2,1,0:T(8,128)(2,1)}, f32[6,196,512]{2,1,0:T(8,128)}, f32[256]{0:T(256)}, f32[256]{0:T(256)}, f32[256,1536]{1,0:T(8,128)}, /*index=...) custom-call(bf16[6,224,512]{2,1,0:T(8,128)(2,1)S(1)} %copy-done.2, ...), custom_call_target="tpu_custom_call" | custom-call | tf_op jit(solution)/shard_map/finish/pallas_call | solution.py:1095
Async XLA Ops:
  77.6 70.8 %copy-start.2 = (bf16[6,224,512]{2,1,0:T(8,128)(2,1)S(1)}, bf16[6,224,512]{2,1,0:T(8,128)(2,1)}, u32[]{:S(2)}) copy-start(bf16[6,224,512]{2,1,0:T(8,128)(2,1)} %get-tuple-element.46.out_win) | copy-start | bytes 4128772
  148.4 1.9 %copy-start = (bf16[12,256,512]{2,1,0:T(8,128)(2,1)S(1)}, bf16[12,256,512]{2,1,0:T(8,128)(2,1)}, u32[]{:S(2)}) copy-start(bf16[12,256,512]{2,1,0:T(8,128)(2,1)} %get-tuple-element.58.f_ref) | copy-start | bytes 9437188
  150.3 1.8 %copy-start.1 = (f32[6,224,512]{2,1,0:T(8,128)S(1)}, f32[6,224,512]{2,1,0:T(8,128)}, u32[]{:S(2)}) copy-start(f32[6,224,512]{2,1,0:T(8,128)} %get-tuple-element.57.tg_win) | copy-start | bytes 8257540
  152.1 0.7 copy-start.3

commit v5 on v4

--- a/solution.py
+++ b/solution.py
@@ -48,14 +48,13 @@
 
 
 def normal_parts(v):
-    size = jnp.abs(v) * 0.7071067811865476
-    bell = jnp.exp(-0.5 * v * v)
-    t = 1.0 / (1.0 + 0.3275911 * size)
+    bell = jnp.exp2(v * v * -0.7213475204444817)
+    t = 1.0 / (1.0 + 0.23164189 * jnp.abs(v))
     tail = t * (
-        0.254829592
-        + t * (-0.284496736 + t * (1.421413741 + t * (-1.453152027 + t * 1.061405429)))
+        0.127414796
+        + t * (-0.142248368 + t * (0.7107068705 + t * (-0.7265760135 + t * 0.5307027145)))
     )
-    half = 0.5 * tail * bell
+    half = tail * bell
     return jnp.where(v < 0, half, 1.0 - half), 0.3989422804014327 * bell
 
 
@@ -182,7 +181,7 @@
 
 
 class Gather:
-    SEMAPHORES = 33
+    SEMAPHORES = 37
 
     def __init__(self, me, w_ref, v_ref, send_sem, recv_sem):
         self.me, self.w, self.v = me, w_ref, v_ref
@@ -249,9 +248,9 @@
     images,
     count_ref,
     qkv_w, proj_w, fc1_w, fc2_w, n1g, n1b, qb, vb, pb, n2g, n2b, f2b, f1b, table_w, index_w, mask_w,
-    tok_ref, up_ref,
+    tok_hbm, up_ref,
     qkv_ref, prob_ref, normed_ref, att_ref, out_ref, gmid_ref, fc_ref, small_ref, vec_out, rel_ref, low_ref,
-    vec_ref, w_ref, acts, bias_ref, place_ref, hmask_ref, att_s, qkv_s, prob_s, acts_s,
+    vec_ref, w_ref, acts, bias_ref, place_ref, hmask_ref, att_s, qkv_s, prob_s, acts_s, fc_send, fc_pair, tok_s, normed_s,
     v0, v1, v2, v3, v4, v5, v6, v7, v8, table_v, index_v, mask_v, square, square_mask, pairs,
     w_sem, in_sem, low_sem, send_sem, recv_sem,
 ):
@@ -260,7 +259,7 @@
     hi = me.hi
     gather = Gather(me, w_ref, vec_ref, send_sem, recv_sem)
     heads = table_w.shape[0] * 2
-    scale = (tok_ref.shape[2] // heads) ** (-0.5)
+    scale = (up_ref.shape[2] // heads) ** (-0.5)
 
     def own_weights(group):
         pairs = []
@@ -291,6 +290,9 @@
             for i, (source, target) in enumerate(zip(sources, targets))
         ]
 
+    def token_copy():
+        return pltpu.make_async_copy(tok_hbm, tok_s, low_sem.at[1])
+
     def low_copy():
         return pltpu.make_async_copy(w_ref.at[pl.ds(0, 4)], low_ref, low_sem.at[0])
 
@@ -309,6 +311,7 @@
         start(own_weights(0))
         start(small_copies)
         start(own_weights(1))
+        token_copy().start()
         peers = [gather.facing(), me.other_core()]
         peers += [me.along(axis, s) for axis in ("y", "z") for s in (1, 2, 3)]
         greet(peers)
@@ -364,6 +367,14 @@
             for w in range(4):
                 bias_ref[w, :half, at] = both[:, :WPAD] + square_mask[w, :half]
                 bias_ref[w, half:, at] = both[:, WPAD:] + square_mask[w, half:]
+        token_copy().wait()
+
+        def norm(b, carry):
+            unit, _ = normalize(nn(place_ref[...], tok_s[b]))
+            normed_s[b] = (unit * vec(0) + vec(1)).astype(BF16)
+            return carry
+
+        lax.fori_loop(0, images, norm, 0)
         arrived(gather.last(0))
         low_copy().start()
 
@@ -379,8 +390,7 @@
     @pl.when(step < images)
     def _():
         hmask = hmask_ref[...]
-        unit, _ = normalize(nn(place_ref[...], tok_ref[0]))
-        normed = (unit * vec(0) + vec(1)).astype(BF16)
+        normed = normed_s[step]
         for n in range(3):
             part = nn(normed, weight(n))
             if n == 0:
@@ -415,9 +425,9 @@
         rows = pl.ds(pl.multiple_of(image * (4 * ROWS), 16), 4 * ROWS)
 
         def keep(block, values):
-            acts_s[block] = values
-
-        middle = nn(place_ref[...], tok_ref[0]) + (nn(att_ref[image], weight(3)) + vec(4))
+            acts[block, rows, :] = values
+
+        middle = nn(place_ref[...], tok_s[image]) + (nn(att_ref[image], weight(3)) + vec(4))
         unit, rate = normalize(middle)
         normed = (unit * vec(5) + vec(6)).astype(BF16)
         keep(0, normed)
@@ -447,15 +457,36 @@
         note(4, grad_middle)
         gmid_ref[0] = grad_middle
         out_ref[0] = (result * valid).astype(BF16)
-        for block in range(10):
-            acts[block, rows, :] = acts_s[block]
-
-    @pl.when(step >= 2 * images)
-    def _():
-        block = step - 2 * images
+
+    def grad_block(number, core):
+        block = 4 * (number // 2) + 2 * core + lax.rem(number, 2)
         left = jnp.where(block < 4, 0, block + 1)
         right = jnp.where(block < 4, block + 1, 9)
-        fc_ref[0] = tn(acts[left], acts[right]).astype(BF16)
+        return tn(acts[left], acts[right])
+
+    def pair_copy(number):
+        return remote(
+            fc_send.at[number], fc_pair.at[number], send_sem, recv_sem, 33 + number, me.other_core()
+        )
+
+    @pl.when((step >= 2 * images) & (step < 2 * images + 4))
+    def _():
+        number = step - 2 * images
+        fc_send[number] = grad_block(number, 1 - me.core).astype(BF16)
+
+    for number in range(4):
+        @pl.when(step == 2 * images + number)
+        def _(number=number):
+            start([pair_copy(number)])
+
+        @pl.when(step == 2 * images + 4 + number)
+        def _(number=number):
+            arrived([pair_copy(number)])
+
+    @pl.when(step >= 2 * images + 4)
+    def _():
+        number = step - 2 * images - 4
+        fc_ref[0] = (grad_block(number, me.core) + fc_pair[number].astype(F32)).astype(BF16)
 
     @pl.when(step == pl.num_programs(0) - 1)
     def _():
@@ -463,6 +494,7 @@
             for copies in (gather.cross, gather.first, gather.second, gather.last):
                 sent(copies(group))
         sent(gather.vectors())
+        sent([pair_copy(number) for number in range(4)])
         low_copy().wait()
 
 
@@ -488,15 +520,12 @@
     def late(b):
         return jnp.clip(b - images, 0, images - 1)
 
-    def twice(b):
-        return jnp.where(b < images, b, late(b))
-
     return pl.pallas_call(
         partial(front_kernel, images),
         grid=(2 * images + 8,),
         in_specs=[pl.BlockSpec(memory_space=pltpu.SMEM)]
         + [far] * (4 + len(small))
-        + [per_image((tokens_image, width), twice), per_image((tokens_image, width), late)],
+        + [far, per_image((tokens_image, width), late)],
         out_specs=[
             per_image((4, WPAD, 3 * BLOCK), early),
             per_image((4, WPAD, heads * WPAD), early),
@@ -504,7 +533,7 @@
             whole((images, rows, width)),
             per_image((rows, width), late),
             per_image((rows, width), late),
-            per_image((BLOCK, BLOCK), lambda b: jnp.maximum(b - 2 * images, 0)),
+            per_image((BLOCK, BLOCK), lambda b: jnp.maximum(b - 2 * images - 4, 0)),
             whole((24, BLOCK)),
             whole((2, 24, 256)),
             whole((WPAD // 2, 2 * WPAD)),
@@ -517,7 +546,7 @@
             jax.ShapeDtypeStruct((images, rows, width), BF16),
             jax.ShapeDtypeStruct((images, rows, width), BF16),
             jax.ShapeDtypeStruct((images, rows, width), F32),
-            jax.ShapeDtypeStruct((8, BLOCK, BLOCK), BF16),
+            jax.ShapeDtypeStruct((4, BLOCK, BLOCK), BF16),
             jax.ShapeDtypeStruct((24, BLOCK), F32),
             jax.ShapeDtypeStruct((2, 24, 256), F32),
             jax.ShapeDtypeStruct((WPAD // 2, 2 * WPAD), F32),
@@ -534,6 +563,10 @@
             pltpu.VMEM((4, WPAD, 3 * BLOCK), BF16),
             pltpu.VMEM((4, WPAD, heads * WPAD), F32),
             pltpu.VMEM((10, rows, BLOCK), BF16),
+            pltpu.VMEM((4, BLOCK, BLOCK), BF16),
+            pltpu.VMEM((4, BLOCK, BLOCK), BF16),
+            pltpu.VMEM(tokens.shape, BF16),
+            pltpu.VMEM((images, rows, BLOCK), BF16),
         ]
         + [pltpu.VMEM(item.shape, item.dtype) for item in small]
         + [
@@ -542,7 +575,7 @@
             pltpu.VMEM((heads * WPAD // 2, 2 * WPAD), F32),
             pltpu.SemaphoreType.DMA((16,)),
             pltpu.SemaphoreType.DMA((len(small),)),
-            pltpu.SemaphoreType.DMA((1,)),
+            pltpu.SemaphoreType.DMA((2,)),
             pltpu.SemaphoreType.DMA((Gather.SEMAPHORES,)),
             pltpu.SemaphoreType.DMA((Gather.SEMAPHORES,)),
         ],
@@ -556,12 +589,12 @@
 class Reduce:
     SEMAPHORES = 36
 
-    def __init__(self, me, source, own, pair, sums, got, sum_one, got_one, sum_two, got_two, f_ref, first_block, sems, base):
-        self.me, self.source, self.own, self.pair, self.sums = me, source, own, pair, sums
+    def __init__(self, me, sums, got, sum_one, got_one, sum_two, got_two, f_ref, first_block, sems, base):
+        self.me, self.sums = me, sums
         self.got, self.sum_one, self.got_one = got, sum_one, got_one
         self.sum_two, self.got_two, self.f_ref = sum_two, got_two, f_ref
         self.first_block, self.sems, self.base = first_block, sems, base
-        self.count = pair.shape[1]
+        self.count = sums.shape[1]
 
     def axes(self, p):
         return (("y", "z"), ("z", "y"))[p]
@@ -569,29 +602,8 @@
     def copy(self, p, number, source, target, device):
         return remote(source, target, *self.sems, self.base + 18 * p + number, device)
 
-    def blocks(self, p, core):
-        return pl.ds((2 * p + core) * self.count, self.count)
-
     def target(self, p):
         return pl.ds(self.first_block + (2 * p + self.me.core) * self.count, self.count)
-
-    def cores(self, p):
-        return [
-            self.copy(
-                p, 0, self.source.at[self.blocks(p, 1 - self.me.core)], self.pair.at[p], self.me.other_core()
-            )
-        ]
-
-    def add_cores(self, p):
-        arrived(self.cores(p))
-        for b in range(self.count):
-            for half in range(2):
-                if self.own is None:
-                    block = self.source[pl.ds((2 * p + self.me.core) * self.count + b, 1), half][0]
-                else:
-                    block = self.own[p, b, half]
-                total = block.astype(F32) + self.pair[p, b, half].astype(F32)
-                self.sums[p, b, half] = total.astype(BF16)
 
     def scatter(self, p, stage):
         me, axis = self.me, self.axes(p)[stage]
@@ -668,10 +680,7 @@
 
     def step(self, number):
         for p in range(2):
-            if number == 0:
-                start(self.cores(p))
-            elif number == 1:
-                self.add_cores(p)
+            if number == 1:
                 start(self.scatter(p, 0))
             elif number == 2:
                 self.add(p, 0)
@@ -694,7 +703,6 @@
 
     def all_sent(self):
         for p in range(2):
-            sent(self.cores(p))
             for stage in range(2):
                 sent(self.scatter(p, stage))
                 sent(self.back(p, stage))
@@ -707,27 +715,26 @@
     heads,
     qkv_ref, prob_ref, normed_ref, att_ref, gmid_ref, tok_ref, w_ref, vec_ref, rel_ref, small_in, fc_ref,
     tg_ref, f_out, small_out,
-    qkv_s, prob_s, gmid_s, acts_s, f_ref, place_ref, hmask_ref, small_ref, pair_ref, fold_s, gatt_s, dqkv_s, acts, low_ref,
-    fc_own, fc_pair, fc_sums, fc_got, fc_sum_one, fc_got_one, fc_sum_two, fc_got_two,
-    lo_pair, lo_sums, lo_got, lo_sum_one, lo_got_one, lo_sum_two, lo_got_two,
+    qkv_s, prob_s, gmid_s, acts_s, f_ref, place_ref, hmask_ref, small_ref, pair_ref, fold_s, gatt_s, dqkv_s, acts,
+    fc_sums, fc_got, fc_sum_one, fc_got_one, fc_sum_two, fc_got_two,
+    low_send, low_own, lo_pair, lo_sums, lo_got, lo_sum_one, lo_got_one, lo_sum_two, lo_got_two,
     small_pair, small_halves, small_x, small_y, small_z, own_sem, out_sem, send_sem, recv_sem,
 ):
     step = pl.program_id(0)
     me = Place()
     scale = (tok_ref.shape[2] // heads) ** (-0.5)
     sems = (send_sem, recv_sem)
-    high = Reduce(
-        me, fc_ref, fc_own, fc_pair, fc_sums, fc_got, fc_sum_one, fc_got_one, fc_sum_two, fc_got_two, f_ref, 4, sems, 0
-    )
-    low = Reduce(
-        me, low_ref, None, lo_pair, lo_sums, lo_got, lo_sum_one, lo_got_one, lo_sum_two, lo_got_two, f_ref, 0, sems, 36
-    )
+    high = Reduce(me, fc_sums, fc_got, fc_sum_one, fc_got_one, fc_sum_two, fc_got_two, f_ref, 4, sems, 0)
+    low = Reduce(me, lo_sums, lo_got, lo_sum_one, lo_got_one, lo_sum_two, lo_got_two, f_ref, 0, sems, 36)
 
     def own_copies():
         return [
-            pltpu.make_async_copy(fc_ref.at[high.blocks(p, me.core)], fc_own.at[p], own_sem.at[p])
+            pltpu.make_async_copy(fc_ref.at[pl.ds(2 * p, 2)], fc_sums.at[p], own_sem.at[p])
             for p in range(2)
         ]
+
+    def low_pair(p):
+        return remote(low_send.at[p], lo_pair.at[p], *sems, 36 + 18 * p, me.other_core())
 
     def weight(n):
         return w_ref[n].reshape(BLOCK, BLOCK)
@@ -744,16 +751,13 @@
         peers = [me.other_core()]
         peers += [me.along(axis, s) for axis in ("x", "y", "z") for s in (1, 2, 3)]
         greet(peers)
-        high.step(0)
+        for copy in own_copies():
+            copy.wait()
+        high.step(1)
         place_ref[...] = place_matrix().astype(BF16)
         hmask_ref[...] = head_mask().astype(BF16)
         small_ref[...] = small_in[...]
         pair_ref[...] = jnp.zeros_like(pair_ref)
-
-    @pl.when(step == 1)
-    def _():
-        for copy in own_copies():
-            copy.wait()
 
     for at_step, moves in PLAN:
         @pl.when(step == at_step)
@@ -858,14 +862,20 @@
 
     @pl.when(step == images)
     def _():
+        def grad_block(n):
+            left = jnp.where(n < 3, 0, 4)
+            right = jnp.where(n < 3, n + 1, 5)
+            return tn(acts[left], acts[right]).reshape(2, 256, BLOCK)
+
         for p in range(2):
-            for n in (2 * p, 2 * p + 1):
-                left, right = ((0, 1), (0, 2), (0, 3), (4, 5))[n]
-                low_ref[n] = tn(acts[left], acts[right]).astype(BF16).reshape(2, 256, BLOCK)
-            start(low.cores(p))
-            if p == 0:
-                for number in DURING_GRADS:
-                    high.step(number)
+            low_send[p] = grad_block(2 * p + 1 - me.core).astype(BF16)
+            start([low_pair(p)])
+        for number in DURING_GRADS[0]:
+            high.step(number)
+        for p in range(2):
+            low_own[p] = grad_block(2 * p + me.core)
+        for number in DURING_GRADS[1]:
+            high.step(number)
         half = WPAD // 2
         for h in range(heads):
             at = slice(h * WPAD, (h + 1) * WPAD)
@@ -882,14 +892,18 @@
         table = total[:heads] + total[heads:]
         small_ref[12 : 12 + heads // 2, :256] = table[: heads // 2]
         small_ref[12 : 12 + heads // 2, 256:] = table[heads // 2 :]
+        for p in range(2):
+            arrived([low_pair(p)])
+            for part in range(2):
+                total = low_own[p, part] + lo_pair[p, part].astype(F32)
+                lo_sums[p, 0, part] = total.astype(BF16)
+        low.step(1)
 
     @pl.when(step == 2 * images)
     def _():
         small_pair[pl.ds(me.core, 1)] = small_ref[...][None]
         start(small_cores())
-        high.step(7)
         high_out = pltpu.make_async_copy(f_ref.at[pl.ds(4, 8)], f_out.at[pl.ds(4, 8)], out_sem.at[0])
-        high_out.start()
         arrived(small_cores())
         small_total = small_pair[0] + small_pair[1]
         small_halves[0] = small_total[:, :256]
@@ -899,10 +913,13 @@
         low.step(2)
         small_start("y", small_sum("x"))
         low.step(3)
+        high.step(6)
         small_start("z", small_sum("y"))
         low.step(4)
         small_out[...] = small_sum("z")
         low.step(5)
+        high.step(7)
+        high_out.start()
         low.step(6)
         low.step(7)
         low_out = pltpu.make_async_copy(f_ref.at[pl.ds(0, 4)], f_out.at[pl.ds(0, 4)], out_sem.at[1])
@@ -911,6 +928,7 @@
         low_out.wait()
         high.all_sent()
         low.all_sent()
+        sent([low_pair(p) for p in range(2)])
         sent(small_cores())
         sent(small_across())
         sent(small_copies("y"))
@@ -918,14 +936,11 @@
 
 
 PLAN = (
-    (1, (("high", 1),)),
     (4, (("high", 2),)),
     (5, (("high", 3),)),
     (6, (("high", 4),)),
-    (8, (("low", 1),)),
-    (9, (("high", 6),)),
 )
-DURING_GRADS = (5,)
+DURING_GRADS = ((), (5,))
 
 
 def run_back(qkv, prob, normed, att, gmid, tokens, weights, vecs, rel_rows, small, fc):
@@ -952,7 +967,6 @@
 
     def reduce_scratch(count):
         return [
-            pltpu.VMEM((2, count, 2, 256, BLOCK), BF16),
             pltpu.VMEM((2, count, 2, 256, BLOCK), BF16),
             pltpu.VMEM((2, 3, count, 2, 64, BLOCK), BF16),
             pltpu.VMEM((2, count, 2, 64, BLOCK), BF16),
@@ -997,10 +1011,13 @@
             pltpu.VMEM((4, WPAD, BLOCK), BF16),
             pltpu.VMEM((rows, 3 * BLOCK), F32),
             pltpu.VMEM((6, images * rows, BLOCK), BF16),
-            pltpu.VMEM((4, 2, 256, BLOCK), BF16),
-            pltpu.VMEM((2, 2, 2, 256, BLOCK), BF16),
         ]
         + reduce_scratch(2)
+        + [
+            pltpu.VMEM((2, 2, 256, BLOCK), BF16),
+            pltpu.VMEM((2, 2, 256, BLOCK), F32),
+            pltpu.VMEM((2, 2, 256, BLOCK), BF16),
+        ]
         + reduce_scratch(1)
         + [
             pltpu.VMEM((2, 24, BLOCK), F32),
@@ -1021,12 +1038,12 @@
 
 
 def finish_kernel(
-    per_step,
     out_win, tg_win, f_ref, small_ref,
     out_ref, tg_ref, n1g, n1b, qkv, qb, vb, table, proj, pb, n2g, n2b, fc1, f1b, fc2, f2b,
-    back_ref, wide, sem,
+    out_in, tg_in, f_in, small_in, out_s, tg_s, wide, in_sem, out_sem, sem,
 ):
-    step = pl.program_id(0)
+    images = out_win.shape[0]
+    per_step = -(-12 // images)
     targets = []
     for n in range(12):
         if n < 3:
@@ -1042,74 +1059,79 @@
             )
         else:
             targets.append([(slice(None), fc2.at[pl.ds((n - 8) * 256, 256)])])
-
-    def stores(n):
-        return [
-            pltpu.make_async_copy(wide.at[n, :, lanes], target, sem.at[n, i])
-            for i, (lanes, target) in enumerate(targets[n])
-        ]
-
-    for n in range(12):
-        @pl.when(step == n // per_step)
-        def _(n=n):
-            wide[n] = f_ref[n % per_step].astype(F32)
-            start(stores(n))
-
-    @pl.when(step == 0)
-    def _():
-        back_ref[...] = back_matrix().astype(BF16)
-        for row, ref in enumerate((n1g, n1b, qb, vb, pb, n2g, n2b, f2b)):
-            ref[...] = small_ref[row : row + 1, :].reshape(256)
-        for m in range(4):
-            f1b[pl.ds(m * 256, 256)] = small_ref[8 + m : 9 + m, :].reshape(256)
-        table[...] = small_ref[12:20, 0 : table.shape[1]]
-
-    out_ref[0] = nn(back_ref[...], out_win[0]).astype(BF16)
-    total = tg_win[0]
-    upper = total.astype(BF16)
-    rest = (total - upper.astype(F32)).astype(BF16)
-    tg_ref[0] = nn(back_ref[...], upper) + nn(back_ref[...], rest)
-
-    @pl.when(step == pl.num_programs(0) - 1)
-    def _():
-        for n in range(12):
-            for copy in stores(n):
-                copy.wait()
+    blocks = [range(b * per_step, min(12, (b + 1) * per_step)) for b in range(images)]
+    small_copy = pltpu.make_async_copy(small_ref, small_in, in_sem.at[3 * images])
+    loads = []
+    for b in range(images):
+        copies = [
+            pltpu.make_async_copy(tg_win.at[b], tg_in.at[b], in_sem.at[3 * b]),
+            pltpu.make_async_copy(out_win.at[b], out_in.at[b], in_sem.at[3 * b + 1]),
+        ]
+        if len(blocks[b]):
+            part = pl.ds(blocks[b][0], len(blocks[b]))
+            copies.append(pltpu.make_async_copy(f_ref.at[part], f_in.at[part], in_sem.at[3 * b + 2]))
+        start(copies)
+        loads.append(copies)
+    small_copy.start()
+    back = back_matrix().astype(BF16)
+    stores = []
+    for b in range(images):
+        for copy in loads[b]:
+            copy.wait()
+        for n in blocks[b]:
+            wide[n] = f_in[n].astype(F32)
+            for i, (lanes, target) in enumerate(targets[n]):
+                stores.append(pltpu.make_async_copy(wide.at[n, :, lanes], target, sem.at[n, i]))
+                stores[-1].start()
+        total = tg_in[b]
+        upper = total.astype(BF16)
+        rest = (total - upper.astype(F32)).astype(BF16)
+        tg_s[b] = nn(back, upper) + nn(back, rest)
+        stores.append(pltpu.make_async_copy(tg_s.at[b], tg_ref.at[b], out_sem.at[2 * b]))
+        stores[-1].start()
+        out_s[b] = nn(back, out_in[b]).astype(BF16)
+        stores.append(pltpu.make_async_copy(out_s.at[b], out_ref.at[b], out_sem.at[2 * b + 1]))
+        stores[-1].start()
+    small_copy.wait()
+    for row, ref in enumerate((n1g, n1b, qb, vb, pb, n2g, n2b, f2b)):
+        ref[...] = small_in[row : row + 1, :].reshape(256)
+    for m in range(4):
+        f1b[pl.ds(m * 256, 256)] = small_in[8 + m : 9 + m, :].reshape(256)
+    table[...] = small_in[12:20, 0 : table.shape[1]]
+    for copy in stores:
+        copy.wait()
 
 
 def finish(out_win, tg_win, grads, small, table_rows, heads_here):
     images, rows, width = out_win.shape
     tokens_image = SIDE * SIDE
-    per_step = -(-12 // images)
-    last_block = 12 // per_step - 1
     vmem = pl.BlockSpec(memory_space=pltpu.VMEM)
     far = pl.BlockSpec(memory_space=pltpu.HBM)
     vector, hidden = ((256,), vmem), ((1024,), vmem)
-    image = pl.BlockSpec((1, rows, width), lambda b: (b, 0, 0))
-    image_out = pl.BlockSpec((1, tokens_image, width), lambda b: (b, 0, 0))
     outs = [
         vector, vector, ((256, 3 * BLOCK), far), vector, vector, ((heads_here, table_rows), vmem),
         ((256, BLOCK), far), vector, vector, vector, ((256, 4 * BLOCK), far), hidden,
         ((1024, BLOCK), far), vector,
     ]
     return pl.pallas_call(
-        partial(finish_kernel, per_step),
-        grid=(images,),
-        in_specs=[
-            image,
-            image,
-            pl.BlockSpec((per_step, 256, BLOCK), lambda b: (jnp.minimum(b, last_block), 0, 0)),
-            pl.BlockSpec(small.shape, lambda b: (0, 0)),
-        ],
-        out_specs=[image_out, image_out] + [spec for _, spec in outs],
+        finish_kernel,
+        in_specs=[far] * 4,
+        out_specs=[far, far] + [spec for _, spec in outs],
         out_shape=[
             jax.ShapeDtypeStruct((images, tokens_image, width), BF16),
             jax.ShapeDtypeStruct((images, tokens_image, width), F32),
         ]
         + [jax.ShapeDtypeStruct(shape, F32) for shape, _ in outs],
         scratch_shapes=[
-            pltpu.VMEM((tokens_image, rows), BF16),
+            pltpu.VMEM(out_win.shape, BF16),
+            pltpu.VMEM(tg_win.shape, F32),
+            pltpu.VMEM(grads.shape, BF16),
+            pltpu.VMEM(small.shape, F32),
+            pltpu.VMEM((images, tokens_image, width), BF16),
+            pltpu.VMEM((images, tokens_image, width), F32),
             pltpu.VMEM((12, 256, BLOCK), F32),
+            pltpu.SemaphoreType.DMA((3 * images + 1,)),
+            pltpu.SemaphoreType.DMA((2 * images,)),
             pltpu.SemaphoreType.DMA((12, 2)),
         ],
         compiler_params=pltpu.CompilerParams(vmem_limit_bytes=40 * 1024 * 1024),
@@ -1129,7 +1151,7 @@
         fc1_bias, rel_table.T, rel_index, shift_mask.transpose(1, 0, 2), tokens, out_grad, image_counts,
     )
     tokens_grad, grads, small = run_back(
-        qkv, prob, normed, att, gmid, tokens, low_weights, vecs, rel_rows, small, fc.reshape(8, 2, 256, BLOCK)
+        qkv, prob, normed, att, gmid, tokens, low_weights, vecs, rel_rows, small, fc.reshape(4, 2, 256, BLOCK)
     )
     outs = finish(block_out, tokens_grad, grads, small, table_rows, heads_here)
     return (*outs[:7], outs[7].T, *outs[8:])

time: 158 us -> 159 us (level)
    pallas_call x1, Pallas kernels: 5.17 us -> 9.52 us  [finish(): pl.pallas_call(finish_kernel, in_specs=[far] * 4, out_specs=[far, far] +...]
    pallas_call x1, Pallas kernels: 76.3 us -> 74.4 us  [run_front(): pl.pallas_call(partial(front_kernel, images), grid=(2 * images + 8,), in_...]
    pallas_call x1, Pallas kernels: 70.8 us -> 68.9 us  [run_back(): pl.pallas_call(partial(back_kernel, images, heads), grid=(2 * images + 1,...]
where the time goes in v5:
time: 159 us
  Pallas kernels  153 us (96%)
  local copies, waits for them, and re-layouts  4.4 us (3%)
    pallas_call x1, Pallas kernels, run_front(): pl.pallas_call(partial(front_kernel, images), grid=(2 * images + 8,), in_...  74.4 us
    pallas_call x1, Pallas kernels, run_back(): pl.pallas_call(partial(back_kernel, images, heads), grid=(2 * images + 1,...  68.9 us
    pallas_call x1, Pallas kernels, finish(): pl.pallas_call(finish_kernel, in_specs=[far] * 4, out_specs=[far, far] +...  9.52 us
    unnamed x8, local copies, waits for them, and re-layouts  4.4 us

profile of v5, /device:TPU:1, one launch (start us, length us, event | category | flops | bytes accessed | tf_op | source)
XLA Modules:
  0.0 158.7 jit_solution(16201163580586518824)
XLA Ops:
  1.3 74.4 %front.1 = (bf16[6,4,64,1536]{3,2,1,0:T(8,128)(2,1)}, f32[6,4,64,1024]{3,2,1,0:T(8,128)}, bf16[6,224,512]{2,1,0:T(8,128)(2,1)}, bf16[6,224,512]{2,1,0:T(8,128)(2...) custom-call(s32[1]{0:T(128)S(6)} %copy.35.count_ref, ...), custom_call_target="tpu_custom_call" | custom-call | tf_op jit(solution)/shard_map/front/pallas_call | solution.py:523
  75.7 0.0 copy-start.2
  75.7 68.9 %back.1 = (f32[6,224,512]{2,1,0:T(8,128)}, bf16[12,256,512]{2,1,0:T(8,128)(2,1)}, f32[24,256]{1,0:T(8,128)}) custom-call(bf16[6,4,64,1536]{3,2,1,0:T(8,128)(2,1)} %get-tuple-element.47.qkv_ref, f32[6,4,64,1024]{3,2,1,0:T(8,128)} %get-tuple-element.48.prob_ref, bf16[6,224,512]{2,1,0:T(8,128)(2,1)} %get-tuple-element.49.normed_ref, ...), custom_call_target="tpu_custom_call" | custom-call | tf_op jit(solution)/shard_map/back/pallas_call | solution.py:978
  144.6 0.0 copy-done.2
  144.6 0.0 copy-start
  144.7 1.9 %copy-done = bf16[12,256,512]{2,1,0:T(8,128)(2,1)S(1)} copy-done((bf16[12,256,512]{2,1,0:T(8,128)(2,1)S(1)}, bf16[12,256,512]{2,1,0:T(8,128)(2,1)}, u32[]{:S(2)}) %copy-start) | copy-done | bytes 3145752
  146.5 0.0 copy-start.1
  146.5 1.8 %copy-done.1 = f32[6,224,512]{2,1,0:T(8,128)S(1)} copy-done((f32[6,224,512]{2,1,0:T(8,128)S(1)}, f32[6,224,512]{2,1,0:T(8,128)}, u32[]{:S(2)}) %copy-start.1) | copy-done | bytes 2752536
  148.3 0.0 copy-start.3
  148.3 0.7 copy-done.3
  149.1 9.5 %finish.1 = (bf16[6,196,512]{2,1,0:T(8,128)(2,1)}, f32[6,196,512]{2,1,0:T(8,128)}, f32[256]{0:T(256)}, f32[256]{0:T(256)}, f32[256,1536]{1,0:T(8,128)}, /*index=...) custom-call(bf16[6,224,512]{2,1,0:T(8,128)(2,1)S(1)} %copy-done.2, ...), custom_call_target="tpu_custom_call" | custom-call | tf_op jit(solution)/shard_map/finish/pallas_call | solution.py:1116
Async XLA Ops:
  75.7 68.9 %copy-start.2 = (bf16[6,224,512]{2,1,0:T(8,128)(2,1)S(1)}, bf16[6,224,512]{2,1,0:T(8,128)(2,1)}, u32[]{:S(2)}) copy-start(bf16[6,224,512]{2,1,0:T(8,128)(2,1)} %get-tuple-element.46.out_win) | copy-start | bytes 4128772
  144.6 1.9 %copy-start = (bf16[12,256,512]{2,1,0:T(8,128)(2,1)S(1)}, bf16[12,256,512]{2,1,0:T(8,128)(2,1)}, u32[]{:S(2)}) copy-start(bf16[12,256,512]{2,1,0:T(8,128)(2,1)} %get-tuple-element.58.f_ref) | copy-start | bytes 9437188
  146.5 1.8 %copy-start.1 = (f32[6,224,512]{2,1,0:T(8,128)S(1)}, f32[6,224,512]{2,1,0:T(8,128)}, u32[]{:S(2)}) copy-start(f32[6,224,512]{2,1,0:T(8,128)} %get-tuple-element.57.tg_win) | copy-start | bytes 8257540
  148.3 0.7 copy-start.3

commit v6 on v5

--- a/solution.py
+++ b/solution.py
@@ -435,8 +435,7 @@
         up_low = upstream.astype(BF16)
         keep(9, up_low)
         note(7, upstream)
-        branch = None
-        grad = None
+        act_parts, pre_parts = [], []
         for c in range(4):
             pre = nn(normed, weight(4 + c)) + vec(8 + c)
             below, density = normal_parts(pre)
@@ -446,10 +445,12 @@
             note(8 + c, grad_pre)
             pre_low = grad_pre.astype(BF16)
             keep(1 + c, pre_low)
-            first = nn(act, weight(8 + c))
-            second = nt(pre_low, weight(4 + c))
-            branch = first if c == 0 else branch + first
-            grad = second if c == 0 else grad + second
+            act_parts.append(act)
+            pre_parts.append(pre_low)
+        branch = nn(jnp.concatenate(act_parts, 1), w_ref[8:12].reshape(4 * BLOCK, BLOCK))
+        grad = nt(
+            jnp.concatenate(pre_parts, 1), jnp.concatenate([weight(4 + c) for c in range(4)], 1)
+        )
         result = middle + (branch + vec(7))
         note(5, grad * unit)
         note(6, grad)
@@ -1134,7 +1135,7 @@
             pltpu.SemaphoreType.DMA((2 * images,)),
             pltpu.SemaphoreType.DMA((12, 2)),
         ],
-        compiler_params=pltpu.CompilerParams(vmem_limit_bytes=40 * 1024 * 1024),
+        compiler_params=pltpu.CompilerParams(vmem_limit_bytes=60 * 1024 * 1024),
         name="finish",
     )(out_win, tg_win, grads, small)
 

time: 159 us -> 151 us (0.950)
  local copies, waits for them, and re-layouts: 4.4 us -> 0 us
  Pallas kernels: 153 us -> 149 us
    unnamed x8 -> x0, local copies, waits for them, and re-layouts: 4.4 us -> none
    pallas_call x1, Pallas kernels: 9.52 us -> 7.11 us  [finish(): pl.pallas_call(finish_kernel, in_specs=[far] * 4, out_specs=[far, far] +...]
where the time goes in v6:
time: 151 us; the launch traced here: 150 us
  Pallas kernels  149 us (99%)
    pallas_call x1, Pallas kernels, run_front(): pl.pallas_call(partial(front_kernel, images), grid=(2 * images + 8,), in_...  73 us
    pallas_call x1, Pallas kernels, run_back(): pl.pallas_call(partial(back_kernel, images, heads), grid=(2 * images + 1,...  68.8 us
    pallas_call x1, Pallas kernels, finish(): pl.pallas_call(finish_kernel, in_specs=[far] * 4, out_specs=[far, far] +...  7.11 us

profile of v6, /device:TPU:1, one launch (start us, length us, event | category | flops | bytes accessed | tf_op | source)
XLA Modules:
  0.0 150.4 jit_solution(5523443599724935714)
XLA Ops:
  1.3 73.0 %front.1 = (bf16[6,4,64,1536]{3,2,1,0:T(8,128)(2,1)}, f32[6,4,64,1024]{3,2,1,0:T(8,128)}, bf16[6,224,512]{2,1,0:T(8,128)(2,1)}, bf16[6,224,512]{2,1,0:T(8,128)(2...) custom-call(s32[1]{0:T(128)S(6)} %copy.35.count_ref, ...), custom_call_target="tpu_custom_call" | custom-call | tf_op jit(solution)/shard_map/front/pallas_call | solution.py:524
  74.3 68.8 %back.1 = (f32[6,224,512]{2,1,0:T(8,128)}, bf16[12,256,512]{2,1,0:T(8,128)(2,1)}, f32[24,256]{1,0:T(8,128)}) custom-call(bf16[6,4,64,1536]{3,2,1,0:T(8,128)(2,1)} %get-tuple-element.47.qkv_ref, f32[6,4,64,1024]{3,2,1,0:T(8,128)} %get-tuple-element.48.prob_ref, bf16[6,224,512]{2,1,0:T(8,128)(2,1)} %get-tuple-element.49.normed_ref, ...), custom_call_target="tpu_custom_call" | custom-call | tf_op jit(solution)/shard_map/back/pallas_call | solution.py:979
  143.1 7.1 %finish.1 = (bf16[6,196,512]{2,1,0:T(8,128)(2,1)}, f32[6,196,512]{2,1,0:T(8,128)}, f32[256]{0:T(256)}, f32[256]{0:T(256)}, f32[256,1536]{1,0:T(8,128)}, /*index=...) custom-call(bf16[6,224,512]{2,1,0:T(8,128)(2,1)} %get-tuple-element., ...), custom_call_target="tpu_custom_call" | custom-call | tf_op jit(solution)/shard_map/finish/pallas_call | solution.py:1117
